TPU v7x, 32 devices: a whole 2x2x4 slice. The times are simulated.
32 devices in a mesh: seq: 16 (over z, y, x), mp: 2 (over core).
Axes of the slice: x: 2, y: 2, z: 4, core: 2. Of those that a mesh axis runs over, the one named last changes fastest.
Arguments:
- kv_cache: bfloat16 [32768, 8, 256], P('seq', 'mp'), may hold values from -6 to 6
- keep_list: int32 [32768], P('seq'), may hold values from 0 to 1, as said below
- drop_level: int32 [32768], P('seq'), may hold values from 0 to 15
- drop_table: float32 [4, 16], replicated, may hold values from 0.02 to 2
- req_blocks: int32 [128], replicated, may hold values from 1 to 64, 256 in all
- tenant_sizes: int32 [4], replicated, may hold values from 1 to 64, 128 in all
- queries: bfloat16 [128, 32, 128], P(None, 'mp'), may hold values from -100 to 100
- residual: bfloat16 [128, 5120], P(None, 'seq'), may hold values from -6 to 6
- w_out: bfloat16 [4096, 5120], P('mp', 'seq'), may hold values from -0.09375 to 0.09375
- norm_gain: float32 [5120], P('seq'), may hold values from 0.5 to 1.5
- w_gate: bfloat16 [5120, 32768], P(None, ('seq', 'mp')), may hold values from -0.078125 to 0.078125
- w_up: bfloat16 [5120, 32768], P(None, ('seq', 'mp')), may hold values from -0.078125 to 0.078125
- w_down: bfloat16 [32768, 5120], P(('seq', 'mp')), may hold values from -0.0625 to 0.0625
Outputs:
- summaries: bfloat16 [256, 8, 256], P('seq', 'mp')
- packed: bfloat16 [16, 1024, 8, 256], P('seq', None, 'mp')
- final: bfloat16 [128, 5120], P(None, 'seq')
Inputs may be any that keep to these rules, and one draw needn't show every extreme that they name: `keep_list`: each aligned block of 128 entries keeps between 32 and 64 of them; in every draw the 2048 entries of one index of seq keep 128 // 2 of every block. `req_blocks`: blocks of each request's cache in order; they sum to 256. `tenant_sizes`: requests of each tenant in order; they sum to 128.
All inputs are finite; a program needn't handle non-finite values.
Results may differ from a plain program's by a relative error of at most 0.007.
Values may be sent and summed in bfloat16 or wider, within the bound.
No kernel may reach another device: no remote copies, remote signals or barrier semaphores. Data moves between devices by JAX's collectives and lax.ppermute only.
A program may use at most 192 MiB of HBM per device.

v0:
```python
import math

import jax
import jax.numpy as jnp
from jax import lax
from jax.sharding import PartitionSpec as P

D = 5120
BLK = 128


def entering(shard, axis, combine, identity):
    size, mine = (lax.axis_size(axis), lax.axis_index(axis))
    everything = lax.all_gather(shard, axis)
    start = jnp.broadcast_to(jnp.asarray(identity, shard.dtype), shard.shape)

    def lap(k, before):
        reached = k < mine
        new = combine(before, everything[k])
        return jnp.where(reached, new, before)

    return lax.fori_loop(0, size, lap, start)


def merged_2(value, axis, join):
    pieces = jax.tree.map(lambda part: lax.all_gather(part, axis), value)
    head = jax.tree.map(lambda part: part[0], pieces)
    tail = jax.tree.map(lambda part: part[1:], pieces)
    running, _ = lax.scan(lambda running, piece: (join(running, piece), None), head, tail)
    return running


def owner_index(positions, bounds):
    return jnp.sum((positions[:, None] >= bounds[None, :]).astype(jnp.int32), axis=1)


def residue_count(limit, residue, modulus):
    return (limit + modulus - 1 - residue) // modulus


def partial_softmax(rows, row_ids, row_bias, query_heads, requests):
    head_size = rows.shape[-1] // 2
    score_scale = 1.0 / math.sqrt(head_size)
    safe_ids = jnp.minimum(row_ids, requests - 1)
    picked = query_heads[safe_ids]
    scores = jnp.einsum(
        "nkgd,nkd->nkg", picked, rows[..., :head_size], preferred_element_type=jnp.float32
    )
    scores = scores * score_scale + row_bias[:, None, None]
    member = row_ids[:, None] == jnp.arange(requests, dtype=jnp.int32)[None, :]
    onehot = member.astype(jnp.float32)
    masked = jnp.where(member[:, None, None, :], scores[..., None], -jnp.inf)
    row_max = jnp.maximum(jnp.max(masked, axis=0), -1e30)
    row_max = jnp.transpose(row_max, (2, 0, 1))
    max_rows = jnp.einsum("nr,rkg->nkg", onehot, row_max, precision=lax.Precision.HIGHEST)
    weights = jnp.exp(scores - max_rows)
    totals = jnp.einsum("nr,nkg->rkg", onehot, weights, precision=lax.Precision.HIGHEST)
    weighted_onehot = weights[..., None] * onehot[:, None, None, :]
    values = rows[..., head_size:].astype(jnp.float32)
    mixed_sum = jnp.einsum(
        "nkgr,nkd->rkgd", weighted_onehot, values, precision=lax.Precision.HIGHEST
    )
    return (row_max, totals, mixed_sum)


def join_parts(earlier, later):
    row_max = jnp.maximum(earlier[0], later[0])
    first_factor = jnp.exp(earlier[0] - row_max)
    second_factor = jnp.exp(later[0] - row_max)
    totals = earlier[1] * first_factor + later[1] * second_factor
    mixed_sum = earlier[2] * first_factor[..., None] + later[2] * second_factor[..., None]
    return (row_max, totals, mixed_sum)


def add_counts(earlier, later):
    return earlier + later


def shards(
    kv_cache,
    keep_list,
    drop_level,
    drop_table,
    req_blocks,
    tenant_sizes,
    queries,
    residual,
    w_out,
    norm_gain,
    w_gate,
    w_up,
    w_down,
):
    entries, kv_local, width_two = kv_cache.shape
    head_size = width_two // 2
    requests = queries.shape[0]
    groups = queries.shape[1] // kv_local
    seq_devices = lax.axis_size("seq")
    own_index = lax.axis_index("seq")
    local_blocks = entries // BLK
    new_slots = entries // 2
    slot_rows = new_slots // seq_devices
    request_ids = jnp.arange(requests, dtype=jnp.int32)
    block_ids = own_index * local_blocks + jnp.arange(local_blocks, dtype=jnp.int32)
    block_req = owner_index(block_ids, jnp.cumsum(req_blocks))
    req_tenant = owner_index(request_ids, jnp.cumsum(tenant_sizes))
    block_match = block_req[:, None] == request_ids[None, :]
    block_tenant = jnp.sum(jnp.where(block_match, req_tenant[None, :], 0), axis=1)
    tenant_onehot = (
        block_tenant[:, None] == jnp.arange(drop_table.shape[0], dtype=jnp.int32)[None, :]
    ).astype(jnp.float32)
    table_rows = jnp.dot(tenant_onehot, drop_table, precision=lax.Precision.HIGHEST)
    level_rows = drop_level.reshape(local_blocks, BLK)
    level_onehot = (
        level_rows[:, :, None] == jnp.arange(drop_table.shape[1], dtype=jnp.int32)[None, None, :]
    )
    weight_rows = jnp.sum(jnp.where(level_onehot, table_rows[:, None, :], 0.0), axis=2)
    keep_rows = keep_list.reshape(local_blocks, BLK)
    drop_weight = jnp.where(keep_rows == 1, 0.0, weight_rows).astype(jnp.bfloat16)
    drop_mass = jnp.sum(drop_weight.astype(jnp.float32), axis=1)
    block_rows = kv_cache.reshape(local_blocks, BLK, kv_local * width_two)
    numer = jnp.einsum("bi,bic->bc", drop_weight, block_rows, preferred_element_type=jnp.float32)
    summaries = (
        (numer / drop_mass[:, None]).astype(jnp.bfloat16).reshape(local_blocks, kv_local, width_two)
    )
    kept_local = jnp.sum(keep_list)
    kept_rank = jnp.cumsum(keep_list) - 1
    peer_ids = jnp.arange(seq_devices, dtype=jnp.int32)
    before = entering(kept_local[None], "seq", add_counts, jnp.zeros((1,), jnp.int32))
    offset = before[0]
    sent_counts = residue_count(offset + kept_local, peer_ids, seq_devices) - residue_count(
        offset, peer_ids, seq_devices
    )
    from_each = lax.all_to_all(
        sent_counts.astype(jnp.int32), "seq", split_axis=0, concat_axis=0, tiled=True
    )
    new_position = offset + kept_rank
    destination = new_position % seq_devices
    lead_residue = offset % seq_devices
    slot_index = (
        new_position // seq_devices
        - offset // seq_devices
        - (destination < lead_residue).astype(jnp.int32)
    )
    send_slot = jnp.where(
        keep_list == 1, destination * slot_rows + slot_index, seq_devices * slot_rows
    ).astype(jnp.int32)
    outgoing = (
        jnp.zeros((seq_devices * slot_rows, kv_local, width_two), jnp.bfloat16)
        .at[send_slot]
        .set(kv_cache, mode="drop")
    )
    outgoing = outgoing.reshape(seq_devices, slot_rows, kv_local, width_two)
    incoming = lax.all_to_all(outgoing, "seq", split_axis=0, concat_axis=0, tiled=True)
    incoming_start = jnp.cumsum(from_each) - from_each
    slot_range = jnp.arange(slot_rows, dtype=jnp.int32)
    place_at = jnp.where(
        slot_range[None, :] < from_each[:, None],
        incoming_start[:, None] + slot_range[None, :],
        new_slots,
    )
    packed = (
        jnp.zeros((new_slots, kv_local, width_two), jnp.bfloat16)
        .at[place_at.reshape(-1)]
        .set(incoming.reshape(seq_devices * slot_rows, kv_local, width_two), mode="drop")
    )
    query_heads = queries.reshape(requests, kv_local, groups, head_size)
    summary_part = partial_softmax(summaries, block_req, jnp.log(drop_mass), query_heads, requests)
    block_kept = jnp.sum(keep_rows, axis=1)
    local_totals = jnp.sum(jnp.where(block_match, block_kept[:, None], 0), axis=0)
    request_kept = lax.psum(local_totals, "seq")
    slot_position = jnp.arange(new_slots, dtype=jnp.int32) * seq_devices + own_index
    slot_req = owner_index(slot_position, jnp.cumsum(request_kept))
    slot_bias = jnp.where(slot_req < requests, 0.0, -jnp.inf).astype(jnp.float32)
    entry_part = partial_softmax(packed, slot_req, slot_bias, query_heads, requests)
    local_part = join_parts(entry_part, summary_part)
    merged = merged_2(local_part, "seq", join_parts)
    attended = (
        (merged[2] / merged[1][..., None])
        .astype(jnp.bfloat16)
        .reshape(requests, kv_local * groups * head_size)
    )
    projected = lax.psum(jnp.dot(attended, w_out, preferred_element_type=jnp.float32), "mp")
    hidden_in = residual.astype(jnp.float32) + projected
    square_total = lax.psum(jnp.sum(hidden_in * hidden_in, axis=1), "seq")
    normed = (hidden_in * lax.rsqrt(square_total / D + 1e-05)[:, None] * norm_gain).astype(
        jnp.bfloat16
    )
    piece_rows = lax.all_gather(normed, "seq", axis=1, tiled=True)
    gate_next = jnp.dot(piece_rows, w_gate, preferred_element_type=jnp.float32)
    up_next = jnp.dot(piece_rows, w_up, preferred_element_type=jnp.float32)
    hidden = (jax.nn.silu(gate_next) * up_next).astype(jnp.bfloat16)
    down_terms = jnp.dot(hidden, w_down, preferred_element_type=jnp.float32)
    down_local = lax.psum_scatter(down_terms, "seq", scatter_dimension=1, tiled=True)
    down_local = lax.psum(down_local.astype(jnp.bfloat16), "mp").astype(jnp.float32)
    final = (hidden_in + down_local).astype(jnp.bfloat16)
    return (summaries, packed[None], final)


def solution(mesh):
    placed = (
        P("seq", "mp", None),
        P("seq"),
        P("seq"),
        P(),
        P(),
        P(),
        P(None, "mp", None),
        P(None, "seq"),
        P("mp", "seq"),
        P("seq"),
        P(None, ("seq", "mp")),
        P(None, ("seq", "mp")),
        P(("seq", "mp"), None),
    )
    return jax.shard_map(
        shards,
        mesh=mesh,
        in_specs=placed,
        out_specs=(P("seq", "mp", None), P("seq", None, "mp", None), P(None, "seq")),
        check_vma=False,
    )
```

profile of v0, /device:TPU:0, one launch (start us, length us, event | category | flops | bytes accessed | tf_op | source)
XLA Modules:
  0.0 1078.6 jit_solution(3971147169600702661)
XLA Ops:
  14.3 16.2 %all-reduce.1 = (s32[16]{0:T(128)S(1)}, s32[128,1]{0,1:T(1,128)S(1)}) all-reduce(s32[16]{0:T(128)S(1)} %dynamic-update-slice, s32[128,1]{0,1:T(1,128)S(1)} %bitcast.203), channel_id=1, replica_groups=mesh['seq'=16,'mp'=2] {'seq'}, use_global_device_ids=true, to_apply=%add | all-reduce | flops 144 | bytes 1152
  30.5 20.4 %while.27 = (s32[]{:T(128)}, s32[1]{0:T(128)}, s32[]{:T(128)}, s32[16,1]{0,1:T(1,128)S(1)}, s32[]{:T(128)}) while((s32[]{:T(128)}, s32[1]{0:T(128)}, s32[]{:T(128)}, s32[16,1]{0,1:T(1,128)S(1)}, s32[]{:T(128)}) %tuple.88), condition=%wide.region_9.10_spmd, body=%wide.region_8.9_spmd.sunk | while | flops 5 | bytes 115 | solution.py:22
  52.3 3.5 all-to-all-start
  60.0 7.7 reshape.447
  67.8 1.9 broadcast.327.clone
  69.7 246.9 %scatter_fusion = bf16[1024,4,256]{2,1,0:T(4,128)(2,1)} fusion(bf16[1024,4,256]{2,1,0:T(4,128)(2,1)} %broadcast.327.clone, s32[2048]{0:T(1024)S(1)} %compare_select_fusion.2, bf16[2048,4,256]{2,1,0:T(4,128)(2,1)} %param.17), kind=kCustom, calls=%fused_computation.2 | custom fusion | bytes 12591104 | tf_op jit(solution)/shard_map/scatter | solution.py:151
  316.6 3.4 copy.91
  320.6 9.1 all-to-all-start.1
  330.4 10.9 %gather_fusion = bf16[1024,4,4,128]{3,2,1,0:T(4,128)(2,1)} fusion(bf16[128,4,4,128]{3,2,1,0:T(4,128)(2,1)S(1)} %bitcast.180, s32[1024]{0:T(1024)S(1)} %broadcast_clamp_fusion), kind=kCustom, calls=%fused_computation | custom fusion | bytes 8392704 | tf_op jit(solution)/shard_map/gather | solution.py:45
  341.2 2.8 fusion.48
  349.1 20.0 %all-to-all-done.1 = bf16[16,64,4,256]{3,1,2,0:T(8,128)(2,1)} async-done(((bf16[16,64,4,256]{3,1,2,0:T(8,128)(2,1)}), bf16[16,64,4,256]{3,1,2,0:T(8,128)(2,1)}, u32[]{:S(2)}, u32[]{:S(2)}) %all-to-all-start.1) | async-done | bytes 2097184 | tf_op jit(solution)/shard_map/all_to_all | solution.py:154
  369.1 1.7 copy.92
  370.8 2.9 copy.93
  374.3 75.0 %scatter_fusion.1 = bf16[1024,4,256]{2,1,0:T(4,128)(2,1)S(1)} fusion(bf16[1024,4,256]{2,1,0:T(4,128)(2,1)S(1)} %broadcast.327, s32[1024]{0:T(1024)} %bitcast.198, bf16[1024,4,256]{2,1,0:T(4,128)(2,1)} %copy.93), kind=kCustom, calls=%fused_computation.3 | custom fusion | bytes 6295552 | tf_op jit(solution)/shard_map/scatter | solution.py:165
  449.3 2.1 fusion.65
  451.4 8.3 fusion.6
  459.7 5.5 copy.106
  466.1 2.7 select_reduce_fusion
  471.0 5.2 fusion.13
  476.2 1.7 fusion.9
  478.2 45.3 %all-gather = f32[2048,4,4]{0,2,1:T(4,128)S(1)} all-gather(f32[128,4,4]{0,2,1:T(4,128)S(1)} %get-tuple-element.201), channel_id=2, replica_groups=mesh['seq'=16,'mp'=2] {'seq'}, dimensions={0}, use_global_device_ids=true | all-gather | bytes 139264 | tf_op jit(solution)/shard_map/all_gather | solution.py:26
  523.9 37.3 %all-gather.1 = f32[2048,4,4]{0,2,1:T(4,128)S(1)} all-gather(f32[128,4,4]{0,2,1:T(4,128)S(1)} %fusion.18), channel_id=3, replica_groups=mesh['seq'=16,'mp'=2] {'seq'}, dimensions={0}, use_global_device_ids=true | all-gather | bytes 139264 | tf_op jit(solution)/shard_map/all_gather | solution.py:26
  562.6 157.2 %all-gather.8.cloned.1.call-done = f32[2048,4,4,128]{0,3,2,1:T(8,128)} async-done(((f32[128,4,4,128]{0,3,2,1:T(8,128)}), f32[2048,4,4,128]{0,3,2,1:T(8,128)}) %all-gather.8.cloned.1.call-update) | async-done | bytes 16777232 | tf_op jit(solution)/shard_map/all_gather | solution.py:26
  719.8 12.6 %slice.70 = f32[1920,4,4,128]{0,3,2,1:T(8,128)} slice(f32[2048,4,4,128]{0,3,2,1:T(8,128)} %all-gather.8.cloned.1.call-done), slice={[128:2048], [0:4], [0:4], [0:128]} | slice | bytes 31457280 | tf_op jit(solution)/shard_map/slice | solution.py:28
  732.3 15.7 %copy.97 = f32[1920,4,4,128]{3,0,2,1:T(8,128)} copy(f32[1920,4,4,128]{0,3,2,1:T(8,128)} %slice.70) | data formatting | bytes 31457280 | tf_op jit(solution)/shard_map/slice | solution.py:28
  748.8 87.2 %while.28 = (s32[]{:T(128)}, f32[128,4,4]{0,2,1:T(4,128)S(1)}, f32[128,4,4]{0,2,1:T(4,128)S(1)}, f32[128,4,4,128]{3,2,1,0:T(4,128)S(1)}, f32[15,128,4,4]{1,0,3,2...) while((s32[]{:T(128)}, f32[128,4,4]{0,2,1:T(4,128)S(1)}, ...), condition=%wide.region_23.24_spmd, body=%wide.region_22.23_spmd.sunk | while | flops 798722 | bytes 5390437 | solution.py:29
  751.3 3.2 fusion.84
  757.1 3.2 fusion.84
  763.0 3.2 fusion.84
  768.8 3.2 fusion.84
  774.6 3.2 fusion.84
  780.4 3.2 fusion.84
  786.2 3.2 fusion.84
  792.0 3.2 fusion.84
  797.8 3.2 fusion.84
  803.6 3.2 fusion.84
  809.5 3.2 fusion.84
  815.3 3.2 fusion.84
  821.1 3.2 fusion.84
  826.9 3.2 fusion.84
  832.7 3.2 fusion.84
  838.5 16.3 %all-reduce.5.cloned.1.call-done = f32[128,320]{0,1:T(8,128)} async-done(((f32[128,320]{0,1:T(8,128)}), f32[128,320]{0,1:T(8,128)}) %all-reduce.5.cloned.1.call-update) | async-done | bytes 163856 | tf_op jit(solution)/shard_map/psum | solution.py:183
  855.8 41.9 %psum.30 = f32[128]{0:T(128)S(1)} all-reduce(f32[128]{0:T(128)S(1)} %multiply_reduce_fusion), channel_id=1, replica_groups=mesh['seq'=16,'mp'=2] {'seq'}, use_global_device_ids=true, to_apply=%region_26.27 | all-reduce | flops 128 | bytes 1024 | tf_op jit(solution)/shard_map/psum | solution.py:185
  899.8 52.6 %all-gather.6.cloned.1.call-done = bf16[128,5120]{0,1:T(8,128)(2,1)} async-done(((bf16[128,320]{0,1:T(8,128)(2,1)}), bf16[128,5120]{0,1:T(8,128)(2,1)}) %all-gather.6.cloned.1.call-update) | async-done | bytes 1310736 | tf_op jit(solution)/shard_map/all_gather | solution.py:189
  952.3 6.0 fusion.68
  958.4 13.2 %fusion.20 = f32[128,5120]{0,1:T(8,128)} fusion(bf16[1024,5120]{1,0:T(8,128)(2,1)} %param.29, bf16[128,5120]{0,1:T(8,128)(2,1)S(1)} %copy-done.3, bf16[5120,1024]{1,0:T(8,128)(2,1)} %param.28, f32[128,1024]{1,0:T(8,128)S(1)} %fusion.68), kind=kOutput, calls=%fused_computation.35 | convolution fusion | flops 2685140992 | bytes 25427968 | tf_op jit(solution)/shard_map/dot_general | solution.py:193
  971.7 81.3 %reduce-scatter.2.cloned.1.call-done = f32[128,320]{0,1:T(8,128)} async-done(((f32[128,5120]{0,1:T(8,128)}), f32[128,320]{0,1:T(8,128)}) %reduce-scatter.2.cloned.1.call-update) | async-done | bytes 163856 | tf_op jit(solution)/shard_map/reduce_scatter | solution.py:194
  1054.5 16.0 %all-reduce.7.cloned.1.call-done = bf16[128,320]{0,1:T(8,128)(2,1)} async-done(((bf16[128,320]{0,1:T(8,128)(2,1)}), bf16[128,320]{0,1:T(8,128)(2,1)}) %all-reduce.7.cloned.1.call-update) | async-done | bytes 81936 | tf_op jit(solution)/shard_map/psum | solution.py:195
  (211 shorter events, 81.4 us)
Async XLA Ops:
  7.2 830.1 %copy-start = (bf16[2048,320]{0,1:T(8,128)(2,1)S(1)}, bf16[2048,320]{0,1:T(8,128)(2,1)}, u32[]{:S(2)}) copy-start(bf16[2048,320]{0,1:T(8,128)(2,1)} %param.25) | copy-start | bytes 3932164
  12.8 333.2 %copy-start.12 = (s32[16]{0:T(128)}, s32[16]{0:T(128)S(1)}, u32[]{:S(2)}) copy-start(s32[16]{0:T(128)S(1)} %get-tuple-element.206) | copy-start | bytes 196
  52.3 268.3 %all-to-all-start = ((s32[16,1,1]{2,1,0:T(1,128)}), s32[16,1,1]{2,1,0:T(1,128)S(1)}, u32[]{:S(2)}, u32[]{:S(2)}) async-start(s32[16,1,1]{2,1,0:T(1,128)} %fusion.50), calls=%async_computation | async-start | bytes 16384 | tf_op jit(solution)/shard_map/all_to_all | solution.py:134
  60.0 7.7 copy-start.7
  316.6 3.4 copy-start.1
  320.6 48.5 %all-to-all-start.1 = ((bf16[16,64,4,256]{3,1,2,0:T(8,128)(2,1)}), bf16[16,64,4,256]{3,1,2,0:T(8,128)(2,1)}, u32[]{:S(2)}, u32[]{:S(2)}) async-start(bf16[16,64,4,256]{3,1,2,0:T(8,128)(2,1)} %copy.91), calls=%async_computation.1 | async-start | bytes 4194304 | tf_op jit(solution)/shard_map/all_to_all | solution.py:154
  329.7 390.0 %all-gather.8.cloned.1.call-start = ((), (), s32[]{:S(2)}) async-start(), calls=%async_computation.7 | async-start | bytes 17825792 | tf_op jit(solution)/shard_map/all_gather | solution.py:26
  344.2 29.6 %copy-start.8 = (bf16[16,4,256]{2,1,0:T(4,128)(2,1)}, bf16[16,4,256]{2,1,0:T(4,128)(2,1)S(1)}, u32[]{:S(2)}) copy-start(bf16[16,4,256]{2,1,0:T(4,128)(2,1)S(1)} %reshape.448) | copy-start | bytes 98308
  449.3 10.4 copy-start.2
  465.2 10.9 %copy-start.9 = (bf16[16,4,128]{2,1,0:T(4,128)(2,1)S(1)}, bf16[16,4,128]{2,1,0:T(4,128)(2,1)}, u32[]{:S(2)}) copy-start(bf16[16,4,128]{2,1,0:T(4,128)(2,1)} %get-tuple-element.197) | copy-start | bytes 49156
  465.2 10.9 %copy-start.10 = (f32[16,4,4]{0,2,1:T(4,128)S(1)}, f32[16,4,4]{0,2,1:T(4,128)}, u32[]{:S(2)}) copy-start(f32[16,4,4]{0,2,1:T(4,128)} %subtract_exponential_fusion.2) | copy-start | bytes 3076
  465.2 11.0 %copy-start.11 = (f32[16,128]{1,0:T(8,128)S(1)}, f32[16,128]{1,0:T(8,128)}, u32[]{:S(2)}) copy-start(f32[16,128]{1,0:T(8,128)} %get-tuple-element.204) | copy-start | bytes 24580
  470.9 7.0 copy-start.13
  477.9 376.9 %all-reduce.5.cloned.1.call-start = ((), (), s32[]{:S(2)}) async-start(), calls=%async_computation.3 | async-start | bytes 327680 | tf_op jit(solution)/shard_map/psum | solution.py:183
  523.4 208.9 %copy-start.6 = (f32[2048,4,4]{0,2,1:T(4,128)}, f32[2048,4,4]{0,2,1:T(4,128)S(1)}, u32[]{:S(2)}) copy-start(f32[2048,4,4]{0,2,1:T(4,128)S(1)} %all-gather) | copy-start | bytes 393220
  732.3 15.7 %slice-start = ((f32[2048,4,4,128]{0,3,2,1:T(8,128)}), f32[128,4,4,128]{0,3,2,1:T(8,128)S(1)}, s32[]{:S(2)}) async-start(f32[2048,4,4,128]{0,3,2,1:T(8,128)} %all-gather.8.cloned.1.call-done), calls=%async_computation.8 | async-start | bytes 2097152 | tf_op jit(solution)/shard_map/slice | solution.py:27
  748.0 0.7 slice-start.1
  835.9 18.9 %copy-start.5 = (bf16[128,320]{0,1:T(8,128)(2,1)S(1)}, bf16[128,320]{0,1:T(8,128)(2,1)}, u32[]{:S(2)}) copy-start(bf16[128,320]{0,1:T(8,128)(2,1)} %param.24) | copy-start | bytes 245764
  835.9 61.8 %copy-start.14 = (f32[320]{0:T(512)S(1)}, f32[320]{0:T(512)}, u32[]{:S(2)}) copy-start(f32[320]{0:T(512)} %param.26) | copy-start | bytes 3844
  838.5 113.9 %all-gather.6.cloned.1.call-start = ((), (), s32[]{:S(2)}) async-start(), calls=%async_computation.4 | async-start | bytes 1392640 | tf_op jit(solution)/shard_map/all_gather | solution.py:189
  899.4 153.5 %reduce-scatter.2.cloned.1.call-start = ((), (), s32[]{:S(2)}) async-start(), calls=%async_computation.5 | async-start | bytes 2785280 | tf_op jit(solution)/shard_map/reduce_scatter | solution.py:194
  952.3 6.0 copy-start.3
  958.3 112.2 %copy-start.4 = (f32[128,320]{0,1:T(8,128)S(1)}, f32[128,320]{0,1:T(8,128)}, u32[]{:S(2)}) copy-start(f32[128,320]{0,1:T(8,128)} %all-reduce.5.cloned.1.call-done) | copy-start | bytes 491524
  971.6 98.9 %all-reduce.7.cloned.1.call-start = ((), (), s32[]{:S(2)}) async-start(), calls=%async_computation.6 | async-start | bytes 163840 | tf_op jit(solution)/shard_map/psum | solution.py:195
Sparse Core Ops, SparseCore 0:
  478.0 241.6 all-gather.7
  838.6 16.1 all-reduce.4
  899.6 52.7 all-gather.5
  971.7 81.1 reduce-scatter.1
  1055.6 14.8 all-reduce.6
where the time goes:
time: 1100 us; the launch traced here: 1080 us
  local copies, waits for them, and re-layouts  444 us (40%)
  waiting for transfers between devices  343 us (31%)
  blocking collectives  141 us (13%)
  other arithmetic  70 us (6%)
  matrix products  40.8 us (4%)
  between operations  14.9 us (1%)
  starting transfers between devices  13.2 us (1%)
  loops' own time  11.5 us (1%)
    scatter x1, local copies, waits for them, and re-layouts, shards(): outgoing = jnp.zeros((seq_devices * slot_rows, kv_local, width_two), jnp....  247 us
    all_gather x1, waiting for transfers between devices, merged_2(): pieces = jax.tree.map(lambda part: lax.all_gather(part, axis), value)  157 us
    all_gather x2, blocking collectives, merged_2(): pieces = jax.tree.map(lambda part: lax.all_gather(part, axis), value)  82.6 us
    reduce_scatter x1, waiting for transfers between devices, shards(): lax.psum_scatter(down_terms, 'seq', scatter_dimension=1, tiled=True)  81.3 us
    scatter x1, local copies, waits for them, and re-layouts, shards(): packed = jnp.zeros((new_slots, kv_local, width_two), jnp.bfloat16).at[pla...  75 us
    all_gather x1, waiting for transfers between devices, shards(): piece_rows = lax.all_gather(normed, 'seq', axis=1, tiled=True)  52.6 us
    add x15, other arithmetic, join_parts(): earlier[2] * first_factor[..., None] + later[2] * second_factor[..., None]  48.1 us
    psum x1, blocking collectives, shards(): square_total = lax.psum(jnp.sum(hidden_in * hidden_in, axis=1), 'seq')  41.9 us
  transfers between devices with their start and end apart: 7, of which 6 were waited for; matrix products, arithmetic and copies ran while one was open for 26% of the time, Pallas kernels for 0%

commit v1 on v0

v1 whole, which is shorter than its diff:
```python
import functools
import math

import jax
import jax.numpy as jnp
from jax import lax
from jax.experimental import pallas as pl
from jax.experimental.pallas import tpu as pltpu
from jax.sharding import PartitionSpec as P

BLK = 128
LANE = 128
STAT = 16
BF = jnp.bfloat16
F32 = jnp.float32
VMEM = pl.BlockSpec(memory_space=pltpu.VMEM)
SMEM = pl.BlockSpec(memory_space=pltpu.SMEM)
ANY = pl.BlockSpec(memory_space=pl.ANY)
MIB = 1 << 20


def params(mib):
    return pltpu.CompilerParams(vmem_limit_bytes=mib * MIB)


def three(value):
    hi = value.astype(BF).astype(F32)
    mid = (value - hi).astype(BF).astype(F32)
    lo = (value - hi - mid).astype(BF).astype(F32)
    return hi, mid, lo


def attend_kernel(kvl, breq, bten, table, kv_any, keep_ref, level_ref, q_ref,
                  o_ref, sum_ref, rank_ref, kv, o_scr, sum_scr, sem):
    nb = keep_ref.shape[0]
    heads = q_ref.shape[1]
    groups = heads // kvl
    rpe = 2 * kvl
    rows = BLK * rpe
    levels = table.shape[1]
    copies = []
    for b in range(nb):
        c = pltpu.make_async_copy(kv_any.at[pl.ds(b * rows, rows)], kv.at[pl.ds(b * rows, rows)], sem.at[b])
        c.start()
        copies.append(c)
    keep = keep_ref[...]
    keep_f = keep.astype(F32)
    up = (lax.broadcasted_iota(jnp.int32, (BLK, BLK), 0) <= lax.broadcasted_iota(jnp.int32, (BLK, BLK), 1))
    within = jnp.dot(keep_f.astype(BF), up.astype(F32).astype(BF), preferred_element_type=F32)
    count = jnp.broadcast_to(jnp.sum(keep_f, axis=1, keepdims=True), (nb, BLK))
    before = jnp.zeros((nb, BLK), F32)
    row_id = lax.broadcasted_iota(jnp.int32, (nb, BLK), 0)
    for b in range(nb - 1):
        before = before + jnp.where(row_id > b, count[b:b + 1], 0.0)
    rank_ref[...] = jnp.where(keep == 1, (within + before).astype(jnp.int32) - 1, -1)
    weights = []
    for b in range(nb):
        tenant = bten[b]
        level = level_ref[b:b + 1, :]
        w = jnp.zeros((1, BLK), F32)
        for j in range(levels):
            w = jnp.where(level == j, table[tenant, j], w)
        weights.append(w)
    weight = jnp.where(keep == 1, 0.0, jnp.concatenate(weights, axis=0)).astype(BF)
    mass = jnp.sum(weight.astype(F32), axis=1, keepdims=True)
    log_mass = jnp.log(mass)
    spread = (lax.broadcasted_iota(jnp.int32, (BLK, rows), 1) // rpe
              == lax.broadcasted_iota(jnp.int32, (BLK, rows), 0)).astype(F32).astype(BF)
    wide = jnp.dot(jnp.concatenate([keep_f.astype(BF), weight], axis=0), spread, preferred_element_type=F32)
    lane_in = lax.broadcasted_iota(jnp.int32, (heads, rows), 1) % rpe
    head_of = lax.broadcasted_iota(jnp.int32, (heads, rows), 0) // groups
    is_key = lane_in == head_of
    is_value = lane_in == head_of + kvl
    scale = 1.0 / math.sqrt(LANE)
    lse_all = jnp.zeros((heads, LANE), F32)
    lane_id = lax.broadcasted_iota(jnp.int32, (heads, LANE), 1)
    for b in range(nb):
        copies[b].wait()
        block = kv[b * rows:(b + 1) * rows, :]
        q = q_ref[breq[b]]
        s = lax.dot_general(q, block, (((1,), (1,)), ((), ())), preferred_element_type=F32) * scale
        valid = is_key & (wide[b:b + 1] > 0.5)
        s = jnp.where(valid, s, -1e30)
        m = jnp.max(s, axis=1, keepdims=True)
        p = jnp.where(valid, jnp.exp(s - m), 0.0)
        total = jnp.sum(p, axis=1, keepdims=True)
        p = pltpu.roll(p, kvl, 1)
        p_hi = p.astype(BF)
        p_lo = (p - p_hi.astype(F32)).astype(BF)
        w_row = wide[nb + b:nb + b + 1]
        w_key = jnp.where(is_key, w_row, 0.0).astype(BF)
        w_val = jnp.where(is_value, w_row, 0.0).astype(BF)
        left = jnp.concatenate([p_hi, p_lo, w_key, w_val], axis=0)
        out = jnp.dot(left, block, preferred_element_type=F32)
        o = out[:heads] + out[heads:2 * heads]
        s_key = (out[2 * heads:3 * heads] / mass[b:b + 1]).astype(BF).astype(F32)
        s_val = (out[3 * heads:] / mass[b:b + 1]).astype(BF).astype(F32)
        s_score = jnp.sum(q.astype(F32) * s_key, axis=1, keepdims=True) * scale + log_mass[b:b + 1]
        top = jnp.maximum(m, s_score)
        a = jnp.exp(m - top)
        e = jnp.exp(s_score - top)
        total = total * a + e
        o_scr[:, b, :] = (o * a + s_val * e) / total
        lse_all = jnp.where(lane_id == b, top + jnp.log(total), lse_all)
        for h in range(kvl):
            sum_scr[b, h:h + 1, :LANE] = s_key[h * groups:h * groups + 1]
            sum_scr[b, h:h + 1, LANE:] = s_val[h * groups:h * groups + 1]
    o_ref[:heads] = o_scr[...].astype(BF)
    sum_ref[...] = sum_scr[...].astype(BF)
    square = jnp.concatenate([lse_all, jnp.zeros((LANE - heads, LANE), F32)], axis=0)
    lse = jnp.transpose(square)[:nb]
    hi, mid, lo = three(lse)
    o_ref[heads] = (hi + pltpu.roll(mid, 32, 1) + pltpu.roll(lo, 64, 1)).astype(BF)


def attend(kv_rows, keep, level, queries, breq, bten, table, kvl):
    nb = keep.shape[0]
    heads = queries.shape[1]
    return pl.pallas_call(
        functools.partial(attend_kernel, kvl),
        out_shape=(
            jax.ShapeDtypeStruct((heads + 1, nb, LANE), BF),
            jax.ShapeDtypeStruct((nb, kvl, 2 * LANE), BF),
            jax.ShapeDtypeStruct((nb, BLK), jnp.int32),
        ),
        in_specs=[SMEM, SMEM, SMEM, ANY, VMEM, VMEM, VMEM],
        out_specs=(VMEM, VMEM, VMEM),
        scratch_shapes=[
            pltpu.VMEM(kv_rows.shape, BF),
            pltpu.VMEM((heads, nb, LANE), F32),
            pltpu.VMEM((nb, kvl, 2 * LANE), F32),
            pltpu.SemaphoreType.DMA((nb,)),
        ],
        compiler_params=params(24),
        cost_estimate=pl.CostEstimate(flops=nb * 2 * 80 * 1024 * 128, bytes_accessed=5 * MIB, transcendentals=nb * 16384),
        name="attend",
    )(breq, bten, table, kv_rows, keep, level, queries)


def compact_kernel(dst, kv_any, out_any, kv, out, sem, out_sem):
    nb = dst.shape[0]
    slots = out_any.shape[0]
    for b in range(nb):
        pltpu.make_async_copy(kv_any.at[pl.ds(b * BLK, BLK)], kv.at[pl.ds(b * BLK, BLK)], sem.at[b]).start()

    def one(b, carry):
        pltpu.make_async_copy(kv_any.at[pl.ds(b * BLK, BLK)], kv.at[pl.ds(b * BLK, BLK)], sem.at[b]).wait()
        for i in range(BLK):
            out[dst[b, i]] = kv[b * BLK + i]
        return carry

    lax.fori_loop(0, nb, one, 0)
    copy = pltpu.make_async_copy(out.at[pl.ds(0, slots)], out_any, out_sem)
    copy.start()
    copy.wait()


def compact(kv_entries, dst, slots):
    nb = dst.shape[0]
    rpe = kv_entries.shape[1]
    return pl.pallas_call(
        compact_kernel,
        out_shape=jax.ShapeDtypeStruct((slots, rpe, LANE), BF),
        in_specs=[SMEM, ANY],
        out_specs=ANY,
        scratch_shapes=[
            pltpu.VMEM(kv_entries.shape, BF),
            pltpu.VMEM((slots + 8, rpe, LANE), BF),
            pltpu.SemaphoreType.DMA((nb,)),
            pltpu.SemaphoreType.DMA,
        ],
        compiler_params=params(16),
        cost_estimate=pl.CostEstimate(flops=0, bytes_accessed=16 * MIB, transcendentals=0),
        name="compact",
    )(dst, kv_entries)


def place_kernel(start, count, total, in_any, out_any, zeros, sem, zero_sem):
    sources, chunk = in_any.shape[0], in_any.shape[1]
    slots = out_any.shape[0]
    zeros[...] = jnp.zeros(zeros.shape, zeros.dtype)

    def piece(s):
        n = count[s]
        return pltpu.make_async_copy(in_any.at[s, pl.ds(0, n)], out_any.at[pl.ds(start[s], n)], sem.at[s])

    def blank(j):
        first = jnp.maximum(total[0], j * chunk)
        n = (j + 1) * chunk - first
        return n, lambda: pltpu.make_async_copy(zeros.at[pl.ds(0, n)], out_any.at[pl.ds(first, n)], zero_sem.at[j])

    for s in range(sources):
        pl.when(count[s] > 0)(lambda s=s: piece(s).start())
    for j in range(slots // chunk):
        n, made = blank(j)
        pl.when(n > 0)(lambda made=made: made().start())
    for s in range(sources):
        pl.when(count[s] > 0)(lambda s=s: piece(s).wait())
    for j in range(slots // chunk):
        n, made = blank(j)
        pl.when(n > 0)(lambda made=made: made().wait())


def place(incoming, start, count, total):
    sources, chunk, rpe, _ = incoming.shape
    slots = sources * chunk
    return pl.pallas_call(
        place_kernel,
        out_shape=jax.ShapeDtypeStruct((slots, rpe, LANE), BF),
        in_specs=[SMEM, SMEM, SMEM, ANY],
        out_specs=ANY,
        scratch_shapes=[
            pltpu.VMEM((chunk, rpe, LANE), BF),
            pltpu.SemaphoreType.DMA((sources,)),
            pltpu.SemaphoreType.DMA((slots // chunk,)),
        ],
        cost_estimate=pl.CostEstimate(flops=0, bytes_accessed=4 * MIB, transcendentals=0),
        name="place",
    )(start, count, total, incoming)


def strides(size):
    inner = max(size // 4, 1)
    return [j * inner for j in range(size // inner)], list(range(inner))


def swap(value, axis, size, distance):
    return lax.ppermute(value, axis, [(i, i ^ distance) for i in range(size)])


def gather_xor(value, size):
    outer, inner = strides(size)
    near = jnp.stack([value if d == 0 else swap(value, "seq", size, d) for d in outer])
    return [near if k == 0 else swap(near, "seq", size, k) for k in inner]


def relative(size, own, position):
    outer, inner = strides(size)
    n = len(outer)
    return own ^ ((position % n) * len(inner)) ^ (position // n)


def project_kernel(size, halves, place_ref, ends_ref, starts_ref, w_ref, *refs):
    parts = refs[:len(strides(size)[1])]
    outs, (att, full) = refs[len(parts):-2], refs[-2:]
    heads = parts[0].shape[1] - 1
    nb = parts[0].shape[2]
    blocks = size * nb
    requests = ends_ref.shape[1]
    own, half = place_ref[0], place_ref[1]
    at = lax.broadcasted_iota(jnp.int32, (blocks, requests), 0)
    ids = relative(size, own, at // nb) * nb + at % nb
    member = (ids >= starts_ref[...]) & (ids < ends_ref[...])
    packed = jnp.concatenate([part[:, heads].reshape(-1, LANE) for part in parts], axis=0).astype(F32)
    lse = packed + pltpu.roll(packed, LANE - 32, 1) + pltpu.roll(packed, LANE - 64, 1)
    for g in range(heads):
        column = jnp.where(member, lse[:, g:g + 1], -1e30)
        top = jnp.max(column, axis=0, keepdims=True)
        weight = jnp.where(member, jnp.exp(column - top), 0.0).astype(BF)
        total = jnp.sum(weight.astype(F32), axis=0, keepdims=True)
        o = jnp.concatenate([part[:, g].reshape(-1, LANE) for part in parts], axis=0)
        mixed = lax.dot_general(o, weight, (((0,), (0,)), ((), ())), preferred_element_type=F32)
        att[g * LANE:(g + 1) * LANE, :] = (mixed / total).astype(BF)
    full[...] = jnp.dot(w_ref[...], att[...], preferred_element_type=F32)
    if halves == 2:
        n = full.shape[0] // 2
        outs[0][...] = full[pl.ds(pl.multiple_of(half * n, 8), n), :]
        outs[1][...] = full[pl.ds(pl.multiple_of((1 - half) * n, 8), n), :]
    else:
        outs[0][...] = full[...]


def project(size, halves, where, ends, starts, w_out_t, parts):
    width, depth = w_out_t.shape
    requests = ends.shape[1]
    outs = tuple(jax.ShapeDtypeStruct((width // halves, requests), F32) for _ in range(halves))
    return pl.pallas_call(
        functools.partial(project_kernel, size, halves),
        out_shape=outs,
        in_specs=[SMEM] + [VMEM] * (3 + len(parts)),
        out_specs=tuple(VMEM for _ in outs),
        scratch_shapes=[pltpu.VMEM((depth, requests), BF), pltpu.VMEM((width, requests), F32)],
        compiler_params=params(24),
        cost_estimate=pl.CostEstimate(flops=2 * 128 * 2048 * 600, bytes_accessed=3 * MIB, transcendentals=16 * 32768),
        name="project",
    )(where, ends, starts, w_out_t, *parts)


def stream_kernel(halves, place_ref, res_ref, gain_ref, *refs):
    terms, (hidden_ref, msg_ref) = refs[:-2], refs[-2:]
    n = hidden_ref.shape[0]
    first = pl.multiple_of(place_ref[1] * n, 16) if halves == 2 else 0
    hidden = res_ref[pl.ds(first, n), :].astype(F32)
    for term in terms:
        hidden = hidden + term[...]
    hidden_ref[...] = hidden
    msg_ref[:n, :] = (hidden * gain_ref[pl.ds(first, n), :]).astype(BF)
    squares = jnp.sum(hidden * hidden, axis=0, keepdims=True)
    row = lax.broadcasted_iota(jnp.int32, (STAT, hidden.shape[1]), 0)
    stat = jnp.zeros((STAT, hidden.shape[1]), F32)
    for j, part in enumerate(three(squares)):
        stat = jnp.where(row == j, part, stat)
    msg_ref[n:, :] = stat.astype(BF)


def stream(halves, where, residual_t, gain_wide, terms):
    n, requests = terms[0].shape
    return pl.pallas_call(
        functools.partial(stream_kernel, halves),
        out_shape=(jax.ShapeDtypeStruct((n, requests), F32), jax.ShapeDtypeStruct((n + STAT, requests), BF)),
        in_specs=[SMEM] + [VMEM] * (2 + len(terms)),
        out_specs=(VMEM, VMEM),
        cost_estimate=pl.CostEstimate(flops=n * 512, bytes_accessed=MIB // 2, transcendentals=0),
        name="stream",
    )(where, residual_t, gain_wide, *terms)


def swiglu_kernel(size, halves, chunk, place_ref, gate_any, up_any, down_any, *refs):
    n_in = len(strides(size)[1])
    msgs = [refs[h * n_in:(h + 1) * n_in] for h in range(halves)]
    outs = [refs[(halves + h) * n_in:(halves + h + 1) * n_in] for h in range(halves)]
    gate, up, down, x, xt, acc_g, acc_u, h_scr, full, sem = refs[2 * halves * n_in:]
    width, units = gate.shape
    requests = x.shape[1]
    pieces = width // chunk
    n_outer = len(strides(size)[0])
    own, half = place_ref[0], place_ref[1]
    n = msgs[0][0].shape[1] - STAT

    def copies(i):
        at = pl.ds(i * chunk if isinstance(i, int) else pl.multiple_of(i * chunk, chunk), chunk)
        return (pltpu.make_async_copy(gate_any.at[at], gate.at[at], sem.at[0, i]),
                pltpu.make_async_copy(up_any.at[at], up.at[at], sem.at[1, i]))

    def down_copy(i):
        at = pl.ds(i * chunk if isinstance(i, int) else pl.multiple_of(i * chunk, chunk), chunk)
        return pltpu.make_async_copy(down_any.at[:, at], down.at[:, at], sem.at[2, i])

    for i in range(pieces):
        for c in copies(i):
            c.start()
    for i in range(pieces):
        down_copy(i).start()

    squares = jnp.zeros((1, requests), F32)
    for h in range(halves):
        side = half if h == 0 else 1 - half
        for k in range(n_in):
            for j in range(n_outer):
                s = relative(size, own, k * n_outer + j)
                at = s * (n * halves) + (side * n if halves == 2 else 0)
                x[pl.ds(pl.multiple_of(at, 16), n), :] = msgs[h][k][j, :n, :]
                stat = msgs[h][k][j, n:, :].astype(F32)
                squares = squares + jnp.sum(stat, axis=0, keepdims=True)
    scale = lax.rsqrt(squares / width + 1e-05)
    column = jnp.transpose(jnp.broadcast_to(scale, (requests, requests)))[:, :1]
    for i in range(width // LANE):
        xt[:, i * LANE:(i + 1) * LANE] = jnp.transpose(x[i * LANE:(i + 1) * LANE, :])
    acc_g[...] = jnp.zeros_like(acc_g)
    acc_u[...] = jnp.zeros_like(acc_u)

    def lap(i, carry):
        for c in copies(i):
            c.wait()
        at = pl.ds(pl.multiple_of(i * chunk, chunk), chunk)
        acc_g[...] += jnp.dot(xt[:, at], gate[at, :], preferred_element_type=F32)
        acc_u[...] += jnp.dot(xt[:, at], up[at, :], preferred_element_type=F32)
        return carry

    lax.fori_loop(0, pieces, lap, 0)
    g = acc_g[...] * column
    h_scr[...] = (g / (1.0 + jnp.exp(-g)) * (acc_u[...] * column)).astype(BF)

    def lap_down(i, carry):
        down_copy(i).wait()
        at = pl.ds(pl.multiple_of(i * chunk, chunk), chunk)
        full[at, :] = jnp.transpose(jnp.dot(h_scr[...], down[:, at], preferred_element_type=F32))
        return carry

    lax.fori_loop(0, pieces, lap_down, 0)
    for h in range(halves):
        side = half if h == 0 else 1 - half
        for k in range(n_in):
            for j in range(n_outer):
                s = relative(size, own, k * n_outer + j)
                at = s * (n * halves) + (side * n if halves == 2 else 0)
                outs[h][k][j] = full[pl.ds(pl.multiple_of(at, 8), n), :].astype(outs[h][k].dtype)


def swiglu(size, halves, where, w_gate, w_up, w_down, messages):
    outer, inner = strides(size)
    width, units = w_gate.shape
    requests = messages[0].shape[-1]
    n = messages[0].shape[1] - STAT
    chunk = 512
    outs = tuple(
        jax.ShapeDtypeStruct((len(outer), n, requests), F32 if h == 0 else BF) for h in range(halves) for _ in inner
    )
    return pl.pallas_call(
        functools.partial(swiglu_kernel, size, halves, chunk),
        out_shape=outs,
        in_specs=[SMEM, ANY, ANY, ANY] + [VMEM] * len(messages),
        out_specs=tuple(VMEM for _ in outs),
        scratch_shapes=[
            pltpu.VMEM((width, units), BF),
            pltpu.VMEM((width, units), BF),
            pltpu.VMEM((units, width), BF),
            pltpu.VMEM((width, requests), BF),
            pltpu.VMEM((requests, width), BF),
            pltpu.VMEM((requests, units), F32),
            pltpu.VMEM((requests, units), F32),
            pltpu.VMEM((requests, units), BF),
            pltpu.VMEM((width, requests), F32),
            pltpu.SemaphoreType.DMA((3, width // chunk)),
        ],
        compiler_params=params(56),
        cost_estimate=pl.CostEstimate(
            flops=6 * requests * width * units, bytes_accessed=6 * width * units, transcendentals=requests * units
        ),
        name="swiglu",
    )(where, w_gate, w_up, w_down, *messages)


def shards(
    kv_cache,
    keep_list,
    drop_level,
    drop_table,
    req_blocks,
    tenant_sizes,
    queries,
    residual,
    w_out,
    norm_gain,
    w_gate,
    w_up,
    w_down,
):
    entries, kvl, _ = kv_cache.shape
    requests = queries.shape[0]
    size = lax.axis_size("seq")
    mp = lax.axis_size("mp")
    halves = 2 if mp == 2 else 1
    own = lax.axis_index("seq")
    half = lax.axis_index("mp")
    where = jnp.stack([own, half]).astype(jnp.int32)
    nb = entries // BLK
    slots = entries // 2
    chunk = slots // size
    keep = keep_list.reshape(nb, BLK)
    level = drop_level.reshape(nb, BLK)
    by_entry = kv_cache.reshape(entries, kvl, 2, LANE).transpose(0, 2, 1, 3).reshape(entries, 2 * kvl, LANE)
    by_row = by_entry.reshape(entries * 2 * kvl, LANE)

    kept = jnp.sum(keep_list)
    counts = lax.all_to_all(jnp.broadcast_to(kept, (size,)), "seq", split_axis=0, concat_axis=0, tiled=True)
    seq_ids = jnp.arange(size, dtype=jnp.int32)
    offsets = jnp.sum(jnp.where(seq_ids[None, :] < seq_ids[:, None], counts[None, :], 0), axis=1)
    offset = jnp.sum(jnp.where(seq_ids < own, counts, 0))

    request_ids = jnp.arange(requests, dtype=jnp.int32)
    ends = jnp.sum(jnp.where(request_ids[None, :] <= request_ids[:, None], req_blocks[None, :], 0), axis=1)
    starts = ends - req_blocks
    block_ids = own * nb + jnp.arange(nb, dtype=jnp.int32)
    block_req = jnp.sum((block_ids[:, None] >= ends[None, :]).astype(jnp.int32), axis=1)
    tenants = tenant_sizes.shape[0]
    tenant_ids = jnp.arange(tenants, dtype=jnp.int32)
    tenant_ends = jnp.sum(jnp.where(tenant_ids[None, :] <= tenant_ids[:, None], tenant_sizes[None, :], 0), axis=1)
    block_tenant = jnp.sum((block_req[:, None] >= tenant_ends[None, :]).astype(jnp.int32), axis=1)

    partial, summaries, rank = attend(by_row, keep, level, queries, block_req, block_tenant, drop_table, kvl)

    position = offset + rank
    owner = position % size
    slot = position // size - (offset + size - 1 - owner) // size
    dst = jnp.where(rank >= 0, owner * chunk + slot, slots).astype(jnp.int32)
    outgoing = compact(by_entry, dst, slots).reshape(size, chunk, 2 * kvl, LANE)
    incoming = lax.all_to_all(outgoing, "seq", split_axis=0, concat_axis=0, tiled=True)
    first = (offsets + size - 1 - own) // size
    past = (offsets + counts + size - 1 - own) // size
    filled = (jnp.sum(counts) + size - 1 - own) // size
    packed = place(incoming, first, past - first, filled.reshape(1))
    packed = packed.reshape(entries // 2, 2, kvl, LANE).transpose(0, 2, 1, 3).reshape(1, slots, kvl, 2 * LANE)

    parts = gather_xor(partial, size)
    terms = project(size, halves, where, ends.reshape(1, -1), starts.reshape(1, -1), w_out.T, parts)
    if halves == 2:
        terms = (terms[0], swap(terms[1], "mp", 2, 1))
    else:
        terms = (lax.psum(terms[0], "mp"),)
    gain_wide = jnp.broadcast_to(norm_gain[:, None], (norm_gain.shape[0], requests))
    hidden, message = stream(halves, where, residual.T, gain_wide, terms)

    messages = gather_xor(message, size)
    if halves == 2:
        messages = messages + [swap(m, "mp", 2, 1) for m in messages]
    outs = swiglu(size, halves, where, w_gate, w_up, w_down, messages)
    n_in = len(outs) // halves
    if halves == 2:
        sums = [(mine + swap(theirs, "mp", 2, 1).astype(F32)).astype(BF) for mine, theirs in zip(outs[:n_in], outs[n_in:])]
    else:
        sums = [mine.astype(BF) for mine in outs]
    outer, inner = strides(size)
    near = sums[0].astype(F32)
    for k in inner[1:]:
        near = near + swap(sums[k], "seq", size, k).astype(F32)
    sent = near.astype(BF)
    down = near[0]
    for j, d in list(enumerate(outer))[1:]:
        down = down + swap(sent[j], "seq", size, d).astype(F32)
    if halves == 2:
        final = (hidden + down).astype(BF)
        other = swap(final, "mp", 2, 1)
        final = jnp.concatenate([jnp.where(half == 0, final, other), jnp.where(half == 0, other, final)], axis=0)
    else:
        down = lax.psum(down.astype(BF), "mp").astype(F32)
        final = (hidden + down).astype(BF)
    return (summaries, packed, final.T)


def solution(mesh):
    placed = (
        P("seq", "mp", None),
        P("seq"),
        P("seq"),
        P(),
        P(),
        P(),
        P(None, "mp", None),
        P(None, "seq"),
        P("mp", "seq"),
        P("seq"),
        P(None, ("seq", "mp")),
        P(None, ("seq", "mp")),
        P(("seq", "mp"), None),
    )
    return jax.shard_map(
        shards,
        mesh=mesh,
        in_specs=placed,
        out_specs=(P("seq", "mp", None), P("seq", None, "mp", None), P(None, "seq")),
        check_vma=False,
    )
```

time: 1100 us -> 239 us (0.22); the launches traced: 1080 us -> 238 us
  local copies, waits for them, and re-layouts: 444 us -> 12.6 us
  waiting for transfers between devices: 343 us -> 83.2 us
  blocking collectives: 141 us -> 0 us
  Pallas kernels: 0 us -> 86.4 us
  other arithmetic: 70 us -> 13.4 us
  matrix products: 40.8 us -> 0 us
  starting transfers between devices: 13.2 us -> 40.6 us
  between operations: 14.9 us -> 2.2 us
  loops' own time: 11.5 us -> 0 us
    scatter x2 -> x0, local copies, waits for them, and re-layouts: 322 us -> none  [the longest x1 247 us: shards(): outgoing = jnp.zeros((seq_devices * slot_rows, kv_local, width_two), jnp....]
    all_gather x2 -> x0, waiting for transfers between devices: 210 us -> none  [the longest x1 157 us: merged_2(): pieces = jax.tree.map(lambda part: lax.all_gather(part, axis), value)]
    pallas_call x0 -> x6, Pallas kernels: none -> 86.4 us  [the longest x1 50.7 us: place(): pl.pallas_call(place_kernel, out_shape=jax.ShapeDtypeStruct((slots, rpe,...]
    ppermute x0 -> x28, waiting for transfers between devices: none -> 83.2 us  [swap(): return lax.ppermute(value, axis, [(i, i ^ distance) for i in range(size)])]
    all_gather x2 -> x0, blocking collectives: 82.6 us -> none  [merged_2(): pieces = jax.tree.map(lambda part: lax.all_gather(part, axis), value)]
    reduce_scatter x1 -> x0, waiting for transfers between devices: 81.3 us -> none  [shards(): lax.psum_scatter(down_terms, 'seq', scatter_dimension=1, tiled=True)]
    add x34 -> x1, other arithmetic: 49.2 us -> 0.01 us  [shards(): block_ids = own * nb + jnp.arange(nb, dtype=jnp.int32)]
    dynamic_slice x46 -> x0, local copies, waits for them, and re-layouts: 42.7 us -> none  [the longest x30 33 us: merged_2(): lax.scan(lambda running, piece: (join(running, piece), None), head, tail)]
  transfers between devices with their start and end apart: 7 -> 30, of which waited for: 6 -> 20; matrix products, arithmetic and copies ran while one was open for 26% -> 4% of each run, Pallas kernels for 0% -> 13%
where the time goes in v1:
time: 239 us; the launch traced here: 238 us
  Pallas kernels  86.4 us (36%)
  waiting for transfers between devices  83.2 us (35%)
  starting transfers between devices  40.6 us (17%)
  other arithmetic  13.4 us (6%)
  local copies, waits for them, and re-layouts  12.6 us (5%)
    ppermute x28, waiting for transfers between devices, swap(): return lax.ppermute(value, axis, [(i, i ^ distance) for i in range(size)])  83.2 us
    pallas_call x1, Pallas kernels, place(): pl.pallas_call(place_kernel, out_shape=jax.ShapeDtypeStruct((slots, rpe,...  50.7 us
    ppermute x28, starting transfers between devices, swap(): return lax.ppermute(value, axis, [(i, i ^ distance) for i in range(size)])  25.3 us
    pallas_call x1, Pallas kernels, swiglu(): pl.pallas_call(functools.partial(swiglu_kernel, size, halves, chunk), out...  15.1 us
    pallas_call x1, Pallas kernels, attend(): pl.pallas_call(functools.partial(attend_kernel, kvl), out_shape=(jax.Shap...  11.9 us
    unnamed x42, local copies, waits for them, and re-layouts  10.6 us
    all_to_all x1, starting transfers between devices, shards(): lax.all_to_all(jnp.broadcast_to(kept, (size,)), 'seq', split_axis=0, conc...  8.31 us
    all_to_all x1, starting transfers between devices, shards(): lax.all_to_all(outgoing, 'seq', split_axis=0, concat_axis=0, tiled=True)  6.91 us
  transfers between devices with their start and end apart: 30, of which 20 were waited for; matrix products, arithmetic and copies ran while one was open for 4% of the time, Pallas kernels for 13%

profile of v1, /device:TPU:0, one launch (start us, length us, event | category | flops | bytes accessed | tf_op | source)
XLA Modules:
  0.0 238.3 jit_solution(15662243371637004576)
XLA Ops:
  0.6 1.3 reduce_sum.76
  2.0 1.2 broadcast_in_dim.72
  3.2 8.3 %all-to-all-start = ((s32[16,1,1]{2,1,0:T(1,128)}), s32[16,1,1]{2,1,0:T(1,128)S(1)}, u32[]{:S(2)}, u32[]{:S(2)}) async-start(s32[16,1,1]{2,1,0:T(1,128)} %broadcast_in_dim.72), calls=%async_computation | async-start | bytes 16384 | tf_op jit(solution)/shard_map/all_to_all | solution.py:456
  13.4 2.2 copy-done
  15.6 1.0 copy-done.3
  18.7 11.9 %attend.1 = (bf16[17,16,128]{2,1,0:T(8,128)(2,1)S(1)}, bf16[16,4,256]{2,1,0:T(4,128)(2,1)}, s32[16,128]{1,0:T(8,128)S(1)}) custom-call(s32[16]{0:T(128)S(1)} %convert_reduce_fusion.breq, s32[16]{0:T(128)S(1)} %convert_reduce_fusion.1.bten, f32[4,16]{1,0:T(4,128)S(1)} %copy-done.8, bf16[16384,128]{1,0:T(8,128)(2,1)S(1)} %bitcast.51, s32[16,128]{1,0:T(8,128)S(1)} %bitcast.55, ...), custom_call_target="tpu_custom_call" | custom-call | flops 335544320 | bytes 5242880 | tf_op jit(solution)/shard_map/attend/pallas_call | solution.py:119
  30.6 1.0 fusion.14
  31.7 1.2 fusion.13
  34.2 2.2 copy-done.1
  36.4 4.7 %compact.1 = bf16[1024,8,128]{2,1,0:T(8,128)(2,1)} custom-call(s32[16,128]{1,0:T(8,128)S(1)} %fusion.7.dst, bf16[2048,8,128]{2,1,0:T(8,128)(2,1)S(1)} %bitcast.52), custom_call_target="tpu_custom_call" | custom-call | bytes 16777216 | tf_op jit(solution)/shard_map/compact/pallas_call | solution.py:161
  41.1 6.9 %all-to-all-start.1 = ((bf16[16,64,8,128]{3,2,1,0:T(8,128)(2,1)}), bf16[16,64,8,128]{3,2,1,0:T(8,128)(2,1)S(1)}, u32[]{:S(2)}, u32[]{:S(2)}) async-start(bf16[16,64,8,128]{3,2,1,0:T(8,128)(2,1)} %bitcast.8), calls=%async_computation.1 | async-start | bytes 4194304 | tf_op jit(solution)/shard_map/all_to_all | solution.py:478
  48.0 3.7 %collective-permute-start.2 = (bf16[17,16,128]{2,1,0:T(8,128)(2,1)S(1)}, bf16[17,16,128]{2,1,0:T(8,128)(2,1)S(1)}, u32[]{:S(2)}, u32[]{:S(2)}) collective-permute-start(bf16[17,16,128]{2,1,0:T(8,128)(2,1)S(1)} %get-tuple-element.20), channel_id=1, source_target_pairs={{0,24},{2,26},{4,28},{6,30},{8,16},{10,18},{12,20},{14,22},{16,8},... | collective-permute-start | bytes 208904 | tf_op jit(solution)/shard_map/ppermute | solution.py:228
  52.4 36.0 %collective-permute-done.2 = bf16[17,16,128]{2,1,0:T(8,128)(2,1)S(1)} collective-permute-done((bf16[17,16,128]{2,1,0:T(8,128)(2,1)S(1)}, bf16[17,16,128]{2,1,0:T(8,128)(2,1)S(1)}, u32[]{:S(2)}, u32[]{:S(2)}) %collective-permute-start.2) | collective-permute-done | bytes 69664 | tf_op jit(solution)/shard_map/ppermute | solution.py:228
  88.4 13.3 %collective-permute-done.1 = bf16[17,16,128]{2,1,0:T(8,128)(2,1)} collective-permute-done((bf16[17,16,128]{2,1,0:T(8,128)(2,1)S(1)}, bf16[17,16,128]{2,1,0:T(8,128)(2,1)}, u32[]{:S(2)}, u32[]{:S(2)}) %collective-permute-start.1) | collective-permute-done | bytes 69664 | tf_op jit(solution)/shard_map/ppermute | solution.py:228
  101.7 1.0 pad_maximum_fusion.refs_0_
  102.6 3.0 %collective-permute-start.5 = (bf16[4,17,16,128]{3,2,1,0:T(8,128)(2,1)S(1)}, bf16[4,17,16,128]{3,2,1,0:T(8,128)(2,1)S(1)}, u32[]{:S(2)}, u32[]{:S(2)}) collective-permute-start(bf16[4,17,16,128]{3,2,1,0:T(8,128)(2,1)S(1)} %pad_maximum_fusion.refs_0_), channel_id=1, source_target_pairs={{0,6},{2,4},{4,2},{6,0},{8,14},{10,12},{12,10},{14,8},{16,22},{18,... | collective-permute-start | bytes 835592 | tf_op jit(solution)/shard_map/ppermute | solution.py:228
  105.7 1.0 collective-permute-start.3
  107.4 5.9 %collective-permute-done.5.refs_3_ = bf16[4,17,16,128]{3,2,1,0:T(8,128)(2,1)S(1)} collective-permute-done((bf16[4,17,16,128]{3,2,1,0:T(8,128)(2,1)S(1)}, bf16[4,17,16,128]{3,2,1,0:T(8,128)(2,1)S(1)}, u32[]{:S(2)}, u32[]{:S(2)}) %collective-permute-start.5) | collective-permute-done | bytes 278560 | tf_op jit(solution)/shard_map/ppermute | solution.py:228
  113.3 3.9 %collective-permute-done.4.refs_2_ = bf16[4,17,16,128]{3,2,1,0:T(8,128)(2,1)S(1)} collective-permute-done((bf16[4,17,16,128]{3,2,1,0:T(8,128)(2,1)S(1)}, bf16[4,17,16,128]{3,2,1,0:T(8,128)(2,1)S(1)}, u32[]{:S(2)}, u32[]{:S(2)}) %collective-permute-start.4) | collective-permute-done | bytes 278560 | tf_op jit(solution)/shard_map/ppermute | solution.py:228
  118.0 2.3 project.1
  120.9 1.3 collective-permute-done.6.refs_1_
  123.0 1.7 stream.1
  125.4 3.7 %collective-permute-start.7 = (bf16[176,128]{1,0:T(8,128)(2,1)}, bf16[176,128]{1,0:T(8,128)(2,1)S(1)}, u32[]{:S(2)}, u32[]{:S(2)}) collective-permute-start(bf16[176,128]{1,0:T(8,128)(2,1)} %get-tuple-element.24), channel_id=1, source_target_pairs={{0,8},{2,10},{4,12},{6,14},{8,0},{10,2},{12,4},{14,6},{16,24},{18,... | collective-permute-start | bytes 135176 | tf_op jit(solution)/shard_map/ppermute | solution.py:228
  129.1 2.2 collective-permute-done.9
  131.8 0.8 pad_maximum_fusion.1.refs_0_
  132.7 1.5 collective-permute-start.12
  134.2 1.0 collective-permute-start.11
  135.2 1.0 collective-permute-start.10
  136.2 4.8 %collective-permute-done.12.refs_3_ = bf16[4,176,128]{2,1,0:T(8,128)(2,1)S(1)} collective-permute-done((bf16[4,176,128]{2,1,0:T(8,128)(2,1)S(1)}, bf16[4,176,128]{2,1,0:T(8,128)(2,1)S(1)}, u32[]{:S(2)}, u32[]{:S(2)}) %collective-permute-start.12) | collective-permute-done | bytes 180256 | tf_op jit(solution)/shard_map/ppermute | solution.py:228
  141.0 1.9 collective-permute-done.11.refs_2_
  143.5 0.9 collective-permute-done.15.refs_6_
  145.7 15.1 %swiglu.1 = (f32[4,160,128]{2,1,0:T(8,128)}, f32[4,160,128]{2,1,0:T(8,128)}, f32[4,160,128]{2,1,0:T(8,128)}, f32[4,160,128]{2,1,0:T(8,128)}, bf16[4,160,128]{2,1...) custom-call(s32[2]{0:T(128)} %copy-done.7, ...), custom_call_target="tpu_custom_call" | custom-call | flops 4026531840 | bytes 31457280 | tf_op jit(solution)/shard_map/swiglu/pallas_call | solution.py:399
  162.5 1.0 add_convert_fusion.2
  163.5 1.1 collective-permute-start.19
  164.6 1.0 add_convert_fusion.1
  165.6 1.1 collective-permute-start.21
  166.7 1.0 add_convert_fusion
  167.7 1.6 collective-permute-start.23
  169.8 5.3 %collective-permute-done.21 = bf16[4,160,128]{2,1,0:T(8,128)(2,1)S(1)} collective-permute-done((bf16[4,160,128]{2,1,0:T(8,128)(2,1)S(1)}, bf16[4,160,128]{2,1,0:T(8,128)(2,1)S(1)}, u32[]{:S(2)}, u32[]{:S(2)}) %collective-permute-start.21) | collective-permute-done | bytes 163872 | tf_op jit(solution)/shard_map/ppermute | solution.py:228
  175.1 1.1 fusion.15
  176.2 1.4 collective-permute-start.24
  177.6 1.3 collective-permute-start.26
  178.9 0.9 collective-permute-start.25
  179.8 0.8 collective-permute-done.24
  180.6 2.8 %collective-permute-done.26 = bf16[160,128]{1,0:T(8,128)(2,1)S(1)} collective-permute-done((bf16[160,128]{1,0:T(8,128)(2,1)S(1)}, bf16[160,128]{1,0:T(8,128)(2,1)S(1)}, u32[]{:S(2)}, u32[]{:S(2)}) %collective-permute-start.26) | collective-permute-done | bytes 40992 | tf_op jit(solution)/shard_map/ppermute | solution.py:228
  183.4 0.9 collective-permute-done.25
  186.3 1.3 copy-done.9
  187.6 50.7 %place.1 = bf16[1024,8,128]{2,1,0:T(8,128)(2,1)} custom-call(s32[16]{0:T(128)} %get-tuple-element.38.start, s32[16]{0:T(128)} %get-tuple-element.37.count, s32[1]{0:T(128)} %bitcast.5.total, bf16[16,64,8,128]{3,2,1,0:T(8,128)(2,1)} %copy-done.9), custom_call_target="tpu_custom_call" | custom-call | bytes 4194304 | tf_op jit(solution)/shard_map/place/pallas_call | solution.py:207
  (84 shorter events, 15.0 us)
Async XLA Ops:
  3.2 27.3 %all-to-all-start = ((s32[16,1,1]{2,1,0:T(1,128)}), s32[16,1,1]{2,1,0:T(1,128)S(1)}, u32[]{:S(2)}, u32[]{:S(2)}) async-start(s32[16,1,1]{2,1,0:T(1,128)} %broadcast_in_dim.72), calls=%async_computation | async-start | bytes 16384 | tf_op jit(solution)/shard_map/all_to_all | solution.py:456
  13.4 2.2 copy-start
  15.6 1.0 copy-start.3
  16.6 0.7 copy-start.5
  17.3 0.7 copy-start.6
  34.2 2.2 copy-start.1
  36.4 81.6 %copy-start.2 = (bf16[2048,320]{0,1:T(8,128)(2,1)S(1)}, bf16[2048,320]{0,1:T(8,128)(2,1)}, u32[]{:S(2)}) copy-start(bf16[2048,320]{0,1:T(8,128)(2,1)} %param.21) | copy-start | bytes 3932164
  41.0 81.2 %copy-start.20 = (f32[320]{0:T(512)S(1)}, f32[320]{0:T(512)}, u32[]{:S(2)}) copy-start(f32[320]{0:T(512)} %param.22) | copy-start | bytes 3844
  41.1 145.2 %all-to-all-start.1 = ((bf16[16,64,8,128]{3,2,1,0:T(8,128)(2,1)}), bf16[16,64,8,128]{3,2,1,0:T(8,128)(2,1)S(1)}, u32[]{:S(2)}, u32[]{:S(2)}) async-start(bf16[16,64,8,128]{3,2,1,0:T(8,128)(2,1)} %bitcast.8), calls=%async_computation.1 | async-start | bytes 4194304 | tf_op jit(solution)/shard_map/all_to_all | solution.py:478
  48.0 40.4 %collective-permute-start.2 = (bf16[17,16,128]{2,1,0:T(8,128)(2,1)S(1)}, bf16[17,16,128]{2,1,0:T(8,128)(2,1)S(1)}, u32[]{:S(2)}, u32[]{:S(2)}) collective-permute-start(bf16[17,16,128]{2,1,0:T(8,128)(2,1)S(1)} %get-tuple-element.20), channel_id=1, source_target_pairs={{0,24},{2,26},{4,28},{6,30},{8,16},{10,18},{12,20},{14,22},{16,8},... | collective-permute-start | bytes 208904 | tf_op jit(solution)/shard_map/ppermute | solution.py:228
  51.7 50.0 %collective-permute-start.1 = (bf16[17,16,128]{2,1,0:T(8,128)(2,1)S(1)}, bf16[17,16,128]{2,1,0:T(8,128)(2,1)}, u32[]{:S(2)}, u32[]{:S(2)}) collective-permute-start(bf16[17,16,128]{2,1,0:T(8,128)(2,1)S(1)} %get-tuple-element.20), channel_id=1, source_target_pairs={{0,16},{2,18},{4,20},{6,22},{8,24},{10,26},{12,28},{14,30},{16,0},... | collective-permute-start | bytes 208904 | tf_op jit(solution)/shard_map/ppermute | solution.py:228
  51.7 50.0 %collective-permute-start = (bf16[17,16,128]{2,1,0:T(8,128)(2,1)S(1)}, bf16[17,16,128]{2,1,0:T(8,128)(2,1)}, u32[]{:S(2)}, u32[]{:S(2)}) collective-permute-start(bf16[17,16,128]{2,1,0:T(8,128)(2,1)S(1)} %get-tuple-element.20), channel_id=1, source_target_pairs={{0,8},{2,10},{4,12},{6,14},{8,0},{10,2},{12,4},{14,6},{16,24},{18,... | collective-permute-start | bytes 208904 | tf_op jit(solution)/shard_map/ppermute | solution.py:228
  102.6 10.6 %collective-permute-start.5 = (bf16[4,17,16,128]{3,2,1,0:T(8,128)(2,1)S(1)}, bf16[4,17,16,128]{3,2,1,0:T(8,128)(2,1)S(1)}, u32[]{:S(2)}, u32[]{:S(2)}) collective-permute-start(bf16[4,17,16,128]{3,2,1,0:T(8,128)(2,1)S(1)} %pad_maximum_fusion.refs_0_), channel_id=1, source_target_pairs={{0,6},{2,4},{4,2},{6,0},{8,14},{10,12},{12,10},{14,8},{16,22},{18,... | collective-permute-start | bytes 835592 | tf_op jit(solution)/shard_map/ppermute | solution.py:228
  105.7 11.5 %collective-permute-start.4 = (bf16[4,17,16,128]{3,2,1,0:T(8,128)(2,1)S(1)}, bf16[4,17,16,128]{3,2,1,0:T(8,128)(2,1)S(1)}, u32[]{:S(2)}, u32[]{:S(2)}) collective-permute-start(bf16[4,17,16,128]{3,2,1,0:T(8,128)(2,1)S(1)} %pad_maximum_fusion.refs_0_), channel_id=1, source_target_pairs={{0,4},{2,6},{4,0},{6,2},{8,12},{10,14},{12,8},{14,10},{16,20},{18,... | collective-permute-start | bytes 835592 | tf_op jit(solution)/shard_map/ppermute | solution.py:228
  105.7 12.3 %collective-permute-start.3 = (bf16[4,17,16,128]{3,2,1,0:T(8,128)(2,1)S(1)}, bf16[4,17,16,128]{3,2,1,0:T(8,128)(2,1)S(1)}, u32[]{:S(2)}, u32[]{:S(2)}) collective-permute-start(bf16[4,17,16,128]{3,2,1,0:T(8,128)(2,1)S(1)} %pad_maximum_fusion.refs_0_), channel_id=1, source_target_pairs={{0,2},{2,0},{4,6},{6,4},{8,10},{10,8},{12,14},{14,12},{16,18},{18,... | collective-permute-start | bytes 835592 | tf_op jit(solution)/shard_map/ppermute | solution.py:228
  106.8 16.2 %copy-start.7 = (s32[2]{0:T(128)}, s32[2]{0:T(128)S(1)}, u32[]{:S(2)}) copy-start(s32[2]{0:T(128)S(1)} %pad_add_fusion.place_ref) | copy-start | bytes 28
  120.9 1.3 collective-permute-start.6
  122.2 0.8 copy-start.19
  124.7 6.6 %collective-permute-start.9 = (bf16[176,128]{1,0:T(8,128)(2,1)}, bf16[176,128]{1,0:T(8,128)(2,1)S(1)}, u32[]{:S(2)}, u32[]{:S(2)}) collective-permute-start(bf16[176,128]{1,0:T(8,128)(2,1)} %get-tuple-element.24), channel_id=1, source_target_pairs={{0,24},{2,26},{4,28},{6,30},{8,16},{10,18},{12,20},{14,22},{16,8},... | collective-permute-start | bytes 135176 | tf_op jit(solution)/shard_map/ppermute | solution.py:228
  124.7 6.7 %collective-permute-start.8 = (bf16[176,128]{1,0:T(8,128)(2,1)}, bf16[176,128]{1,0:T(8,128)(2,1)S(1)}, u32[]{:S(2)}, u32[]{:S(2)}) collective-permute-start(bf16[176,128]{1,0:T(8,128)(2,1)} %get-tuple-element.24), channel_id=1, source_target_pairs={{0,16},{2,18},{4,20},{6,22},{8,24},{10,26},{12,28},{14,30},{16,0},... | collective-permute-start | bytes 135176 | tf_op jit(solution)/shard_map/ppermute | solution.py:228
  125.4 6.4 %collective-permute-start.7 = (bf16[176,128]{1,0:T(8,128)(2,1)}, bf16[176,128]{1,0:T(8,128)(2,1)S(1)}, u32[]{:S(2)}, u32[]{:S(2)}) collective-permute-start(bf16[176,128]{1,0:T(8,128)(2,1)} %get-tuple-element.24), channel_id=1, source_target_pairs={{0,8},{2,10},{4,12},{6,14},{8,0},{10,2},{12,4},{14,6},{16,24},{18,... | collective-permute-start | bytes 135176 | tf_op jit(solution)/shard_map/ppermute | solution.py:228
  132.6 12.0 %copy-start.10 = (bf16[4,176,128]{2,1,0:T(8,128)(2,1)}, bf16[4,176,128]{2,1,0:T(8,128)(2,1)S(1)}, u32[]{:S(2)}) copy-start(bf16[4,176,128]{2,1,0:T(8,128)(2,1)S(1)} %pad_maximum_fusion.1.refs_0_) | copy-start | bytes 540676
  132.7 51.6 %copy-start.18 = (f32[160,128]{1,0:T(8,128)S(1)}, f32[160,128]{1,0:T(8,128)}, u32[]{:S(2)}) copy-start(f32[160,128]{1,0:T(8,128)} %get-tuple-element.23) | copy-start | bytes 245764
  132.7 8.4 %collective-permute-start.12 = (bf16[4,176,128]{2,1,0:T(8,128)(2,1)S(1)}, bf16[4,176,128]{2,1,0:T(8,128)(2,1)S(1)}, u32[]{:S(2)}, u32[]{:S(2)}) collective-permute-start(bf16[4,176,128]{2,1,0:T(8,128)(2,1)S(1)} %pad_maximum_fusion.1.refs_0_), channel_id=1, source_target_pairs={{0,6},{2,4},{4,2},{6,0},{8,14},{10,12},{12,10},{14,8},{16,22},{18,... | collective-permute-start | bytes 540680 | tf_op jit(solution)/shard_map/ppermute | solution.py:228
  134.2 8.7 %collective-permute-start.11 = (bf16[4,176,128]{2,1,0:T(8,128)(2,1)S(1)}, bf16[4,176,128]{2,1,0:T(8,128)(2,1)S(1)}, u32[]{:S(2)}, u32[]{:S(2)}) collective-permute-start(bf16[4,176,128]{2,1,0:T(8,128)(2,1)S(1)} %pad_maximum_fusion.1.refs_0_), channel_id=1, source_target_pairs={{0,4},{2,6},{4,0},{6,2},{8,12},{10,14},{12,8},{14,10},{16,20},{18,... | collective-permute-start | bytes 540680 | tf_op jit(solution)/shard_map/ppermute | solution.py:228
  135.2 7.7 %collective-permute-start.10 = (bf16[4,176,128]{2,1,0:T(8,128)(2,1)S(1)}, bf16[4,176,128]{2,1,0:T(8,128)(2,1)S(1)}, u32[]{:S(2)}, u32[]{:S(2)}) collective-permute-start(bf16[4,176,128]{2,1,0:T(8,128)(2,1)S(1)} %pad_maximum_fusion.1.refs_0_), channel_id=1, source_target_pairs={{0,2},{2,0},{4,6},{6,4},{8,10},{10,8},{12,14},{14,12},{16,18},{18,... | collective-permute-start | bytes 540680 | tf_op jit(solution)/shard_map/ppermute | solution.py:228
  136.2 7.2 %collective-permute-start.13 = (bf16[4,176,128]{2,1,0:T(8,128)(2,1)S(1)}, bf16[4,176,128]{2,1,0:T(8,128)(2,1)S(1)}, u32[]{:S(2)}, u32[]{:S(2)}) collective-permute-start(bf16[4,176,128]{2,1,0:T(8,128)(2,1)S(1)} %pad_maximum_fusion.1.refs_0_), channel_id=1, source_target_pairs={{0,1},{1,0},{2,3},{3,2},{4,5},{5,4},{6,7},{7,6},{8,9},{9,8},{10,11... | collective-permute-start | bytes 540680 | tf_op jit(solution)/shard_map/ppermute | solution.py:228
  141.0 3.6 %copy-start.11 = (bf16[4,176,128]{2,1,0:T(8,128)(2,1)}, bf16[4,176,128]{2,1,0:T(8,128)(2,1)S(1)}, u32[]{:S(2)}) copy-start(bf16[4,176,128]{2,1,0:T(8,128)(2,1)S(1)} %collective-permute-done.12.refs_3_) | copy-start | bytes 540676
  141.0 2.4 %collective-permute-start.16 = (bf16[4,176,128]{2,1,0:T(8,128)(2,1)S(1)}, bf16[4,176,128]{2,1,0:T(8,128)(2,1)S(1)}, u32[]{:S(2)}, u32[]{:S(2)}) collective-permute-start(bf16[4,176,128]{2,1,0:T(8,128)(2,1)S(1)} %collective-permute-done.12.refs_3_), channel_id=1, source_target_pairs={{0,1},{1,0},{2,3},{3,2},{4,5},{5,4},{6,7},{7,6},{8,9},{9,8},{10,11... | collective-permute-start | bytes 540680 | tf_op jit(solution)/shard_map/ppermute | solution.py:228
  142.9 1.7 copy-start.12
  142.9 1.4 collective-permute-start.15
  142.9 1.7 copy-start.13
  143.0 1.7 collective-permute-start.14
  143.5 1.2 copy-start.14
  143.5 1.2 copy-start.15
  144.4 0.7 copy-start.16
  160.8 1.7 collective-permute-start.18
  161.0 8.2 %collective-permute-start.17 = (bf16[4,160,128]{2,1,0:T(8,128)(2,1)}, bf16[4,160,128]{2,1,0:T(8,128)(2,1)S(1)}, u32[]{:S(2)}, u32[]{:S(2)}) collective-permute-start(bf16[4,160,128]{2,1,0:T(8,128)(2,1)} %get-tuple-element.26), channel_id=1, source_target_pairs={{0,1},{1,0},{2,3},{3,2},{4,5},{5,4},{6,7},{7,6},{8,9},{9,8},{10,11... | collective-permute-start | bytes 491528 | tf_op jit(solution)/shard_map/ppermute | solution.py:228
  161.4 3.2 %collective-permute-start.20 = (bf16[4,160,128]{2,1,0:T(8,128)(2,1)}, bf16[4,160,128]{2,1,0:T(8,128)(2,1)S(1)}, u32[]{:S(2)}, u32[]{:S(2)}) collective-permute-start(bf16[4,160,128]{2,1,0:T(8,128)(2,1)} %get-tuple-element.30), channel_id=1, source_target_pairs={{0,1},{1,0},{2,3},{3,2},{4,5},{5,4},{6,7},{7,6},{8,9},{9,8},{10,11... | collective-permute-start | bytes 491528 | tf_op jit(solution)/shard_map/ppermute | solution.py:228
  161.5 5.1 %collective-permute-start.22 = (bf16[4,160,128]{2,1,0:T(8,128)(2,1)}, bf16[4,160,128]{2,1,0:T(8,128)(2,1)S(1)}, u32[]{:S(2)}, u32[]{:S(2)}) collective-permute-start(bf16[4,160,128]{2,1,0:T(8,128)(2,1)} %get-tuple-element.32), channel_id=1, source_target_pairs={{0,1},{1,0},{2,3},{3,2},{4,5},{5,4},{6,7},{7,6},{8,9},{9,8},{10,11... | collective-permute-start | bytes 491528 | tf_op jit(solution)/shard_map/ppermute | solution.py:228
  163.5 6.3 %collective-permute-start.19 = (bf16[4,160,128]{2,1,0:T(8,128)(2,1)S(1)}, bf16[4,160,128]{2,1,0:T(8,128)(2,1)S(1)}, u32[]{:S(2)}, u32[]{:S(2)}) collective-permute-start(bf16[4,160,128]{2,1,0:T(8,128)(2,1)S(1)} %add_convert_fusion.2), channel_id=1, source_target_pairs={{0,2},{2,0},{4,6},{6,4},{8,10},{10,8},{12,14},{14,12},{16,18},{18,... | collective-permute-start | bytes 491528 | tf_op jit(solution)/shard_map/ppermute | solution.py:228
  165.6 9.6 %collective-permute-start.21 = (bf16[4,160,128]{2,1,0:T(8,128)(2,1)S(1)}, bf16[4,160,128]{2,1,0:T(8,128)(2,1)S(1)}, u32[]{:S(2)}, u32[]{:S(2)}) collective-permute-start(bf16[4,160,128]{2,1,0:T(8,128)(2,1)S(1)} %add_convert_fusion.1), channel_id=1, source_target_pairs={{0,4},{2,6},{4,0},{6,2},{8,12},{10,14},{12,8},{14,10},{16,20},{18,... | collective-permute-start | bytes 491528 | tf_op jit(solution)/shard_map/ppermute | solution.py:228
  167.7 7.5 %collective-permute-start.23 = (bf16[4,160,128]{2,1,0:T(8,128)(2,1)S(1)}, bf16[4,160,128]{2,1,0:T(8,128)(2,1)S(1)}, u32[]{:S(2)}, u32[]{:S(2)}) collective-permute-start(bf16[4,160,128]{2,1,0:T(8,128)(2,1)S(1)} %add_convert_fusion), channel_id=1, source_target_pairs={{0,6},{2,4},{4,2},{6,0},{8,14},{10,12},{12,10},{14,8},{16,22},{18,... | collective-permute-start | bytes 491528 | tf_op jit(solution)/shard_map/ppermute | solution.py:228
  176.2 4.4 %collective-permute-start.24 = (bf16[160,128]{1,0:T(8,128)(2,1)S(1)}, bf16[160,128]{1,0:T(8,128)(2,1)S(1)}, u32[]{:S(2)}, u32[]{:S(2)}) collective-permute-start(bf16[160,128]{1,0:T(8,128)(2,1)S(1)} %get-tuple-element.39), channel_id=1, source_target_pairs={{0,8},{2,10},{4,12},{6,14},{8,0},{10,2},{12,4},{14,6},{16,24},{18,... | collective-permute-start | bytes 122888 | tf_op jit(solution)/shard_map/ppermute | solution.py:228
  177.6 5.8 %collective-permute-start.26 = (bf16[160,128]{1,0:T(8,128)(2,1)S(1)}, bf16[160,128]{1,0:T(8,128)(2,1)S(1)}, u32[]{:S(2)}, u32[]{:S(2)}) collective-permute-start(bf16[160,128]{1,0:T(8,128)(2,1)S(1)} %get-tuple-element.40), channel_id=1, source_target_pairs={{0,24},{2,26},{4,28},{6,30},{8,16},{10,18},{12,20},{14,22},{16,8},... | collective-permute-start | bytes 122888 | tf_op jit(solution)/shard_map/ppermute | solution.py:228
  178.9 5.3 %collective-permute-start.25 = (bf16[160,128]{1,0:T(8,128)(2,1)S(1)}, bf16[160,128]{1,0:T(8,128)(2,1)S(1)}, u32[]{:S(2)}, u32[]{:S(2)}) collective-permute-start(bf16[160,128]{1,0:T(8,128)(2,1)S(1)} %get-tuple-element.41), channel_id=1, source_target_pairs={{0,16},{2,18},{4,20},{6,22},{8,24},{10,26},{12,28},{14,30},{16,0},... | collective-permute-start | bytes 122888 | tf_op jit(solution)/shard_map/ppermute | solution.py:228
  184.3 1.3 collective-permute-start.27
  186.3 1.3 copy-start.9
  (3 other events, 2.0 us)

commit v2 on v1

--- a/solution.py
+++ b/solution.py
@@ -30,19 +30,38 @@
     return hi, mid, lo
 
 
-def attend_kernel(kvl, breq, bten, table, kv_any, keep_ref, level_ref, q_ref,
-                  o_ref, sum_ref, rank_ref, kv, o_scr, sum_scr, sem):
+def attend_kernel(kvl, place_ref, req_ref, ten_ref, table, kv_any, keep_ref, level_ref, q_ref,
+                  o_ref, sum_ref, rank_ref, count_ref, kv, s_scr, left, out_scr, o_scr, sum_scr, breq, sem):
     nb = keep_ref.shape[0]
-    heads = q_ref.shape[1]
+    requests, heads = q_ref.shape[0], q_ref.shape[1]
     groups = heads // kvl
     rpe = 2 * kvl
     rows = BLK * rpe
-    levels = table.shape[1]
+    tenants, levels = table.shape
     copies = []
     for b in range(nb):
         c = pltpu.make_async_copy(kv_any.at[pl.ds(b * rows, rows)], kv.at[pl.ds(b * rows, rows)], sem.at[b])
         c.start()
         copies.append(c)
+    first = place_ref[0] * nb
+
+    def owned(r, begin):
+        end = begin + req_ref[r]
+
+        def mark(b, carry):
+            breq[b] = r
+            return carry
+
+        lax.fori_loop(jnp.maximum(begin - first, 0), jnp.minimum(end - first, nb), mark, 0)
+        return end
+
+    lax.fori_loop(0, requests, owned, jnp.int32(0))
+    scale = 1.0 / math.sqrt(LANE)
+    for b in range(nb):
+        copies[b].wait()
+        s_scr[b * heads:(b + 1) * heads, :] = lax.dot_general(
+            q_ref[breq[b]], kv[b * rows:(b + 1) * rows, :], (((1,), (1,)), ((), ())), preferred_element_type=F32
+        )
     keep = keep_ref[...]
     keep_f = keep.astype(F32)
     up = (lax.broadcasted_iota(jnp.int32, (BLK, BLK), 0) <= lax.broadcasted_iota(jnp.int32, (BLK, BLK), 1))
@@ -53,9 +72,14 @@
     for b in range(nb - 1):
         before = before + jnp.where(row_id > b, count[b:b + 1], 0.0)
     rank_ref[...] = jnp.where(keep == 1, (within + before).astype(jnp.int32) - 1, -1)
+    count_ref[...] = (before[nb - 1:] + count[nb - 1:]).astype(jnp.int32)
     weights = []
     for b in range(nb):
-        tenant = bten[b]
+        request = breq[b]
+        end, tenant = ten_ref[0], jnp.int32(0)
+        for t in range(1, tenants):
+            tenant = tenant + (request >= end).astype(jnp.int32)
+            end = end + ten_ref[t]
         level = level_ref[b:b + 1, :]
         w = jnp.zeros((1, BLK), F32)
         for j in range(levels):
@@ -71,31 +95,30 @@
     head_of = lax.broadcasted_iota(jnp.int32, (heads, rows), 0) // groups
     is_key = lane_in == head_of
     is_value = lane_in == head_of + kvl
-    scale = 1.0 / math.sqrt(LANE)
+    tops, totals = [], []
+    for b in range(nb):
+        s = jnp.where(is_key & (wide[b:b + 1] > 0.5), s_scr[b * heads:(b + 1) * heads, :] * scale, -1e30)
+        m = jnp.max(s, axis=1, keepdims=True)
+        p = jnp.exp(s - m)
+        tops.append(m)
+        totals.append(jnp.sum(p, axis=1, keepdims=True))
+        p = pltpu.roll(p, kvl, 1)
+        p_hi = p.astype(BF)
+        w_row = wide[nb + b:nb + b + 1]
+        left[b, :heads] = p_hi
+        left[b, heads:2 * heads] = (p - p_hi.astype(F32)).astype(BF)
+        left[b, 2 * heads:3 * heads] = jnp.where(is_key, w_row, 0.0).astype(BF)
+        left[b, 3 * heads:] = jnp.where(is_value, w_row, 0.0).astype(BF)
+    for b in range(nb):
+        out_scr[b] = jnp.dot(left[b], kv[b * rows:(b + 1) * rows, :], preferred_element_type=F32)
     lse_all = jnp.zeros((heads, LANE), F32)
     lane_id = lax.broadcasted_iota(jnp.int32, (heads, LANE), 1)
     for b in range(nb):
-        copies[b].wait()
-        block = kv[b * rows:(b + 1) * rows, :]
-        q = q_ref[breq[b]]
-        s = lax.dot_general(q, block, (((1,), (1,)), ((), ())), preferred_element_type=F32) * scale
-        valid = is_key & (wide[b:b + 1] > 0.5)
-        s = jnp.where(valid, s, -1e30)
-        m = jnp.max(s, axis=1, keepdims=True)
-        p = jnp.where(valid, jnp.exp(s - m), 0.0)
-        total = jnp.sum(p, axis=1, keepdims=True)
-        p = pltpu.roll(p, kvl, 1)
-        p_hi = p.astype(BF)
-        p_lo = (p - p_hi.astype(F32)).astype(BF)
-        w_row = wide[nb + b:nb + b + 1]
-        w_key = jnp.where(is_key, w_row, 0.0).astype(BF)
-        w_val = jnp.where(is_value, w_row, 0.0).astype(BF)
-        left = jnp.concatenate([p_hi, p_lo, w_key, w_val], axis=0)
-        out = jnp.dot(left, block, preferred_element_type=F32)
-        o = out[:heads] + out[heads:2 * heads]
-        s_key = (out[2 * heads:3 * heads] / mass[b:b + 1]).astype(BF).astype(F32)
-        s_val = (out[3 * heads:] / mass[b:b + 1]).astype(BF).astype(F32)
-        s_score = jnp.sum(q.astype(F32) * s_key, axis=1, keepdims=True) * scale + log_mass[b:b + 1]
+        m, total = tops[b], totals[b]
+        o = out_scr[b, :heads] + out_scr[b, heads:2 * heads]
+        s_key = (out_scr[b, 2 * heads:3 * heads] / mass[b:b + 1]).astype(BF).astype(F32)
+        s_val = (out_scr[b, 3 * heads:] / mass[b:b + 1]).astype(BF).astype(F32)
+        s_score = jnp.sum(q_ref[breq[b]].astype(F32) * s_key, axis=1, keepdims=True) * scale + log_mass[b:b + 1]
         top = jnp.maximum(m, s_score)
         a = jnp.exp(m - top)
         e = jnp.exp(s_score - top)
@@ -113,33 +136,40 @@
     o_ref[heads] = (hi + pltpu.roll(mid, 32, 1) + pltpu.roll(lo, 64, 1)).astype(BF)
 
 
-def attend(kv_rows, keep, level, queries, breq, bten, table, kvl):
+def attend(where, req_blocks, tenant_sizes, table, kv_rows, keep, level, queries, kvl):
     nb = keep.shape[0]
     heads = queries.shape[1]
+    rows = BLK * 2 * kvl
     return pl.pallas_call(
         functools.partial(attend_kernel, kvl),
         out_shape=(
             jax.ShapeDtypeStruct((heads + 1, nb, LANE), BF),
             jax.ShapeDtypeStruct((nb, kvl, 2 * LANE), BF),
             jax.ShapeDtypeStruct((nb, BLK), jnp.int32),
+            jax.ShapeDtypeStruct((1, LANE), jnp.int32),
         ),
-        in_specs=[SMEM, SMEM, SMEM, ANY, VMEM, VMEM, VMEM],
-        out_specs=(VMEM, VMEM, VMEM),
+        in_specs=[SMEM, SMEM, SMEM, SMEM, ANY, VMEM, VMEM, VMEM],
+        out_specs=(VMEM, VMEM, VMEM, VMEM),
         scratch_shapes=[
             pltpu.VMEM(kv_rows.shape, BF),
+            pltpu.VMEM((nb * heads, rows), F32),
+            pltpu.VMEM((nb, 4 * heads, rows), BF),
+            pltpu.VMEM((nb, 4 * heads, LANE), F32),
             pltpu.VMEM((heads, nb, LANE), F32),
             pltpu.VMEM((nb, kvl, 2 * LANE), F32),
+            pltpu.SMEM((nb,), jnp.int32),
             pltpu.SemaphoreType.DMA((nb,)),
         ],
         compiler_params=params(24),
         cost_estimate=pl.CostEstimate(flops=nb * 2 * 80 * 1024 * 128, bytes_accessed=5 * MIB, transcendentals=nb * 16384),
         name="attend",
-    )(breq, bten, table, kv_rows, keep, level, queries)
-
-
-def compact_kernel(dst, kv_any, out_any, kv, out, sem, out_sem):
+    )(where, req_blocks, tenant_sizes, table, kv_rows, keep, level, queries)
+
+
+def compact_kernel(dst, kv_any, *refs):
+    outs, (kv, out, sem, out_sem) = refs[:-4], refs[-4:]
     nb = dst.shape[0]
-    slots = out_any.shape[0]
+    slots = outs[0].shape[0]
     for b in range(nb):
         pltpu.make_async_copy(kv_any.at[pl.ds(b * BLK, BLK)], kv.at[pl.ds(b * BLK, BLK)], sem.at[b]).start()
 
@@ -150,24 +180,26 @@
         return carry
 
     lax.fori_loop(0, nb, one, 0)
-    copy = pltpu.make_async_copy(out.at[pl.ds(0, slots)], out_any, out_sem)
-    copy.start()
-    copy.wait()
-
-
-def compact(kv_entries, dst, slots):
+    copies = [pltpu.make_async_copy(out.at[pl.ds(j * slots, slots)], ref, out_sem.at[j]) for j, ref in enumerate(outs)]
+    for copy in copies:
+        copy.start()
+    for copy in copies:
+        copy.wait()
+
+
+def compact(kv_entries, dst, slots, pieces):
     nb = dst.shape[0]
     rpe = kv_entries.shape[1]
     return pl.pallas_call(
         compact_kernel,
-        out_shape=jax.ShapeDtypeStruct((slots, rpe, LANE), BF),
+        out_shape=(jax.ShapeDtypeStruct((slots // pieces, rpe, LANE), BF),) * pieces,
         in_specs=[SMEM, ANY],
-        out_specs=ANY,
+        out_specs=(ANY,) * pieces,
         scratch_shapes=[
             pltpu.VMEM(kv_entries.shape, BF),
             pltpu.VMEM((slots + 8, rpe, LANE), BF),
             pltpu.SemaphoreType.DMA((nb,)),
-            pltpu.SemaphoreType.DMA,
+            pltpu.SemaphoreType.DMA((pieces,)),
         ],
         compiler_params=params(16),
         cost_estimate=pl.CostEstimate(flops=0, bytes_accessed=16 * MIB, transcendentals=0),
@@ -175,48 +207,62 @@
     )(dst, kv_entries)
 
 
-def place_kernel(start, count, total, in_any, out_any, zeros, sem, zero_sem):
-    sources, chunk = in_any.shape[0], in_any.shape[1]
+def place_kernel(size, place_ref, start, total, *refs):
+    parts, (out_any, got, out, sem, out_sem) = refs[:-5], refs[-5:]
+    near, chunk = parts[0].shape[0], parts[0].shape[1]
     slots = out_any.shape[0]
-    zeros[...] = jnp.zeros(zeros.shape, zeros.dtype)
-
-    def piece(s):
-        n = count[s]
-        return pltpu.make_async_copy(in_any.at[s, pl.ds(0, n)], out_any.at[pl.ds(start[s], n)], sem.at[s])
-
-    def blank(j):
-        first = jnp.maximum(total[0], j * chunk)
-        n = (j + 1) * chunk - first
-        return n, lambda: pltpu.make_async_copy(zeros.at[pl.ds(0, n)], out_any.at[pl.ds(first, n)], zero_sem.at[j])
-
-    for s in range(sources):
-        pl.when(count[s] > 0)(lambda s=s: piece(s).start())
-    for j in range(slots // chunk):
-        n, made = blank(j)
-        pl.when(n > 0)(lambda made=made: made().start())
-    for s in range(sources):
-        pl.when(count[s] > 0)(lambda s=s: piece(s).wait())
-    for j in range(slots // chunk):
-        n, made = blank(j)
-        pl.when(n > 0)(lambda made=made: made().wait())
-
-
-def place(incoming, start, count, total):
-    sources, chunk, rpe, _ = incoming.shape
-    slots = sources * chunk
+    inner = len(parts)
+    copies = []
+    for k, part in enumerate(parts):
+        c = pltpu.make_async_copy(part, got.at[pl.ds(k * near, near)], sem.at[k])
+        c.start()
+        copies.append(c)
+    blank = jnp.zeros(out.shape[1:], out.dtype)
+
+    def clear(i, carry):
+        for j in range(16):
+            out[i * 16 + j] = blank
+        return carry
+
+    lax.fori_loop(slots // 2 // 16, slots // 16, clear, 0)
+    for c in copies:
+        c.wait()
+
+    def source(s, carry):
+        apart = place_ref[0] ^ s
+        at = (apart % inner) * near + apart // inner
+        base = start[at]
+        for i in range(chunk):
+            out[base + i] = got[at, i]
+        return carry
+
+    lax.fori_loop(0, size, source, 0)
+    filled = total[0]
+    for i in range(chunk):
+        out[filled + i] = blank
+    copy = pltpu.make_async_copy(out.at[pl.ds(0, slots)], out_any, out_sem)
+    copy.start()
+    copy.wait()
+
+
+def place(size, where, parts, start, total):
+    near, chunk, rpe, _ = parts[0].shape
+    slots = size * chunk
     return pl.pallas_call(
-        place_kernel,
+        functools.partial(place_kernel, size),
         out_shape=jax.ShapeDtypeStruct((slots, rpe, LANE), BF),
-        in_specs=[SMEM, SMEM, SMEM, ANY],
+        in_specs=[SMEM, SMEM, SMEM] + [ANY] * len(parts),
         out_specs=ANY,
         scratch_shapes=[
-            pltpu.VMEM((chunk, rpe, LANE), BF),
-            pltpu.SemaphoreType.DMA((sources,)),
-            pltpu.SemaphoreType.DMA((slots // chunk,)),
+            pltpu.VMEM((size, chunk, rpe, LANE), BF),
+            pltpu.VMEM((slots + chunk, rpe, LANE), BF),
+            pltpu.SemaphoreType.DMA((len(parts),)),
+            pltpu.SemaphoreType.DMA,
         ],
+        compiler_params=params(12),
         cost_estimate=pl.CostEstimate(flops=0, bytes_accessed=4 * MIB, transcendentals=0),
         name="place",
-    )(start, count, total, incoming)
+    )(where, start, total, *parts)
 
 
 def strides(size):
@@ -451,38 +497,36 @@
     level = drop_level.reshape(nb, BLK)
     by_entry = kv_cache.reshape(entries, kvl, 2, LANE).transpose(0, 2, 1, 3).reshape(entries, 2 * kvl, LANE)
     by_row = by_entry.reshape(entries * 2 * kvl, LANE)
-
-    kept = jnp.sum(keep_list)
-    counts = lax.all_to_all(jnp.broadcast_to(kept, (size,)), "seq", split_axis=0, concat_axis=0, tiled=True)
-    seq_ids = jnp.arange(size, dtype=jnp.int32)
-    offsets = jnp.sum(jnp.where(seq_ids[None, :] < seq_ids[:, None], counts[None, :], 0), axis=1)
-    offset = jnp.sum(jnp.where(seq_ids < own, counts, 0))
+    outer, inner = strides(size)
+    n_outer, n_inner = len(outer), len(inner)
+
+    partial, summaries, rank, kept = attend(
+        where, req_blocks, tenant_sizes, drop_table, by_row, keep, level, queries, kvl
+    )
+    parts = gather_xor(partial, size)
+
+    counts = jnp.concatenate([part[:, 0, 0] for part in gather_xor(kept, size)])
+    sources = relative(size, own, jnp.arange(size, dtype=jnp.int32))
+    offsets = jnp.sum(jnp.where(sources[None, :] < sources[:, None], counts[None, :], 0), axis=1)
+    offset = jnp.sum(jnp.where(sources < own, counts, 0))
+
+    position = offset + rank
+    owner = position % size
+    slot = position // size - (offset + size - 1 - owner) // size
+    dst = jnp.where(rank >= 0, (owner ^ own) * chunk + slot, slots).astype(jnp.int32)
+    outgoing = [piece.reshape(n_inner, chunk, 2 * kvl, LANE) for piece in compact(by_entry, dst, slots, n_outer)]
+    across = [piece if d == 0 else swap(piece, "seq", size, d) for piece, d in zip(outgoing, outer)]
+    incoming = [jnp.stack([piece[k] for piece in across]) for k in inner]
+    incoming = [piece if k == 0 else swap(piece, "seq", size, k) for piece, k in zip(incoming, inner)]
+    first = (offsets + size - 1 - own) // size
+    filled = (jnp.sum(counts) + size - 1 - own) // size
+    packed = place(size, where, incoming, first, filled.reshape(1))
+    packed = packed.reshape(slots, 2, kvl, LANE).transpose(0, 2, 1, 3).reshape(1, slots, kvl, 2 * LANE)
 
     request_ids = jnp.arange(requests, dtype=jnp.int32)
     ends = jnp.sum(jnp.where(request_ids[None, :] <= request_ids[:, None], req_blocks[None, :], 0), axis=1)
     starts = ends - req_blocks
-    block_ids = own * nb + jnp.arange(nb, dtype=jnp.int32)
-    block_req = jnp.sum((block_ids[:, None] >= ends[None, :]).astype(jnp.int32), axis=1)
-    tenants = tenant_sizes.shape[0]
-    tenant_ids = jnp.arange(tenants, dtype=jnp.int32)
-    tenant_ends = jnp.sum(jnp.where(tenant_ids[None, :] <= tenant_ids[:, None], tenant_sizes[None, :], 0), axis=1)
-    block_tenant = jnp.sum((block_req[:, None] >= tenant_ends[None, :]).astype(jnp.int32), axis=1)
-
-    partial, summaries, rank = attend(by_row, keep, level, queries, block_req, block_tenant, drop_table, kvl)
-
-    position = offset + rank
-    owner = position % size
-    slot = position // size - (offset + size - 1 - owner) // size
-    dst = jnp.where(rank >= 0, owner * chunk + slot, slots).astype(jnp.int32)
-    outgoing = compact(by_entry, dst, slots).reshape(size, chunk, 2 * kvl, LANE)
-    incoming = lax.all_to_all(outgoing, "seq", split_axis=0, concat_axis=0, tiled=True)
-    first = (offsets + size - 1 - own) // size
-    past = (offsets + counts + size - 1 - own) // size
-    filled = (jnp.sum(counts) + size - 1 - own) // size
-    packed = place(incoming, first, past - first, filled.reshape(1))
-    packed = packed.reshape(entries // 2, 2, kvl, LANE).transpose(0, 2, 1, 3).reshape(1, slots, kvl, 2 * LANE)
-
-    parts = gather_xor(partial, size)
+
     terms = project(size, halves, where, ends.reshape(1, -1), starts.reshape(1, -1), w_out.T, parts)
     if halves == 2:
         terms = (terms[0], swap(terms[1], "mp", 2, 1))
@@ -500,7 +544,6 @@
         sums = [(mine + swap(theirs, "mp", 2, 1).astype(F32)).astype(BF) for mine, theirs in zip(outs[:n_in], outs[n_in:])]
     else:
         sums = [mine.astype(BF) for mine in outs]
-    outer, inner = strides(size)
     near = sums[0].astype(F32)
     for k in inner[1:]:
         near = near + swap(sums[k], "seq", size, k).astype(F32)

time: 239 us -> 159 us (0.67)
  Pallas kernels: 86.4 us -> 34.1 us
  waiting for transfers between devices: 83.2 us -> 42.8 us
  starting transfers between devices: 40.6 us -> 45.7 us
  local copies, waits for them, and re-layouts: 12.6 us -> 17.3 us
    pallas_call x2, Pallas kernels: 55.4 us -> 6.85 us  [the longest x1 4.22 us: compact(): pl.pallas_call(compact_kernel, out_shape=(jax.ShapeDtypeStruct((slots //...]
    ppermute x28 -> x40, waiting for transfers between devices: 83.2 us -> 42.8 us  [swap(): return lax.ppermute(value, axis, [(i, i ^ distance) for i in range(size)])]
    ppermute x28 -> x40, starting transfers between devices: 25.3 us -> 45.7 us  [swap(): return lax.ppermute(value, axis, [(i, i ^ distance) for i in range(size)])]
    all_to_all x2 -> x0, starting transfers between devices: 15.2 us -> none  [the longest x1 8.31 us: shards(): lax.all_to_all(jnp.broadcast_to(kept, (size,)), 'seq', split_axis=0, conc...]
    pallas_call x1, Pallas kernels: 11.9 us -> 8.21 us  [attend(): pl.pallas_call(functools.partial(attend_kernel, kvl), out_shape=(jax.Shap...]
    slice x0 -> x4, local copies, waits for them, and re-layouts: none -> 2.99 us  [shards(): incoming = [jnp.stack([piece[k] for piece in across]) for k in inner]]
    unnamed x42 -> x50, local copies, waits for them, and re-layouts: 10.6 us -> 12.9 us
  transfers between devices with their start and end apart: 30 -> 40, of which waited for: 20 -> 13; matrix products, arithmetic and copies ran while one was open for 4% -> 11% of each run, Pallas kernels for 13% -> 16%
where the time goes in v2:
time: 159 us; the launch traced here: 158 us
  starting transfers between devices  45.7 us (29%)
  waiting for transfers between devices  42.8 us (27%)
  Pallas kernels  34.1 us (21%)
  local copies, waits for them, and re-layouts  17.3 us (11%)
  other arithmetic  13.9 us (9%)
  between operations  4.21 us (3%)
    ppermute x40, starting transfers between devices, swap(): return lax.ppermute(value, axis, [(i, i ^ distance) for i in range(size)])  45.7 us
    ppermute x40, waiting for transfers between devices, swap(): return lax.ppermute(value, axis, [(i, i ^ distance) for i in range(size)])  42.8 us
    pallas_call x1, Pallas kernels, swiglu(): pl.pallas_call(functools.partial(swiglu_kernel, size, halves, chunk), out...  15 us
    unnamed x50, local copies, waits for them, and re-layouts  12.9 us
    pallas_call x1, Pallas kernels, attend(): pl.pallas_call(functools.partial(attend_kernel, kvl), out_shape=(jax.Shap...  8.21 us
    pallas_call x1, Pallas kernels, compact(): pl.pallas_call(compact_kernel, out_shape=(jax.ShapeDtypeStruct((slots //...  4.22 us
  transfers between devices with their start and end apart: 40, of which 13 were waited for; matrix products, arithmetic and copies ran while one was open for 11% of the time, Pallas kernels for 16%

profile of v2, /device:TPU:0, one launch (start us, length us, event | category | flops | bytes accessed | tf_op | source)
XLA Modules:
  0.0 158.1 jit_solution(11060059935087397994)
XLA Ops:
  0.7 2.2 %copy-done = bf16[2048,4,256]{2,1,0:T(4,128)(2,1)S(1)} copy-done((bf16[2048,4,256]{2,1,0:T(4,128)(2,1)S(1)}, bf16[2048,4,256]{2,1,0:T(4,128)(2,1)}, u32[]{:S(2)}) %copy-start) | copy-done | bytes 4194328
  2.9 1.0 copy-done.3
  7.3 8.2 %attend.1 = (bf16[17,16,128]{2,1,0:T(8,128)(2,1)S(1)}, bf16[16,4,256]{2,1,0:T(4,128)(2,1)}, s32[16,128]{1,0:T(8,128)S(1)}, s32[1,128]{1,0:T(1,128)S(1)}) custom-call(s32[2]{0:T(128)S(1)} %pad_add_fusion.1.place_ref, s32[128]{0:T(128)S(1)} %copy-done.11, s32[4]{0:T(128)S(1)} %copy-done.10, f32[4,16]{1,0:T(4,128)S(1)} %copy-done.9, ...), custom_call_target="tpu_custom_call" | custom-call | flops 335544320 | bytes 5242880 | tf_op jit(solution)/shard_map/attend/pallas_call | solution.py:143
  15.6 5.1 %collective-permute-start.2 = (s32[1,128]{1,0:T(1,128)S(1)}, s32[1,128]{1,0:T(1,128)S(1)}, u32[]{:S(2)}, u32[]{:S(2)}) collective-permute-start(s32[1,128]{1,0:T(1,128)S(1)} %get-tuple-element.24), channel_id=1, source_target_pairs={{0,24},{2,26},{4,28},{6,30},{8,16},{10,18},{12,20},{14,22},{16,8},... | collective-permute-start | bytes 1544 | tf_op jit(solution)/shard_map/ppermute | solution.py:274
  21.3 3.7 %collective-permute-start.14 = (bf16[17,16,128]{2,1,0:T(8,128)(2,1)S(1)}, bf16[17,16,128]{2,1,0:T(8,128)(2,1)S(1)}, u32[]{:S(2)}, u32[]{:S(2)}) collective-permute-start(bf16[17,16,128]{2,1,0:T(8,128)(2,1)S(1)} %get-tuple-element.30), channel_id=1, source_target_pairs={{0,24},{2,26},{4,28},{6,30},{8,16},{10,18},{12,20},{14,22},{16,8},... | collective-permute-start | bytes 208904 | tf_op jit(solution)/shard_map/ppermute | solution.py:274
  25.9 2.6 %collective-permute-start.5 = (s32[4,1,128]{2,1,0:T(1,128)S(1)}, s32[4,1,128]{2,1,0:T(1,128)S(1)}, u32[]{:S(2)}, u32[]{:S(2)}) collective-permute-start(s32[4,1,128]{2,1,0:T(1,128)S(1)} %pad_add_fusion), channel_id=1, source_target_pairs={{0,6},{2,4},{4,2},{6,0},{8,14},{10,12},{12,10},{14,8},{16,22},{18,... | collective-permute-start | bytes 6152 | tf_op jit(solution)/shard_map/ppermute | solution.py:274
  30.4 1.6 %collective-permute-start.3 = (s32[4,1,128]{2,1,0:T(1,128)S(1)}, s32[4,1,128]{2,1,0:T(1,128)S(1)}, u32[]{:S(2)}, u32[]{:S(2)}) collective-permute-start(s32[4,1,128]{2,1,0:T(1,128)S(1)} %pad_add_fusion), channel_id=1, source_target_pairs={{0,2},{2,0},{4,6},{6,4},{8,10},{10,8},{12,14},{14,12},{16,18},{18,... | collective-permute-start | bytes 6152 | tf_op jit(solution)/shard_map/ppermute | solution.py:274
  34.0 0.8 slice_reduce_fusion.4
  36.2 2.6 %collective-permute-start.17 = (bf16[4,17,16,128]{3,2,1,0:T(8,128)(2,1)S(1)}, bf16[4,17,16,128]{3,2,1,0:T(8,128)(2,1)S(1)}, u32[]{:S(2)}, u32[]{:S(2)}) collective-permute-start(bf16[4,17,16,128]{3,2,1,0:T(8,128)(2,1)S(1)} %pad_maximum_fusion.4.refs_0_), channel_id=1, source_target_pairs={{0,6},{2,4},{4,2},{6,0},{8,14},{10,12},{12,10},{14,8},{16,22},{18,... | collective-permute-start | bytes 835592 | tf_op jit(solution)/shard_map/ppermute | solution.py:274
  40.5 2.2 %copy-done.1 = bf16[2048,4,256]{2,1,0:T(4,128)(2,1)S(1)} copy-done((bf16[2048,4,256]{2,1,0:T(4,128)(2,1)S(1)}, bf16[2048,4,256]{2,1,0:T(4,128)(2,1)}, u32[]{:S(2)}) %copy-start.1) | copy-done | bytes 4194328
  42.7 4.2 %compact.1 = (bf16[256,8,128]{2,1,0:T(8,128)(2,1)S(1)}, bf16[256,8,128]{2,1,0:T(8,128)(2,1)}, bf16[256,8,128]{2,1,0:T(8,128)(2,1)S(1)}, bf16[256,8,128]{2,1,0:T(8,128)(2,1)S(1)}) custom-call(s32[16,128]{1,0:T(8,128)S(1)} %fusion.7.dst, bf16[2048,8,128]{2,1,0:T(8,128)(2,1)S(1)} %bitcast.66), custom_call_target="tpu_custom_call" | custom-call | bytes 16777216 | tf_op jit(solution)/shard_map/compact/pallas_call | solution.py:193
  46.9 0.8 copy-done.12
  47.7 0.8 copy-done.13
  48.5 1.4 collective-permute-start.6
  50.5 2.9 %collective-permute-start.7 = (bf16[4,64,8,128]{3,2,1,0:T(8,128)(2,1)}, bf16[4,64,8,128]{3,2,1,0:T(8,128)(2,1)}, u32[]{:S(2)}, u32[]{:S(2)}) collective-permute-start(bf16[4,64,8,128]{3,2,1,0:T(8,128)(2,1)} %bitcast.74), channel_id=1, source_target_pairs={{0,16},{2,18},{4,20},{6,22},{8,24},{10,26},{12,28},{14,30},{16,0},... | collective-permute-start | bytes 1572872 | tf_op jit(solution)/shard_map/ppermute | solution.py:274
  53.5 2.3 %project.1 = (f32[160,128]{1,0:T(8,128)S(1)}, f32[160,128]{1,0:T(8,128)S(1)}) custom-call(s32[2]{0:T(128)S(1)} %pad_add_fusion.1.place_ref, s32[1,128]{1,0:T(1,128)S(1)} %bitcast.71, s32[1,128]{1,0:T(1,128)S(1)} %subtract_bitcast_fusion.starts_ref, bf16[320,2048]{1,0:T(8,128)(2,1)S(1)} %bitcast.67, bf16[4,17,16,128]{3,2,1,0:T(8,128)(2,1)S(1)} %pad_maximum_fusion.4.refs_0_, ...), custom_call_target="tpu_custom_call" | custom-call | flops 314572800 | bytes 3145728 | tf_op jit(solution)/shard_map/project/pallas_call | solution.py:323
  58.0 1.7 %stream.1 = (f32[160,128]{1,0:T(8,128)}, bf16[176,128]{1,0:T(8,128)(2,1)}) custom-call(s32[2]{0:T(128)} %copy-done.5, bf16[320,128]{1,0:T(8,128)(2,1)} %bitcast.76, f32[320,128]{1,0:T(8,128)} %broadcast_in_dim.45.gain_ref, f32[160,128]{1,0:T(8,128)} %copy-done.4, f32[160,128]{1,0:T(8,128)} %copy-done.22), custom_call_target="tpu_custom_call" | custom-call | flops 81920 | bytes 524288 | tf_op jit(solution)/shard_map/stream/pallas_call | solution.py:354
  59.8 1.4 collective-permute-start.20
  61.2 2.9 %collective-permute-start.19 = (bf16[176,128]{1,0:T(8,128)(2,1)}, bf16[176,128]{1,0:T(8,128)(2,1)S(1)}, u32[]{:S(2)}, u32[]{:S(2)}) collective-permute-start(bf16[176,128]{1,0:T(8,128)(2,1)} %get-tuple-element.34), channel_id=1, source_target_pairs={{0,8},{2,10},{4,12},{6,14},{8,0},{10,2},{12,4},{14,6},{16,24},{18,... | collective-permute-start | bytes 135176 | tf_op jit(solution)/shard_map/ppermute | solution.py:274
  64.3 10.7 %collective-permute-done.21 = bf16[176,128]{1,0:T(8,128)(2,1)S(1)} collective-permute-done((bf16[176,128]{1,0:T(8,128)(2,1)}, bf16[176,128]{1,0:T(8,128)(2,1)S(1)}, u32[]{:S(2)}, u32[]{:S(2)}) %collective-permute-start.21) | collective-permute-done | bytes 45088 | tf_op jit(solution)/shard_map/ppermute | solution.py:274
  75.0 1.4 collective-permute-start.8
  76.4 13.6 %collective-permute-done.20 = bf16[176,128]{1,0:T(8,128)(2,1)S(1)} collective-permute-done((bf16[176,128]{1,0:T(8,128)(2,1)}, bf16[176,128]{1,0:T(8,128)(2,1)S(1)}, u32[]{:S(2)}, u32[]{:S(2)}) %collective-permute-start.20) | collective-permute-done | bytes 45088 | tf_op jit(solution)/shard_map/ppermute | solution.py:274
  90.0 0.8 pad_maximum_fusion.5.refs_0_
  90.8 2.6 %collective-permute-start.24 = (bf16[4,176,128]{2,1,0:T(8,128)(2,1)S(1)}, bf16[4,176,128]{2,1,0:T(8,128)(2,1)S(1)}, u32[]{:S(2)}, u32[]{:S(2)}) collective-permute-start(bf16[4,176,128]{2,1,0:T(8,128)(2,1)S(1)} %pad_maximum_fusion.5.refs_0_), channel_id=1, source_target_pairs={{0,6},{2,4},{4,2},{6,0},{8,14},{10,12},{12,10},{14,8},{16,22},{18,... | collective-permute-start | bytes 540680 | tf_op jit(solution)/shard_map/ppermute | solution.py:274
  94.4 1.1 fusion.17
  95.6 1.7 %collective-permute-done.24.refs_3_ = bf16[4,176,128]{2,1,0:T(8,128)(2,1)S(1)} collective-permute-done((bf16[4,176,128]{2,1,0:T(8,128)(2,1)S(1)}, bf16[4,176,128]{2,1,0:T(8,128)(2,1)S(1)}, u32[]{:S(2)}, u32[]{:S(2)}) %collective-permute-start.24) | collective-permute-done | bytes 180256 | tf_op jit(solution)/shard_map/ppermute | solution.py:274
  97.3 1.9 %collective-permute-done.23.refs_2_ = bf16[4,176,128]{2,1,0:T(8,128)(2,1)S(1)} collective-permute-done((bf16[4,176,128]{2,1,0:T(8,128)(2,1)S(1)}, bf16[4,176,128]{2,1,0:T(8,128)(2,1)S(1)}, u32[]{:S(2)}, u32[]{:S(2)}) %collective-permute-start.23) | collective-permute-done | bytes 180256 | tf_op jit(solution)/shard_map/ppermute | solution.py:274
  99.7 1.1 fusion.18
  102.3 15.0 %swiglu.1 = (f32[4,160,128]{2,1,0:T(8,128)}, f32[4,160,128]{2,1,0:T(8,128)}, f32[4,160,128]{2,1,0:T(8,128)}, f32[4,160,128]{2,1,0:T(8,128)}, bf16[4,160,128]{2,1...) custom-call(s32[2]{0:T(128)} %copy-done.5, ...), custom_call_target="tpu_custom_call" | custom-call | flops 4026531840 | bytes 31457280 | tf_op jit(solution)/shard_map/swiglu/pallas_call | solution.py:445
  119.2 1.0 add_convert_fusion.2
  120.2 1.6 %collective-permute-start.31 = (bf16[4,160,128]{2,1,0:T(8,128)(2,1)S(1)}, bf16[4,160,128]{2,1,0:T(8,128)(2,1)S(1)}, u32[]{:S(2)}, u32[]{:S(2)}) collective-permute-start(bf16[4,160,128]{2,1,0:T(8,128)(2,1)S(1)} %add_convert_fusion.2), channel_id=1, source_target_pairs={{0,2},{2,0},{4,6},{6,4},{8,10},{10,8},{12,14},{14,12},{16,18},{18,... | collective-permute-start | bytes 491528 | tf_op jit(solution)/shard_map/ppermute | solution.py:274
  121.8 1.0 add_convert_fusion.1
  122.8 1.1 collective-permute-start.33
  123.9 1.0 add_convert_fusion
  124.9 1.0 collective-permute-start.35
  126.0 1.6 %collective-permute-start.9 = (bf16[4,64,8,128]{3,2,1,0:T(8,128)(2,1)S(1)}, bf16[4,64,8,128]{3,2,1,0:T(8,128)(2,1)S(1)}, u32[]{:S(2)}, u32[]{:S(2)}) collective-permute-start(bf16[4,64,8,128]{3,2,1,0:T(8,128)(2,1)S(1)} %pad_maximum_fusion.1), channel_id=1, source_target_pairs={{0,2},{2,0},{4,6},{6,4},{8,10},{10,8},{12,14},{14,12},{16,18},{18,... | collective-permute-start | bytes 1572872 | tf_op jit(solution)/shard_map/ppermute | solution.py:274
  127.7 1.1 collective-permute-start.10
  128.8 4.0 %collective-permute-done.33 = bf16[4,160,128]{2,1,0:T(8,128)(2,1)S(1)} collective-permute-done((bf16[4,160,128]{2,1,0:T(8,128)(2,1)S(1)}, bf16[4,160,128]{2,1,0:T(8,128)(2,1)S(1)}, u32[]{:S(2)}, u32[]{:S(2)}) %collective-permute-start.33) | collective-permute-done | bytes 163872 | tf_op jit(solution)/shard_map/ppermute | solution.py:274
  133.0 1.8 %fusion.16 = (bf16[4,160,128]{2,1,0:T(8,128)(2,1)S(1)}, f32[4,160,128]{2,1,0:T(8,128)}) fusion(bf16[4,160,128]{2,1,0:T(8,128)(2,1)S(1)} %collective-permute-done.35, bf16[4,160,128]{2,1,0:T(8,128)(2,1)S(1)} %collective-permute-done.33, bf16[4,160,128]{2,1,0:T(8,128)(2,1)S(1)} %collective-permute-done.31, f32[4,160,128]{2,1,0:T(8,128)} %get-tuple-element.35, ...), kind=kLoop, calls=%fused_computation.73 | loop fusion | flops 901120 | bytes 1474560 | tf_op jit(solution)/shard_map/convert_element_type | solution.py:550
  135.5 1.3 collective-permute-start.36
  136.9 1.9 %collective-permute-start.11 = (bf16[4,64,8,128]{3,2,1,0:T(8,128)(2,1)S(1)}, bf16[4,64,8,128]{3,2,1,0:T(8,128)(2,1)S(1)}, u32[]{:S(2)}, u32[]{:S(2)}) collective-permute-start(bf16[4,64,8,128]{3,2,1,0:T(8,128)(2,1)S(1)} %pad_maximum_fusion.3), channel_id=1, source_target_pairs={{0,6},{2,4},{4,2},{6,0},{8,14},{10,12},{12,10},{14,8},{16,22},{18,... | collective-permute-start | bytes 1572872 | tf_op jit(solution)/shard_map/ppermute | solution.py:274
  138.8 1.3 collective-permute-start.38
  140.7 0.9 collective-permute-start.37
  144.9 1.0 collective-permute-done.37
  145.9 1.0 fusion.4
  147.0 1.0 pad_maximum_fusion.refs_0_
  148.0 6.8 %collective-permute-done.10.refs_2_ = bf16[4,64,8,128]{3,2,1,0:T(8,128)(2,1)S(1)} collective-permute-done((bf16[4,64,8,128]{3,2,1,0:T(8,128)(2,1)S(1)}, bf16[4,64,8,128]{3,2,1,0:T(8,128)(2,1)S(1)}, u32[]{:S(2)}, u32[]{:S(2)}) %collective-permute-start.10) | collective-permute-done | bytes 524320 | tf_op jit(solution)/shard_map/ppermute | solution.py:274
  154.8 2.6 %place.1 = bf16[1024,8,128]{2,1,0:T(8,128)(2,1)} custom-call(s32[2]{0:T(128)S(1)} %copy-done.6, s32[16]{0:T(128)S(1)} %and_select_fusion.start, s32[1]{0:T(128)} %bitcast.11.total, bf16[4,64,8,128]{3,2,1,0:T(8,128)(2,1)S(1)} %pad_maximum_fusion.refs_0_, bf16[4,64,8,128]{3,2,1,0:T(8,128)(2,1)S(1)} %collective-permute-done.9.refs_1_, ...), custom_call_target="tpu_custom_call" | custom-call | bytes 4194304 | tf_op jit(solution)/shard_map/place/pallas_call | solution.py:251
  (119 shorter events, 22.1 us)
Async XLA Ops:
  0.6 56.5 %copy-start.24 = (f32[320]{0:T(512)S(1)}, f32[320]{0:T(512)}, u32[]{:S(2)}) copy-start(f32[320]{0:T(512)} %param.22) | copy-start | bytes 3844
  0.7 57.2 %copy-start.5 = (s32[2]{0:T(128)}, s32[2]{0:T(128)S(1)}, u32[]{:S(2)}) copy-start(s32[2]{0:T(128)S(1)} %pad_add_fusion.1.place_ref) | copy-start | bytes 28
  0.7 2.2 %copy-start = (bf16[2048,4,256]{2,1,0:T(4,128)(2,1)S(1)}, bf16[2048,4,256]{2,1,0:T(4,128)(2,1)}, u32[]{:S(2)}) copy-start(bf16[2048,4,256]{2,1,0:T(4,128)(2,1)} %param.13) | copy-start | bytes 12582916
  7.3 46.1 %copy-start.2 = (bf16[2048,320]{0,1:T(8,128)(2,1)S(1)}, bf16[2048,320]{0,1:T(8,128)(2,1)}, u32[]{:S(2)}) copy-start(bf16[2048,320]{0,1:T(8,128)(2,1)} %param.21) | copy-start | bytes 3932164
  15.6 9.6 %collective-permute-start.2 = (s32[1,128]{1,0:T(1,128)S(1)}, s32[1,128]{1,0:T(1,128)S(1)}, u32[]{:S(2)}, u32[]{:S(2)}) collective-permute-start(s32[1,128]{1,0:T(1,128)S(1)} %get-tuple-element.24), channel_id=1, source_target_pairs={{0,24},{2,26},{4,28},{6,30},{8,16},{10,18},{12,20},{14,22},{16,8},... | collective-permute-start | bytes 1544 | tf_op jit(solution)/shard_map/ppermute | solution.py:274
  20.7 5.2 %collective-permute-start.1 = (s32[1,128]{1,0:T(1,128)S(1)}, s32[1,128]{1,0:T(1,128)S(1)}, u32[]{:S(2)}, u32[]{:S(2)}) collective-permute-start(s32[1,128]{1,0:T(1,128)S(1)} %get-tuple-element.24), channel_id=1, source_target_pairs={{0,16},{2,18},{4,20},{6,22},{8,24},{10,26},{12,28},{14,30},{16,0},... | collective-permute-start | bytes 1544 | tf_op jit(solution)/shard_map/ppermute | solution.py:274
  20.7 5.2 %collective-permute-start = (s32[1,128]{1,0:T(1,128)S(1)}, s32[1,128]{1,0:T(1,128)S(1)}, u32[]{:S(2)}, u32[]{:S(2)}) collective-permute-start(s32[1,128]{1,0:T(1,128)S(1)} %get-tuple-element.24), channel_id=1, source_target_pairs={{0,8},{2,10},{4,12},{6,14},{8,0},{10,2},{12,4},{14,6},{16,24},{18,... | collective-permute-start | bytes 1544 | tf_op jit(solution)/shard_map/ppermute | solution.py:274
  21.3 14.9 %collective-permute-start.14 = (bf16[17,16,128]{2,1,0:T(8,128)(2,1)S(1)}, bf16[17,16,128]{2,1,0:T(8,128)(2,1)S(1)}, u32[]{:S(2)}, u32[]{:S(2)}) collective-permute-start(bf16[17,16,128]{2,1,0:T(8,128)(2,1)S(1)} %get-tuple-element.30), channel_id=1, source_target_pairs={{0,24},{2,26},{4,28},{6,30},{8,16},{10,18},{12,20},{14,22},{16,8},... | collective-permute-start | bytes 208904 | tf_op jit(solution)/shard_map/ppermute | solution.py:274
  25.1 11.1 %collective-permute-start.13 = (bf16[17,16,128]{2,1,0:T(8,128)(2,1)S(1)}, bf16[17,16,128]{2,1,0:T(8,128)(2,1)S(1)}, u32[]{:S(2)}, u32[]{:S(2)}) collective-permute-start(bf16[17,16,128]{2,1,0:T(8,128)(2,1)S(1)} %get-tuple-element.30), channel_id=1, source_target_pairs={{0,16},{2,18},{4,20},{6,22},{8,24},{10,26},{12,28},{14,30},{16,0},... | collective-permute-start | bytes 208904 | tf_op jit(solution)/shard_map/ppermute | solution.py:274
  25.2 11.0 %collective-permute-start.12 = (bf16[17,16,128]{2,1,0:T(8,128)(2,1)S(1)}, bf16[17,16,128]{2,1,0:T(8,128)(2,1)S(1)}, u32[]{:S(2)}, u32[]{:S(2)}) collective-permute-start(bf16[17,16,128]{2,1,0:T(8,128)(2,1)S(1)} %get-tuple-element.30), channel_id=1, source_target_pairs={{0,8},{2,10},{4,12},{6,14},{8,0},{10,2},{12,4},{14,6},{16,24},{18,... | collective-permute-start | bytes 208904 | tf_op jit(solution)/shard_map/ppermute | solution.py:274
  25.9 4.5 %collective-permute-start.5 = (s32[4,1,128]{2,1,0:T(1,128)S(1)}, s32[4,1,128]{2,1,0:T(1,128)S(1)}, u32[]{:S(2)}, u32[]{:S(2)}) collective-permute-start(s32[4,1,128]{2,1,0:T(1,128)S(1)} %pad_add_fusion), channel_id=1, source_target_pairs={{0,6},{2,4},{4,2},{6,0},{8,14},{10,12},{12,10},{14,8},{16,22},{18,... | collective-permute-start | bytes 6152 | tf_op jit(solution)/shard_map/ppermute | solution.py:274
  29.2 3.6 %collective-permute-start.4 = (s32[4,1,128]{2,1,0:T(1,128)S(1)}, s32[4,1,128]{2,1,0:T(1,128)S(1)}, u32[]{:S(2)}, u32[]{:S(2)}) collective-permute-start(s32[4,1,128]{2,1,0:T(1,128)S(1)} %pad_add_fusion), channel_id=1, source_target_pairs={{0,4},{2,6},{4,0},{6,2},{8,12},{10,14},{12,8},{14,10},{16,20},{18,... | collective-permute-start | bytes 6152 | tf_op jit(solution)/shard_map/ppermute | solution.py:274
  30.4 3.6 %collective-permute-start.3 = (s32[4,1,128]{2,1,0:T(1,128)S(1)}, s32[4,1,128]{2,1,0:T(1,128)S(1)}, u32[]{:S(2)}, u32[]{:S(2)}) collective-permute-start(s32[4,1,128]{2,1,0:T(1,128)S(1)} %pad_add_fusion), channel_id=1, source_target_pairs={{0,2},{2,0},{4,6},{6,4},{8,10},{10,8},{12,14},{14,12},{16,18},{18,... | collective-permute-start | bytes 6152 | tf_op jit(solution)/shard_map/ppermute | solution.py:274
  36.2 17.2 %collective-permute-start.17 = (bf16[4,17,16,128]{3,2,1,0:T(8,128)(2,1)S(1)}, bf16[4,17,16,128]{3,2,1,0:T(8,128)(2,1)S(1)}, u32[]{:S(2)}, u32[]{:S(2)}) collective-permute-start(bf16[4,17,16,128]{3,2,1,0:T(8,128)(2,1)S(1)} %pad_maximum_fusion.4.refs_0_), channel_id=1, source_target_pairs={{0,6},{2,4},{4,2},{6,0},{8,14},{10,12},{12,10},{14,8},{16,22},{18,... | collective-permute-start | bytes 835592 | tf_op jit(solution)/shard_map/ppermute | solution.py:274
  38.9 14.6 %collective-permute-start.16 = (bf16[4,17,16,128]{3,2,1,0:T(8,128)(2,1)S(1)}, bf16[4,17,16,128]{3,2,1,0:T(8,128)(2,1)S(1)}, u32[]{:S(2)}, u32[]{:S(2)}) collective-permute-start(bf16[4,17,16,128]{3,2,1,0:T(8,128)(2,1)S(1)} %pad_maximum_fusion.4.refs_0_), channel_id=1, source_target_pairs={{0,4},{2,6},{4,0},{6,2},{8,12},{10,14},{12,8},{14,10},{16,20},{18,... | collective-permute-start | bytes 835592 | tf_op jit(solution)/shard_map/ppermute | solution.py:274
  39.4 14.1 %collective-permute-start.15 = (bf16[4,17,16,128]{3,2,1,0:T(8,128)(2,1)S(1)}, bf16[4,17,16,128]{3,2,1,0:T(8,128)(2,1)S(1)}, u32[]{:S(2)}, u32[]{:S(2)}) collective-permute-start(bf16[4,17,16,128]{3,2,1,0:T(8,128)(2,1)S(1)} %pad_maximum_fusion.4.refs_0_), channel_id=1, source_target_pairs={{0,2},{2,0},{4,6},{6,4},{8,10},{10,8},{12,14},{14,12},{16,18},{18,... | collective-permute-start | bytes 835592 | tf_op jit(solution)/shard_map/ppermute | solution.py:274
  40.5 2.2 %copy-start.1 = (bf16[2048,4,256]{2,1,0:T(4,128)(2,1)S(1)}, bf16[2048,4,256]{2,1,0:T(4,128)(2,1)}, u32[]{:S(2)}) copy-start(bf16[2048,4,256]{2,1,0:T(4,128)(2,1)} %param.13) | copy-start | bytes 12582916
  48.5 45.4 %collective-permute-start.6 = (bf16[4,64,8,128]{3,2,1,0:T(8,128)(2,1)}, bf16[4,64,8,128]{3,2,1,0:T(8,128)(2,1)}, u32[]{:S(2)}, u32[]{:S(2)}) collective-permute-start(bf16[4,64,8,128]{3,2,1,0:T(8,128)(2,1)} %bitcast.15), channel_id=1, source_target_pairs={{0,8},{2,10},{4,12},{6,14},{8,0},{10,2},{12,4},{14,6},{16,24},{18,... | collective-permute-start | bytes 1572872 | tf_op jit(solution)/shard_map/ppermute | solution.py:274
  50.5 44.9 %collective-permute-start.7 = (bf16[4,64,8,128]{3,2,1,0:T(8,128)(2,1)}, bf16[4,64,8,128]{3,2,1,0:T(8,128)(2,1)}, u32[]{:S(2)}, u32[]{:S(2)}) collective-permute-start(bf16[4,64,8,128]{3,2,1,0:T(8,128)(2,1)} %bitcast.74), channel_id=1, source_target_pairs={{0,16},{2,18},{4,20},{6,22},{8,24},{10,26},{12,28},{14,30},{16,0},... | collective-permute-start | bytes 1572872 | tf_op jit(solution)/shard_map/ppermute | solution.py:274
  55.8 1.3 collective-permute-start.18
  59.7 15.3 %collective-permute-start.21 = (bf16[176,128]{1,0:T(8,128)(2,1)}, bf16[176,128]{1,0:T(8,128)(2,1)S(1)}, u32[]{:S(2)}, u32[]{:S(2)}) collective-permute-start(bf16[176,128]{1,0:T(8,128)(2,1)} %get-tuple-element.34), channel_id=1, source_target_pairs={{0,24},{2,26},{4,28},{6,30},{8,16},{10,18},{12,20},{14,22},{16,8},... | collective-permute-start | bytes 135176 | tf_op jit(solution)/shard_map/ppermute | solution.py:274
  59.8 30.2 %collective-permute-start.20 = (bf16[176,128]{1,0:T(8,128)(2,1)}, bf16[176,128]{1,0:T(8,128)(2,1)S(1)}, u32[]{:S(2)}, u32[]{:S(2)}) collective-permute-start(bf16[176,128]{1,0:T(8,128)(2,1)} %get-tuple-element.34), channel_id=1, source_target_pairs={{0,16},{2,18},{4,20},{6,22},{8,24},{10,26},{12,28},{14,30},{16,0},... | collective-permute-start | bytes 135176 | tf_op jit(solution)/shard_map/ppermute | solution.py:274
  61.2 28.8 %collective-permute-start.19 = (bf16[176,128]{1,0:T(8,128)(2,1)}, bf16[176,128]{1,0:T(8,128)(2,1)S(1)}, u32[]{:S(2)}, u32[]{:S(2)}) collective-permute-start(bf16[176,128]{1,0:T(8,128)(2,1)} %get-tuple-element.34), channel_id=1, source_target_pairs={{0,8},{2,10},{4,12},{6,14},{8,0},{10,2},{12,4},{14,6},{16,24},{18,... | collective-permute-start | bytes 135176 | tf_op jit(solution)/shard_map/ppermute | solution.py:274
  75.0 42.6 %collective-permute-start.8 = (bf16[4,64,8,128]{3,2,1,0:T(8,128)(2,1)}, bf16[4,64,8,128]{3,2,1,0:T(8,128)(2,1)S(1)}, u32[]{:S(2)}, u32[]{:S(2)}) collective-permute-start(bf16[4,64,8,128]{3,2,1,0:T(8,128)(2,1)} %bitcast.73), channel_id=1, source_target_pairs={{0,24},{2,26},{4,28},{6,30},{8,16},{10,18},{12,20},{14,22},{16,8},... | collective-permute-start | bytes 1572872 | tf_op jit(solution)/shard_map/ppermute | solution.py:274
  90.8 10.1 %copy-start.14 = (bf16[4,176,128]{2,1,0:T(8,128)(2,1)}, bf16[4,176,128]{2,1,0:T(8,128)(2,1)S(1)}, u32[]{:S(2)}) copy-start(bf16[4,176,128]{2,1,0:T(8,128)(2,1)S(1)} %pad_maximum_fusion.5.refs_0_) | copy-start | bytes 540676
  90.8 6.5 %collective-permute-start.24 = (bf16[4,176,128]{2,1,0:T(8,128)(2,1)S(1)}, bf16[4,176,128]{2,1,0:T(8,128)(2,1)S(1)}, u32[]{:S(2)}, u32[]{:S(2)}) collective-permute-start(bf16[4,176,128]{2,1,0:T(8,128)(2,1)S(1)} %pad_maximum_fusion.5.refs_0_), channel_id=1, source_target_pairs={{0,6},{2,4},{4,2},{6,0},{8,14},{10,12},{12,10},{14,8},{16,22},{18,... | collective-permute-start | bytes 540680 | tf_op jit(solution)/shard_map/ppermute | solution.py:274
  93.3 5.8 %collective-permute-start.23 = (bf16[4,176,128]{2,1,0:T(8,128)(2,1)S(1)}, bf16[4,176,128]{2,1,0:T(8,128)(2,1)S(1)}, u32[]{:S(2)}, u32[]{:S(2)}) collective-permute-start(bf16[4,176,128]{2,1,0:T(8,128)(2,1)S(1)} %pad_maximum_fusion.5.refs_0_), channel_id=1, source_target_pairs={{0,4},{2,6},{4,0},{6,2},{8,12},{10,14},{12,8},{14,10},{16,20},{18,... | collective-permute-start | bytes 540680 | tf_op jit(solution)/shard_map/ppermute | solution.py:274
  93.9 5.5 %collective-permute-start.22 = (bf16[4,176,128]{2,1,0:T(8,128)(2,1)S(1)}, bf16[4,176,128]{2,1,0:T(8,128)(2,1)S(1)}, u32[]{:S(2)}, u32[]{:S(2)}) collective-permute-start(bf16[4,176,128]{2,1,0:T(8,128)(2,1)S(1)} %pad_maximum_fusion.5.refs_0_), channel_id=1, source_target_pairs={{0,2},{2,0},{4,6},{6,4},{8,10},{10,8},{12,14},{14,12},{16,18},{18,... | collective-permute-start | bytes 540680 | tf_op jit(solution)/shard_map/ppermute | solution.py:274
  95.5 5.4 %collective-permute-start.25 = (bf16[4,176,128]{2,1,0:T(8,128)(2,1)S(1)}, bf16[4,176,128]{2,1,0:T(8,128)(2,1)S(1)}, u32[]{:S(2)}, u32[]{:S(2)}) collective-permute-start(bf16[4,176,128]{2,1,0:T(8,128)(2,1)S(1)} %pad_maximum_fusion.5.refs_0_), channel_id=1, source_target_pairs={{0,1},{1,0},{2,3},{3,2},{4,5},{5,4},{6,7},{7,6},{8,9},{9,8},{10,11... | collective-permute-start | bytes 540680 | tf_op jit(solution)/shard_map/ppermute | solution.py:274
  97.3 3.6 %copy-start.15 = (bf16[4,176,128]{2,1,0:T(8,128)(2,1)}, bf16[4,176,128]{2,1,0:T(8,128)(2,1)S(1)}, u32[]{:S(2)}) copy-start(bf16[4,176,128]{2,1,0:T(8,128)(2,1)S(1)} %collective-permute-done.24.refs_3_) | copy-start | bytes 540676
  97.3 3.6 %collective-permute-start.28 = (bf16[4,176,128]{2,1,0:T(8,128)(2,1)S(1)}, bf16[4,176,128]{2,1,0:T(8,128)(2,1)S(1)}, u32[]{:S(2)}, u32[]{:S(2)}) collective-permute-start(bf16[4,176,128]{2,1,0:T(8,128)(2,1)S(1)} %collective-permute-done.24.refs_3_), channel_id=1, source_target_pairs={{0,1},{1,0},{2,3},{3,2},{4,5},{5,4},{6,7},{7,6},{8,9},{9,8},{10,11... | collective-permute-start | bytes 540680 | tf_op jit(solution)/shard_map/ppermute | solution.py:274
  99.2 1.7 %collective-permute-start.27 = (bf16[4,176,128]{2,1,0:T(8,128)(2,1)S(1)}, bf16[4,176,128]{2,1,0:T(8,128)(2,1)S(1)}, u32[]{:S(2)}, u32[]{:S(2)}) collective-permute-start(bf16[4,176,128]{2,1,0:T(8,128)(2,1)S(1)} %collective-permute-done.23.refs_2_), channel_id=1, source_target_pairs={{0,1},{1,0},{2,3},{3,2},{4,5},{5,4},{6,7},{7,6},{8,9},{9,8},{10,11... | collective-permute-start | bytes 540680 | tf_op jit(solution)/shard_map/ppermute | solution.py:274
  99.4 1.5 collective-permute-start.26
  100.8 53.9 %copy-start.6 = (s32[2]{0:T(128)S(1)}, s32[2]{0:T(128)}, u32[]{:S(2)}) copy-start(s32[2]{0:T(128)} %copy-done.5) | copy-start | bytes 28
  117.4 1.8 %collective-permute-start.30 = (bf16[4,160,128]{2,1,0:T(8,128)(2,1)}, bf16[4,160,128]{2,1,0:T(8,128)(2,1)S(1)}, u32[]{:S(2)}, u32[]{:S(2)}) collective-permute-start(bf16[4,160,128]{2,1,0:T(8,128)(2,1)} %get-tuple-element.38), channel_id=1, source_target_pairs={{0,1},{1,0},{2,3},{3,2},{4,5},{5,4},{6,7},{7,6},{8,9},{9,8},{10,11... | collective-permute-start | bytes 491528 | tf_op jit(solution)/shard_map/ppermute | solution.py:274
  118.3 9.4 %collective-permute-start.29 = (bf16[4,160,128]{2,1,0:T(8,128)(2,1)}, bf16[4,160,128]{2,1,0:T(8,128)(2,1)S(1)}, u32[]{:S(2)}, u32[]{:S(2)}) collective-permute-start(bf16[4,160,128]{2,1,0:T(8,128)(2,1)} %get-tuple-element.36), channel_id=1, source_target_pairs={{0,1},{1,0},{2,3},{3,2},{4,5},{5,4},{6,7},{7,6},{8,9},{9,8},{10,11... | collective-permute-start | bytes 491528 | tf_op jit(solution)/shard_map/ppermute | solution.py:274
  118.6 3.2 %collective-permute-start.32 = (bf16[4,160,128]{2,1,0:T(8,128)(2,1)}, bf16[4,160,128]{2,1,0:T(8,128)(2,1)S(1)}, u32[]{:S(2)}, u32[]{:S(2)}) collective-permute-start(bf16[4,160,128]{2,1,0:T(8,128)(2,1)} %get-tuple-element.40), channel_id=1, source_target_pairs={{0,1},{1,0},{2,3},{3,2},{4,5},{5,4},{6,7},{7,6},{8,9},{9,8},{10,11... | collective-permute-start | bytes 491528 | tf_op jit(solution)/shard_map/ppermute | solution.py:274
  118.8 5.1 %collective-permute-start.34 = (bf16[4,160,128]{2,1,0:T(8,128)(2,1)}, bf16[4,160,128]{2,1,0:T(8,128)(2,1)S(1)}, u32[]{:S(2)}, u32[]{:S(2)}) collective-permute-start(bf16[4,160,128]{2,1,0:T(8,128)(2,1)} %get-tuple-element.42), channel_id=1, source_target_pairs={{0,1},{1,0},{2,3},{3,2},{4,5},{5,4},{6,7},{7,6},{8,9},{9,8},{10,11... | collective-permute-start | bytes 491528 | tf_op jit(solution)/shard_map/ppermute | solution.py:274
  120.2 8.6 %collective-permute-start.31 = (bf16[4,160,128]{2,1,0:T(8,128)(2,1)S(1)}, bf16[4,160,128]{2,1,0:T(8,128)(2,1)S(1)}, u32[]{:S(2)}, u32[]{:S(2)}) collective-permute-start(bf16[4,160,128]{2,1,0:T(8,128)(2,1)S(1)} %add_convert_fusion.2), channel_id=1, source_target_pairs={{0,2},{2,0},{4,6},{6,4},{8,10},{10,8},{12,14},{14,12},{16,18},{18,... | collective-permute-start | bytes 491528 | tf_op jit(solution)/shard_map/ppermute | solution.py:274
  122.8 9.9 %collective-permute-start.33 = (bf16[4,160,128]{2,1,0:T(8,128)(2,1)S(1)}, bf16[4,160,128]{2,1,0:T(8,128)(2,1)S(1)}, u32[]{:S(2)}, u32[]{:S(2)}) collective-permute-start(bf16[4,160,128]{2,1,0:T(8,128)(2,1)S(1)} %add_convert_fusion.1), channel_id=1, source_target_pairs={{0,4},{2,6},{4,0},{6,2},{8,12},{10,14},{12,8},{14,10},{16,20},{18,... | collective-permute-start | bytes 491528 | tf_op jit(solution)/shard_map/ppermute | solution.py:274
  124.9 8.1 %collective-permute-start.35 = (bf16[4,160,128]{2,1,0:T(8,128)(2,1)S(1)}, bf16[4,160,128]{2,1,0:T(8,128)(2,1)S(1)}, u32[]{:S(2)}, u32[]{:S(2)}) collective-permute-start(bf16[4,160,128]{2,1,0:T(8,128)(2,1)S(1)} %add_convert_fusion), channel_id=1, source_target_pairs={{0,6},{2,4},{4,2},{6,0},{8,14},{10,12},{12,10},{14,8},{16,22},{18,... | collective-permute-start | bytes 491528 | tf_op jit(solution)/shard_map/ppermute | solution.py:274
  126.0 22.0 %collective-permute-start.9 = (bf16[4,64,8,128]{3,2,1,0:T(8,128)(2,1)S(1)}, bf16[4,64,8,128]{3,2,1,0:T(8,128)(2,1)S(1)}, u32[]{:S(2)}, u32[]{:S(2)}) collective-permute-start(bf16[4,64,8,128]{3,2,1,0:T(8,128)(2,1)S(1)} %pad_maximum_fusion.1), channel_id=1, source_target_pairs={{0,2},{2,0},{4,6},{6,4},{8,10},{10,8},{12,14},{14,12},{16,18},{18,... | collective-permute-start | bytes 1572872 | tf_op jit(solution)/shard_map/ppermute | solution.py:274
  127.7 27.1 %collective-permute-start.10 = (bf16[4,64,8,128]{3,2,1,0:T(8,128)(2,1)S(1)}, bf16[4,64,8,128]{3,2,1,0:T(8,128)(2,1)S(1)}, u32[]{:S(2)}, u32[]{:S(2)}) collective-permute-start(bf16[4,64,8,128]{3,2,1,0:T(8,128)(2,1)S(1)} %pad_maximum_fusion.2), channel_id=1, source_target_pairs={{0,4},{2,6},{4,0},{6,2},{8,12},{10,14},{12,8},{14,10},{16,20},{18,... | collective-permute-start | bytes 1572872 | tf_op jit(solution)/shard_map/ppermute | solution.py:274
  135.5 4.6 %collective-permute-start.36 = (bf16[160,128]{1,0:T(8,128)(2,1)S(1)}, bf16[160,128]{1,0:T(8,128)(2,1)S(1)}, u32[]{:S(2)}, u32[]{:S(2)}) collective-permute-start(bf16[160,128]{1,0:T(8,128)(2,1)S(1)} %get-tuple-element.71), channel_id=1, source_target_pairs={{0,8},{2,10},{4,12},{6,14},{8,0},{10,2},{12,4},{14,6},{16,24},{18,... | collective-permute-start | bytes 122888 | tf_op jit(solution)/shard_map/ppermute | solution.py:274
  136.9 17.9 %collective-permute-start.11 = (bf16[4,64,8,128]{3,2,1,0:T(8,128)(2,1)S(1)}, bf16[4,64,8,128]{3,2,1,0:T(8,128)(2,1)S(1)}, u32[]{:S(2)}, u32[]{:S(2)}) collective-permute-start(bf16[4,64,8,128]{3,2,1,0:T(8,128)(2,1)S(1)} %pad_maximum_fusion.3), channel_id=1, source_target_pairs={{0,6},{2,4},{4,2},{6,0},{8,14},{10,12},{12,10},{14,8},{16,22},{18,... | collective-permute-start | bytes 1572872 | tf_op jit(solution)/shard_map/ppermute | solution.py:274
  138.8 6.1 %collective-permute-start.38 = (bf16[160,128]{1,0:T(8,128)(2,1)}, bf16[160,128]{1,0:T(8,128)(2,1)}, u32[]{:S(2)}, u32[]{:S(2)}) collective-permute-start(bf16[160,128]{1,0:T(8,128)(2,1)} %get-tuple-element.72), channel_id=1, source_target_pairs={{0,24},{2,26},{4,28},{6,30},{8,16},{10,18},{12,20},{14,22},{16,8},... | collective-permute-start | bytes 122888 | tf_op jit(solution)/shard_map/ppermute | solution.py:274
  140.7 5.2 %collective-permute-start.37 = (bf16[160,128]{1,0:T(8,128)(2,1)}, bf16[160,128]{1,0:T(8,128)(2,1)}, u32[]{:S(2)}, u32[]{:S(2)}) collective-permute-start(bf16[160,128]{1,0:T(8,128)(2,1)} %get-tuple-element.73), channel_id=1, source_target_pairs={{0,16},{2,18},{4,20},{6,22},{8,24},{10,26},{12,28},{14,30},{16,0},... | collective-permute-start | bytes 122888 | tf_op jit(solution)/shard_map/ppermute | solution.py:274
  146.9 10.5 %collective-permute-start.39 = (bf16[160,128]{1,0:T(8,128)(2,1)S(1)}, bf16[160,128]{1,0:T(8,128)(2,1)S(1)}, u32[]{:S(2)}, u32[]{:S(2)}) collective-permute-start(bf16[160,128]{1,0:T(8,128)(2,1)S(1)} %fusion.4), channel_id=1, source_target_pairs={{0,1},{1,0},{2,3},{3,2},{4,5},{5,4},{6,7},{7,6},{8,9},{9,8},{10,11... | collective-permute-start | bytes 122888 | tf_op jit(solution)/shard_map/ppermute | solution.py:274
  (17 other events, 14.2 us)

commit v3 on v2

--- a/solution.py
+++ b/solution.py
@@ -17,6 +17,7 @@
 SMEM = pl.BlockSpec(memory_space=pltpu.SMEM)
 ANY = pl.BlockSpec(memory_space=pl.ANY)
 MIB = 1 << 20
+SMALL = pl.CostEstimate(flops=0, bytes_accessed=1024, transcendentals=0)
 
 
 def params(mib):
@@ -31,7 +32,7 @@
 
 
 def attend_kernel(kvl, place_ref, req_ref, ten_ref, table, kv_any, keep_ref, level_ref, q_ref,
-                  o_ref, sum_ref, rank_ref, count_ref, kv, s_scr, left, out_scr, o_scr, sum_scr, breq, sem):
+                  o_ref, sum_ref, rank_ref, kv, s_scr, left, out_scr, o_scr, sum_scr, breq, sem):
     nb = keep_ref.shape[0]
     requests, heads = q_ref.shape[0], q_ref.shape[1]
     groups = heads // kvl
@@ -72,7 +73,6 @@
     for b in range(nb - 1):
         before = before + jnp.where(row_id > b, count[b:b + 1], 0.0)
     rank_ref[...] = jnp.where(keep == 1, (within + before).astype(jnp.int32) - 1, -1)
-    count_ref[...] = (before[nb - 1:] + count[nb - 1:]).astype(jnp.int32)
     weights = []
     for b in range(nb):
         request = breq[b]
@@ -146,10 +146,9 @@
             jax.ShapeDtypeStruct((heads + 1, nb, LANE), BF),
             jax.ShapeDtypeStruct((nb, kvl, 2 * LANE), BF),
             jax.ShapeDtypeStruct((nb, BLK), jnp.int32),
-            jax.ShapeDtypeStruct((1, LANE), jnp.int32),
         ),
         in_specs=[SMEM, SMEM, SMEM, SMEM, ANY, VMEM, VMEM, VMEM],
-        out_specs=(VMEM, VMEM, VMEM, VMEM),
+        out_specs=(VMEM, VMEM, VMEM),
         scratch_shapes=[
             pltpu.VMEM(kv_rows.shape, BF),
             pltpu.VMEM((nb * heads, rows), F32),
@@ -160,18 +159,41 @@
             pltpu.SMEM((nb,), jnp.int32),
             pltpu.SemaphoreType.DMA((nb,)),
         ],
-        compiler_params=params(24),
+        compiler_params=params(60),
         cost_estimate=pl.CostEstimate(flops=nb * 2 * 80 * 1024 * 128, bytes_accessed=5 * MIB, transcendentals=nb * 16384),
         name="attend",
     )(where, req_blocks, tenant_sizes, table, kv_rows, keep, level, queries)
 
 
-def compact_kernel(dst, kv_any, *refs):
-    outs, (kv, out, sem, out_sem) = refs[:-4], refs[-4:]
-    nb = dst.shape[0]
-    slots = outs[0].shape[0]
+def shift(value, size):
+    return lax.shift_right_logical(value, jnp.int32(size.bit_length() - 1))
+
+
+def compact_kernel(size, early, late, place_ref, rank_ref, kv_any, *refs):
+    count_refs, refs = refs[:len(strides(size)[1])], refs[len(strides(size)[1]):]
+    outs, total_ref, (kv, out, dst_v, dst, sem, out_sem, dst_sem) = refs[:-8], refs[-8], refs[-7:]
+    nb = rank_ref.shape[0]
+    n_outer, n_inner = (len(d) for d in strides(size))
+    own = place_ref[0]
     for b in range(nb):
         pltpu.make_async_copy(kv_any.at[pl.ds(b * BLK, BLK)], kv.at[pl.ds(b * BLK, BLK)], sem.at[b]).start()
+    by_lane = jnp.concatenate([ref[j] for ref in count_refs for j in range(ref.shape[0])], axis=0).astype(F32)
+    counts = jnp.broadcast_to(jnp.sum(by_lane, axis=1, keepdims=True), (size, LANE))
+    total_ref[...] = counts.astype(jnp.int32)
+    source = relative(size, own, lax.broadcasted_iota(jnp.int32, (size, LANE), 0))
+    offset = jnp.sum(jnp.where(source < own, counts, 0.0), axis=0, keepdims=True).astype(jnp.int32)
+    rank = rank_ref[...]
+    position = offset + jnp.maximum(rank, 0)
+    owner = position & (size - 1)
+    slot = shift(position, size) - shift(offset + (size - 1) - owner, size)
+    apart = owner ^ own
+    k, j = apart & (n_inner - 1), shift(apart, n_inner)
+    first = (j * n_inner + k) * early + slot
+    second = size * early + (k * n_outer + j) * late + slot - early
+    dst_v[...] = jnp.where(rank >= 0, jnp.where(slot < early, first, second), size * (early + late))
+    to_scalars = pltpu.make_async_copy(dst_v, dst, dst_sem)
+    to_scalars.start()
+    to_scalars.wait()
 
     def one(b, carry):
         pltpu.make_async_copy(kv_any.at[pl.ds(b * BLK, BLK)], kv.at[pl.ds(b * BLK, BLK)], sem.at[b]).wait()
@@ -180,41 +202,89 @@
         return carry
 
     lax.fori_loop(0, nb, one, 0)
-    copies = [pltpu.make_async_copy(out.at[pl.ds(j * slots, slots)], ref, out_sem.at[j]) for j, ref in enumerate(outs)]
+    copies, at = [], 0
+    for j, ref in enumerate(outs):
+        copies.append(pltpu.make_async_copy(out.at[pl.ds(at, ref.shape[0])], ref, out_sem.at[j]))
+        at += ref.shape[0]
     for copy in copies:
         copy.start()
     for copy in copies:
         copy.wait()
 
 
-def compact(kv_entries, dst, slots, pieces):
-    nb = dst.shape[0]
+def compact(size, early, late, where, rank, counts, kv_entries):
+    nb = rank.shape[0]
     rpe = kv_entries.shape[1]
+    n_outer, n_inner = (len(d) for d in strides(size))
+    lengths = [n_inner * early] * n_outer + [n_outer * late] * n_inner
     return pl.pallas_call(
-        compact_kernel,
-        out_shape=(jax.ShapeDtypeStruct((slots // pieces, rpe, LANE), BF),) * pieces,
-        in_specs=[SMEM, ANY],
-        out_specs=(ANY,) * pieces,
+        functools.partial(compact_kernel, size, early, late),
+        out_shape=tuple(jax.ShapeDtypeStruct((n, rpe, LANE), BF) for n in lengths)
+        + (jax.ShapeDtypeStruct((size, LANE), jnp.int32),),
+        in_specs=[SMEM, VMEM, ANY] + [VMEM] * len(counts),
+        out_specs=(ANY,) * len(lengths) + (VMEM,),
         scratch_shapes=[
             pltpu.VMEM(kv_entries.shape, BF),
-            pltpu.VMEM((slots + 8, rpe, LANE), BF),
+            pltpu.VMEM((sum(lengths) + 8, rpe, LANE), BF),
+            pltpu.VMEM((nb, BLK), jnp.int32),
+            pltpu.SMEM((nb, BLK), jnp.int32),
             pltpu.SemaphoreType.DMA((nb,)),
-            pltpu.SemaphoreType.DMA((pieces,)),
+            pltpu.SemaphoreType.DMA((len(lengths),)),
+            pltpu.SemaphoreType.DMA,
         ],
-        compiler_params=params(16),
-        cost_estimate=pl.CostEstimate(flops=0, bytes_accessed=16 * MIB, transcendentals=0),
+        compiler_params=params(60),
+        cost_estimate=SMALL,
         name="compact",
-    )(dst, kv_entries)
-
-
-def place_kernel(size, place_ref, start, total, *refs):
+    )(where, rank, kv_entries, *counts)
+
+
+def regroup_kernel(n, *refs):
+    ins, outs, held, sem, out_sem = refs[:n], refs[n:-3], refs[-3], refs[-2], refs[-1]
+    m = len(outs)
+    copies = [[pltpu.make_async_copy(ref.at[i], held.at[i, j], sem.at[j, i]) for j, ref in enumerate(ins)] for i in range(m)]
+    for row in copies:
+        for copy in row:
+            copy.start()
+    sends = []
+    for i, row in enumerate(copies):
+        for copy in row:
+            copy.wait()
+        sends.append(pltpu.make_async_copy(held.at[i], outs[i], out_sem.at[i]))
+        sends[-1].start()
+    for copy in sends:
+        copy.wait()
+
+
+def regroup(values):
+    n, m = len(values), values[0].shape[0]
+    return pl.pallas_call(
+        functools.partial(regroup_kernel, n),
+        out_shape=(jax.ShapeDtypeStruct((n, *values[0].shape[1:]), values[0].dtype),) * m,
+        in_specs=[ANY] * n,
+        out_specs=(ANY,) * m,
+        scratch_shapes=[
+            pltpu.VMEM((m, n, *values[0].shape[1:]), values[0].dtype),
+            pltpu.SemaphoreType.DMA((n, m)),
+            pltpu.SemaphoreType.DMA((m,)),
+        ],
+        compiler_params=params(60),
+        cost_estimate=SMALL,
+        name="regroup",
+    )(*values)
+
+
+def place_kernel(size, n_inner, place_ref, count, *refs):
     parts, (out_any, got, out, sem, out_sem) = refs[:-5], refs[-5:]
-    near, chunk = parts[0].shape[0], parts[0].shape[1]
+    early = parts[0].shape[1]
+    chunk = got.shape[2]
     slots = out_any.shape[0]
-    inner = len(parts)
     copies = []
-    for k, part in enumerate(parts):
-        c = pltpu.make_async_copy(part, got.at[pl.ds(k * near, near)], sem.at[k])
+    for i, part in enumerate(parts):
+        if i < n_inner:
+            to = got.at[i, :, pl.ds(0, early)]
+        else:
+            to = got.at[:, i - n_inner, pl.ds(early, chunk - early)]
+        c = pltpu.make_async_copy(part, to, sem.at[i])
         c.start()
         copies.append(c)
     blank = jnp.zeros(out.shape[1:], out.dtype)
@@ -228,16 +298,17 @@
     for c in copies:
         c.wait()
 
-    def source(s, carry):
-        apart = place_ref[0] ^ s
-        at = (apart % inner) * near + apart // inner
-        base = start[at]
+    own = place_ref[0]
+
+    def source(s, before):
+        apart = own ^ s
+        k, j = apart & (n_inner - 1), shift(apart, n_inner)
+        base = shift(before + (size - 1) - own, size)
         for i in range(chunk):
-            out[base + i] = got[at, i]
-        return carry
-
-    lax.fori_loop(0, size, source, 0)
-    filled = total[0]
+            out[base + i] = got[k, j, i]
+        return before + count[k * got.shape[1] + j, 0]
+
+    filled = shift(lax.fori_loop(0, size, source, jnp.int32(0)) + (size - 1) - own, size)
     for i in range(chunk):
         out[filled + i] = blank
     copy = pltpu.make_async_copy(out.at[pl.ds(0, slots)], out_any, out_sem)
@@ -245,24 +316,26 @@
     copy.wait()
 
 
-def place(size, where, parts, start, total):
-    near, chunk, rpe, _ = parts[0].shape
+def place(size, where, early, late, counts):
+    n_outer, n_inner = len(late), len(early)
+    rpe = early[0].shape[2]
+    chunk = early[0].shape[1] + late[0].shape[1]
     slots = size * chunk
     return pl.pallas_call(
-        functools.partial(place_kernel, size),
+        functools.partial(place_kernel, size, n_inner),
         out_shape=jax.ShapeDtypeStruct((slots, rpe, LANE), BF),
-        in_specs=[SMEM, SMEM, SMEM] + [ANY] * len(parts),
+        in_specs=[SMEM, SMEM] + [ANY] * (n_outer + n_inner),
         out_specs=ANY,
         scratch_shapes=[
-            pltpu.VMEM((size, chunk, rpe, LANE), BF),
+            pltpu.VMEM((n_inner, n_outer, chunk, rpe, LANE), BF),
             pltpu.VMEM((slots + chunk, rpe, LANE), BF),
-            pltpu.SemaphoreType.DMA((len(parts),)),
+            pltpu.SemaphoreType.DMA((n_inner + n_outer,)),
             pltpu.SemaphoreType.DMA,
         ],
         compiler_params=params(12),
-        cost_estimate=pl.CostEstimate(flops=0, bytes_accessed=4 * MIB, transcendentals=0),
+        cost_estimate=SMALL,
         name="place",
-    )(where, start, total, *parts)
+    )(where, counts, *early, *late)
 
 
 def strides(size):
@@ -274,10 +347,16 @@
     return lax.ppermute(value, axis, [(i, i ^ distance) for i in range(size)])
 
 
-def gather_xor(value, size):
-    outer, inner = strides(size)
-    near = jnp.stack([value if d == 0 else swap(value, "seq", size, d) for d in outer])
-    return [near if k == 0 else swap(near, "seq", size, k) for k in inner]
+def gather_near(value, size):
+    return jnp.stack([value if d == 0 else swap(value, "seq", size, d) for d in strides(size)[0]])
+
+
+def gather_far(near, size):
+    return [near if k == 0 else swap(near, "seq", size, k) for k in strides(size)[1]]
+
+
+def after(value, *others):
+    return lax.optimization_barrier((value, others))[0]
 
 
 def relative(size, own, position):
@@ -327,7 +406,7 @@
         out_specs=tuple(VMEM for _ in outs),
         scratch_shapes=[pltpu.VMEM((depth, requests), BF), pltpu.VMEM((width, requests), F32)],
         compiler_params=params(24),
-        cost_estimate=pl.CostEstimate(flops=2 * 128 * 2048 * 600, bytes_accessed=3 * MIB, transcendentals=16 * 32768),
+        cost_estimate=SMALL,
         name="project",
     )(where, ends, starts, w_out_t, *parts)
 
@@ -356,7 +435,7 @@
         out_shape=(jax.ShapeDtypeStruct((n, requests), F32), jax.ShapeDtypeStruct((n + STAT, requests), BF)),
         in_specs=[SMEM] + [VMEM] * (2 + len(terms)),
         out_specs=(VMEM, VMEM),
-        cost_estimate=pl.CostEstimate(flops=n * 512, bytes_accessed=MIB // 2, transcendentals=0),
+        cost_estimate=SMALL,
         name="stream",
     )(where, residual_t, gain_wide, *terms)
 
@@ -460,9 +539,7 @@
             pltpu.SemaphoreType.DMA((3, width // chunk)),
         ],
         compiler_params=params(56),
-        cost_estimate=pl.CostEstimate(
-            flops=6 * requests * width * units, bytes_accessed=6 * width * units, transcendentals=requests * units
-        ),
+        cost_estimate=SMALL,
         name="swiglu",
     )(where, w_gate, w_up, w_down, *messages)
 
@@ -500,46 +577,50 @@
     outer, inner = strides(size)
     n_outer, n_inner = len(outer), len(inner)
 
-    partial, summaries, rank, kept = attend(
+    kept = jnp.sum(keep, axis=0, keepdims=True)
+    near_counts = gather_near(kept, size)
+    counts = gather_far(near_counts, size)
+
+    partial, summaries, rank = attend(
         where, req_blocks, tenant_sizes, drop_table, by_row, keep, level, queries, kvl
     )
-    parts = gather_xor(partial, size)
-
-    counts = jnp.concatenate([part[:, 0, 0] for part in gather_xor(kept, size)])
-    sources = relative(size, own, jnp.arange(size, dtype=jnp.int32))
-    offsets = jnp.sum(jnp.where(sources[None, :] < sources[:, None], counts[None, :], 0), axis=1)
-    offset = jnp.sum(jnp.where(sources < own, counts, 0))
-
-    position = offset + rank
-    owner = position % size
-    slot = position // size - (offset + size - 1 - owner) // size
-    dst = jnp.where(rank >= 0, (owner ^ own) * chunk + slot, slots).astype(jnp.int32)
-    outgoing = [piece.reshape(n_inner, chunk, 2 * kvl, LANE) for piece in compact(by_entry, dst, slots, n_outer)]
-    across = [piece if d == 0 else swap(piece, "seq", size, d) for piece, d in zip(outgoing, outer)]
-    incoming = [jnp.stack([piece[k] for piece in across]) for k in inner]
-    incoming = [piece if k == 0 else swap(piece, "seq", size, k) for piece, k in zip(incoming, inner)]
-    first = (offsets + size - 1 - own) // size
-    filled = (jnp.sum(counts) + size - 1 - own) // size
-    packed = place(size, where, incoming, first, filled.reshape(1))
+    gain_wide = jnp.broadcast_to(norm_gain[:, None], (norm_gain.shape[0], requests))
+    near_parts = after(gather_near(after(partial, near_counts), size), counts)
+    parts = gather_far(near_parts, size)
+
+    early = chunk * 7 // 16
+    late = chunk - early
+    *pieces, totals = compact(size, early, late, where, rank, after(counts, near_parts), by_entry)
+    entry = (2 * kvl, LANE)
+
+    def over(values, distances):
+        return [value if d == 0 else swap(value, "seq", size, d) for value, d in zip(values, distances)]
+
+    first_a = over([p.reshape(n_inner, early, *entry) for p in pieces[:n_outer]], outer)
+    first_b = over([p.reshape(n_outer, late, *entry) for p in after(pieces[n_outer:], parts)], inner)
+    second_a, second_b = regroup(first_a), regroup(first_b)
+    early_in, late_in = over(second_a, inner), over(second_b, outer)
+    packed = place(size, where, early_in, late_in, totals)
     packed = packed.reshape(slots, 2, kvl, LANE).transpose(0, 2, 1, 3).reshape(1, slots, kvl, 2 * LANE)
 
     request_ids = jnp.arange(requests, dtype=jnp.int32)
     ends = jnp.sum(jnp.where(request_ids[None, :] <= request_ids[:, None], req_blocks[None, :], 0), axis=1)
     starts = ends - req_blocks
 
-    terms = project(size, halves, where, ends.reshape(1, -1), starts.reshape(1, -1), w_out.T, parts)
+    terms = project(size, halves, where, ends.reshape(1, -1), starts.reshape(1, -1), w_out.T, after(parts, gain_wide))
     if halves == 2:
         terms = (terms[0], swap(terms[1], "mp", 2, 1))
     else:
         terms = (lax.psum(terms[0], "mp"),)
-    gain_wide = jnp.broadcast_to(norm_gain[:, None], (norm_gain.shape[0], requests))
-    hidden, message = stream(halves, where, residual.T, gain_wide, terms)
-
-    messages = gather_xor(message, size)
+    hidden, message = stream(halves, where, residual.T, gain_wide, after(terms, first_a))
+
+    near_message = after(gather_near(message, size), second_a, second_b)
+    messages = gather_far(near_message, size)
     if halves == 2:
         messages = messages + [swap(m, "mp", 2, 1) for m in messages]
     outs = swiglu(size, halves, where, w_gate, w_up, w_down, messages)
     n_in = len(outs) // halves
+    outs = after(outs, early_in, late_in)
     if halves == 2:
         sums = [(mine + swap(theirs, "mp", 2, 1).astype(F32)).astype(BF) for mine, theirs in zip(outs[:n_in], outs[n_in:])]
     else:
@@ -547,7 +628,7 @@
     near = sums[0].astype(F32)
     for k in inner[1:]:
         near = near + swap(sums[k], "seq", size, k).astype(F32)
-    sent = near.astype(BF)
+    sent = after(near.astype(BF), packed)
     down = near[0]
     for j, d in list(enumerate(outer))[1:]:
         down = down + swap(sent[j], "seq", size, d).astype(F32)

time: 159 us -> 141 us (0.89)
  local copies, waits for them, and re-layouts: 17.3 us -> 4.41 us
  waiting for transfers between devices: 42.8 us -> 33.2 us
  Pallas kernels: 34.1 us -> 41.2 us
  starting transfers between devices: 45.7 us -> 51.4 us
  other arithmetic: 13.9 us -> 9.45 us
  between operations: 4.21 us -> 1.09 us
    unnamed x50 -> x54, local copies, waits for them, and re-layouts: 12.9 us -> 2.93 us
    ppermute x40 -> x46, waiting for transfers between devices: 42.8 us -> 33.2 us  [swap(): return lax.ppermute(value, axis, [(i, i ^ distance) for i in range(size)])]
    pallas_call x2 -> x4, Pallas kernels: 6.85 us -> 13.4 us  [the longest x1 6.16 us: compact(): pl.pallas_call(functools.partial(compact_kernel, size, early, late), out_...]
    ppermute x40 -> x46, starting transfers between devices: 45.7 us -> 51.4 us  [swap(): return lax.ppermute(value, axis, [(i, i ^ distance) for i in range(size)])]
    reduce_sum x6 -> x1, other arithmetic: 3.84 us -> 0.82 us  [shards(): kept = jnp.sum(keep, axis=0, keepdims=True)]
    slice x4 -> x0, local copies, waits for them, and re-layouts: 2.99 us -> none  [shards(): incoming = [jnp.stack([piece[k] for piece in across]) for k in inner]]
  transfers between devices with their start and end apart: 40 -> 46, of which waited for: 13 -> 18; matrix products, arithmetic and copies ran while one was open for 11% -> 6% of each run, Pallas kernels for 16% -> 28%
where the time goes in v3:
time: 141 us
  starting transfers between devices  51.4 us (36%)
  Pallas kernels  41.2 us (29%)
  waiting for transfers between devices  33.2 us (24%)
  other arithmetic  9.45 us (7%)
  local copies, waits for them, and re-layouts  4.41 us (3%)
    ppermute x46, starting transfers between devices, swap(): return lax.ppermute(value, axis, [(i, i ^ distance) for i in range(size)])  51.4 us
    ppermute x46, waiting for transfers between devices, swap(): return lax.ppermute(value, axis, [(i, i ^ distance) for i in range(size)])  33.2 us
    pallas_call x1, Pallas kernels, swiglu(): pl.pallas_call(functools.partial(swiglu_kernel, size, halves, chunk), out...  15.1 us
    pallas_call x1, Pallas kernels, attend(): pl.pallas_call(functools.partial(attend_kernel, kvl), out_shape=(jax.Shap...  8.73 us
    pallas_call x1, Pallas kernels, compact(): pl.pallas_call(functools.partial(compact_kernel, size, early, late), out_...  6.16 us
    pallas_call x2, Pallas kernels, regroup(): pl.pallas_call(functools.partial(regroup_kernel, n), out_shape=(jax.Shape...  4.32 us
    convert_element_type x3, other arithmetic, shards(): (mine + swap(theirs, 'mp', 2, 1).astype(F32)).astype(BF)  3.05 us
    unnamed x54, local copies, waits for them, and re-layouts  2.93 us
  transfers between devices with their start and end apart: 46, of which 18 were waited for; matrix products, arithmetic and copies ran while one was open for 6% of the time, Pallas kernels for 28%

profile of v3, /device:TPU:0, one launch (start us, length us, event | category | flops | bytes accessed | tf_op | source)
XLA Modules:
  0.0 140.7 jit_solution(3804316703664201042)
XLA Ops:
  1.5 5.0 %collective-permute-start.2 = (s32[1,128]{1,0:T(1,128)S(1)}, s32[1,128]{1,0:T(1,128)S(1)}, u32[]{:S(2)}, u32[]{:S(2)}) collective-permute-start(s32[1,128]{1,0:T(1,128)S(1)} %bitcast.81), channel_id=1, source_target_pairs={{0,24},{2,26},{4,28},{6,30},{8,16},{10,18},{12,20},{14,22},{16,8},... | collective-permute-start | bytes 1544 | tf_op jit(solution)/shard_map/ppermute | solution.py:347
  7.8 8.7 %attend.1 = (bf16[17,16,128]{2,1,0:T(8,128)(2,1)}, bf16[16,4,256]{2,1,0:T(4,128)(2,1)}, s32[16,128]{1,0:T(8,128)}) custom-call(s32[2]{0:T(128)} %pad_add_fusion.1.place_ref, s32[128]{0:T(128)} %req_ref.1, s32[4]{0:T(128)} %ten_ref.1, f32[4,16]{1,0:T(4,128)} %table.1, bf16[16384,128]{1,0:T(8,128)(2,1)} %bitcast.65, s32[16,128]{1,0:T(8,128)} %bitcast.79, ...), custom_call_target="tpu_custom_call" | custom-call | flops 335544320 | bytes 5242880 | tf_op jit(solution)/shard_map/attend/pallas_call | solution.py:143
  16.6 3.8 %collective-permute-start.8 = (bf16[17,16,128]{2,1,0:T(8,128)(2,1)}, bf16[17,16,128]{2,1,0:T(8,128)(2,1)S(1)}, u32[]{:S(2)}, u32[]{:S(2)}) collective-permute-start(bf16[17,16,128]{2,1,0:T(8,128)(2,1)} %get-tuple-element.64), channel_id=1, source_target_pairs={{0,24},{2,26},{4,28},{6,30},{8,16},{10,18},{12,20},{14,22},{16,8},... | collective-permute-start | bytes 208904 | tf_op jit(solution)/shard_map/ppermute | solution.py:347
  21.1 2.6 %collective-permute-start.5 = (s32[4,1,128]{2,1,0:T(1,128)S(1)}, s32[4,1,128]{2,1,0:T(1,128)S(1)}, u32[]{:S(2)}, u32[]{:S(2)}) collective-permute-start(s32[4,1,128]{2,1,0:T(1,128)S(1)} %pad_add_fusion.refs_0_), channel_id=1, source_target_pairs={{0,6},{2,4},{4,2},{6,0},{8,14},{10,12},{12,10},{14,8},{16,22},{18,... | collective-permute-start | bytes 6152 | tf_op jit(solution)/shard_map/ppermute | solution.py:347
  24.8 1.1 collective-permute-done.7
  27.8 1.9 %collective-permute-start.17 = (bf16[4,17,16,128]{3,2,1,0:T(8,128)(2,1)S(1)}, bf16[4,17,16,128]{3,2,1,0:T(8,128)(2,1)S(1)}, u32[]{:S(2)}, u32[]{:S(2)}) collective-permute-start(bf16[4,17,16,128]{3,2,1,0:T(8,128)(2,1)S(1)} %pad_maximum_fusion.refs_0_), channel_id=1, source_target_pairs={{0,6},{2,4},{4,2},{6,0},{8,14},{10,12},{12,10},{14,8},{16,22},{18,... | collective-permute-start | bytes 835592 | tf_op jit(solution)/shard_map/ppermute | solution.py:347
  30.2 1.1 collective-permute-start.15
  31.3 6.2 %compact.1 = (bf16[112,8,128]{2,1,0:T(8,128)(2,1)}, bf16[112,8,128]{2,1,0:T(8,128)(2,1)}, bf16[112,8,128]{2,1,0:T(8,128)(2,1)}, bf16[112,8,128]{2,1,0:T(8,128)(2...) custom-call(s32[2]{0:T(128)} %pad_add_fusion.1.place_ref, ...), custom_call_target="tpu_custom_call" | custom-call | bytes 1024 | tf_op jit(solution)/shard_map/compact/pallas_call | solution.py:220
  37.4 1.3 collective-permute-start.9
  38.7 2.9 %collective-permute-start.10 = (bf16[4,28,8,128]{3,2,1,0:T(8,128)(2,1)}, bf16[4,28,8,128]{3,2,1,0:T(8,128)(2,1)S(1)}, u32[]{:S(2)}, u32[]{:S(2)}) collective-permute-start(bf16[4,28,8,128]{3,2,1,0:T(8,128)(2,1)} %bitcast.92), channel_id=1, source_target_pairs={{0,16},{2,18},{4,20},{6,22},{8,24},{10,26},{12,28},{14,30},{16,0},... | collective-permute-start | bytes 688136 | tf_op jit(solution)/shard_map/ppermute | solution.py:347
  42.7 0.9 collective-permute-start.18
  43.7 1.5 %collective-permute-start.19 = (bf16[4,36,8,128]{3,2,1,0:T(8,128)(2,1)}, bf16[4,36,8,128]{3,2,1,0:T(8,128)(2,1)S(1)}, u32[]{:S(2)}, u32[]{:S(2)}) collective-permute-start(bf16[4,36,8,128]{3,2,1,0:T(8,128)(2,1)} %bitcast.89), channel_id=1, source_target_pairs={{0,4},{2,6},{4,0},{6,2},{8,12},{10,14},{12,8},{14,10},{16,20},{18,... | collective-permute-start | bytes 884744 | tf_op jit(solution)/shard_map/ppermute | solution.py:347
  45.2 3.3 %collective-permute-done.9.refs_1_ = bf16[4,28,8,128]{3,2,1,0:T(8,128)(2,1)S(1)} collective-permute-done((bf16[4,28,8,128]{3,2,1,0:T(8,128)(2,1)}, bf16[4,28,8,128]{3,2,1,0:T(8,128)(2,1)S(1)}, u32[]{:S(2)}, u32[]{:S(2)}) %collective-permute-start.9) | collective-permute-done | bytes 229408 | tf_op jit(solution)/shard_map/ppermute | solution.py:347
  48.5 2.4 %collective-permute-start.20 = (bf16[4,36,8,128]{3,2,1,0:T(8,128)(2,1)}, bf16[4,36,8,128]{3,2,1,0:T(8,128)(2,1)S(1)}, u32[]{:S(2)}, u32[]{:S(2)}) collective-permute-start(bf16[4,36,8,128]{3,2,1,0:T(8,128)(2,1)} %bitcast.88), channel_id=1, source_target_pairs={{0,6},{2,4},{4,2},{6,0},{8,14},{10,12},{12,10},{14,8},{16,22},{18,... | collective-permute-start | bytes 884744 | tf_op jit(solution)/shard_map/ppermute | solution.py:347
  51.6 1.5 %broadcast_in_dim.25.gain_ref = f32[320,128]{1,0:T(8,128)} broadcast(f32[320]{0:T(512)} %param.22), dimensions={0} | broadcast | bytes 165120 | tf_op jit(solution)/shard_map/broadcast_in_dim | solution.py:587
  53.7 2.3 %project.1 = (f32[160,128]{1,0:T(8,128)S(1)}, f32[160,128]{1,0:T(8,128)S(1)}) custom-call(s32[2]{0:T(128)S(1)} %copy-done.4, s32[1,128]{1,0:T(1,128)S(1)} %bitcast.64, s32[1,128]{1,0:T(1,128)S(1)} %subtract_bitcast_fusion.starts_ref, bf16[320,2048]{1,0:T(8,128)(2,1)S(1)} %bitcast.63, bf16[4,17,16,128]{3,2,1,0:T(8,128)(2,1)S(1)} %pad_maximum_fusion.refs_0_, ...), custom_call_target="tpu_custom_call" | custom-call | bytes 1024 | tf_op jit(solution)/shard_map/project/pallas_call | solution.py:402
  56.7 1.3 collective-permute-done.24.refs_1_
  58.6 1.7 %stream.1 = (f32[160,128]{1,0:T(8,128)}, bf16[176,128]{1,0:T(8,128)(2,1)}) custom-call(s32[2]{0:T(128)} %pad_add_fusion.1.place_ref, bf16[320,128]{1,0:T(8,128)(2,1)} %bitcast.70, f32[320,128]{1,0:T(8,128)} %broadcast_in_dim.25.gain_ref, f32[160,128]{1,0:T(8,128)} %copy-done.3, f32[160,128]{1,0:T(8,128)} %copy-done.22), custom_call_target="tpu_custom_call" | custom-call | bytes 1024 | tf_op jit(solution)/shard_map/stream/pallas_call | solution.py:433
  60.3 2.0 %collective-permute-start.27 = (bf16[176,128]{1,0:T(8,128)(2,1)}, bf16[176,128]{1,0:T(8,128)(2,1)S(1)}, u32[]{:S(2)}, u32[]{:S(2)}) collective-permute-start(bf16[176,128]{1,0:T(8,128)(2,1)} %get-tuple-element.100), channel_id=1, source_target_pairs={{0,24},{2,26},{4,28},{6,30},{8,16},{10,18},{12,20},{14,22},{16,8},... | collective-permute-start | bytes 135176 | tf_op jit(solution)/shard_map/ppermute | solution.py:347
  62.8 3.8 %collective-permute-done.27 = bf16[176,128]{1,0:T(8,128)(2,1)S(1)} collective-permute-done((bf16[176,128]{1,0:T(8,128)(2,1)}, bf16[176,128]{1,0:T(8,128)(2,1)S(1)}, u32[]{:S(2)}, u32[]{:S(2)}) %collective-permute-start.27) | collective-permute-done | bytes 45088 | tf_op jit(solution)/shard_map/ppermute | solution.py:347
  66.6 2.1 %regroup.2 = (bf16[4,28,8,128]{3,2,1,0:T(8,128)(2,1)}, bf16[4,28,8,128]{3,2,1,0:T(8,128)(2,1)}, bf16[4,28,8,128]{3,2,1,0:T(8,128)(2,1)}, bf16[4,28,8,128]{3,2,1,0:T(8,128)(2,1)}) custom-call(bf16[4,28,8,128]{3,2,1,0:T(8,128)(2,1)} %bitcast.69, bf16[4,28,8,128]{3,2,1,0:T(8,128)(2,1)} %copy-done.11, bf16[4,28,8,128]{3,2,1,0:T(8,128)(2,1)} %copy-done.12, ...), custom_call_target="tpu_custom_call" | custom-call | bytes 1024 | tf_op jit(solution)/shard_map/regroup/pallas_call | solution.py:260
  68.7 2.1 %collective-permute-done.25 = bf16[176,128]{1,0:T(8,128)(2,1)S(1)} collective-permute-done((bf16[176,128]{1,0:T(8,128)(2,1)}, bf16[176,128]{1,0:T(8,128)(2,1)S(1)}, u32[]{:S(2)}, u32[]{:S(2)}) %collective-permute-start.25) | collective-permute-done | bytes 45088 | tf_op jit(solution)/shard_map/ppermute | solution.py:347
  72.6 2.2 %regroup.3 = (bf16[4,36,8,128]{3,2,1,0:T(8,128)(2,1)}, bf16[4,36,8,128]{3,2,1,0:T(8,128)(2,1)}, bf16[4,36,8,128]{3,2,1,0:T(8,128)(2,1)}, bf16[4,36,8,128]{3,2,1,0:T(8,128)(2,1)}) custom-call(bf16[4,36,8,128]{3,2,1,0:T(8,128)(2,1)} %bitcast.68, bf16[4,36,8,128]{3,2,1,0:T(8,128)(2,1)} %copy-done.8, bf16[4,36,8,128]{3,2,1,0:T(8,128)(2,1)} %copy-done.9, ...), custom_call_target="tpu_custom_call" | custom-call | bytes 1024 | tf_op jit(solution)/shard_map/regroup/pallas_call | solution.py:260
  74.9 1.3 collective-permute-start.30
  77.1 1.4 collective-permute-start.28
  79.1 4.3 %collective-permute-done.30.refs_3_ = bf16[4,176,128]{2,1,0:T(8,128)(2,1)S(1)} collective-permute-done((bf16[4,176,128]{2,1,0:T(8,128)(2,1)S(1)}, bf16[4,176,128]{2,1,0:T(8,128)(2,1)S(1)}, u32[]{:S(2)}, u32[]{:S(2)}) %collective-permute-start.30) | collective-permute-done | bytes 180256 | tf_op jit(solution)/shard_map/ppermute | solution.py:347
  83.9 1.7 %collective-permute-done.28.refs_1_ = bf16[4,176,128]{2,1,0:T(8,128)(2,1)S(1)} collective-permute-done((bf16[4,176,128]{2,1,0:T(8,128)(2,1)S(1)}, bf16[4,176,128]{2,1,0:T(8,128)(2,1)S(1)}, u32[]{:S(2)}, u32[]{:S(2)}) %collective-permute-start.28) | collective-permute-done | bytes 180256 | tf_op jit(solution)/shard_map/ppermute | solution.py:347
  85.6 2.5 %collective-permute-done.12.refs_1_ = bf16[4,28,8,128]{3,2,1,0:T(8,128)(2,1)S(1)} collective-permute-done((bf16[4,28,8,128]{3,2,1,0:T(8,128)(2,1)}, bf16[4,28,8,128]{3,2,1,0:T(8,128)(2,1)S(1)}, u32[]{:S(2)}, u32[]{:S(2)}) %collective-permute-start.12) | collective-permute-done | bytes 229408 | tf_op jit(solution)/shard_map/ppermute | solution.py:347
  88.6 2.3 %collective-permute-start.22 = (bf16[4,36,8,128]{3,2,1,0:T(8,128)(2,1)}, bf16[4,36,8,128]{3,2,1,0:T(8,128)(2,1)S(1)}, u32[]{:S(2)}, u32[]{:S(2)}) collective-permute-start(bf16[4,36,8,128]{3,2,1,0:T(8,128)(2,1)} %get-tuple-element.89), channel_id=1, source_target_pairs={{0,16},{2,18},{4,20},{6,22},{8,24},{10,26},{12,28},{14,30},{16,0},... | collective-permute-start | bytes 884744 | tf_op jit(solution)/shard_map/ppermute | solution.py:347
  90.9 1.6 %collective-permute-start.23 = (bf16[4,36,8,128]{3,2,1,0:T(8,128)(2,1)}, bf16[4,36,8,128]{3,2,1,0:T(8,128)(2,1)S(1)}, u32[]{:S(2)}, u32[]{:S(2)}) collective-permute-start(bf16[4,36,8,128]{3,2,1,0:T(8,128)(2,1)} %get-tuple-element.90), channel_id=1, source_target_pairs={{0,24},{2,26},{4,28},{6,30},{8,16},{10,18},{12,20},{14,22},{16,8},... | collective-permute-start | bytes 884744 | tf_op jit(solution)/shard_map/ppermute | solution.py:347
  92.5 1.3 collective-permute-start.13
  93.8 1.5 %collective-permute-start.14 = (bf16[4,28,8,128]{3,2,1,0:T(8,128)(2,1)}, bf16[4,28,8,128]{3,2,1,0:T(8,128)(2,1)S(1)}, u32[]{:S(2)}, u32[]{:S(2)}) collective-permute-start(bf16[4,28,8,128]{3,2,1,0:T(8,128)(2,1)} %get-tuple-element.78), channel_id=1, source_target_pairs={{0,6},{2,4},{4,2},{6,0},{8,14},{10,12},{12,10},{14,8},{16,22},{18,... | collective-permute-start | bytes 688136 | tf_op jit(solution)/shard_map/ppermute | solution.py:347
  95.3 15.1 %swiglu.1 = (f32[4,160,128]{2,1,0:T(8,128)}, f32[4,160,128]{2,1,0:T(8,128)}, f32[4,160,128]{2,1,0:T(8,128)}, f32[4,160,128]{2,1,0:T(8,128)}, bf16[4,160,128]{2,1...) custom-call(s32[2]{0:T(128)} %pad_add_fusion.1.place_ref, ...), custom_call_target="tpu_custom_call" | custom-call | bytes 1024 | tf_op jit(solution)/shard_map/swiglu/pallas_call | solution.py:524
  110.4 1.9 %collective-permute-done.22.refs_6_ = bf16[4,36,8,128]{3,2,1,0:T(8,128)(2,1)S(1)} collective-permute-done((bf16[4,36,8,128]{3,2,1,0:T(8,128)(2,1)}, bf16[4,36,8,128]{3,2,1,0:T(8,128)(2,1)S(1)}, u32[]{:S(2)}, u32[]{:S(2)}) %collective-permute-start.22) | collective-permute-done | bytes 294944 | tf_op jit(solution)/shard_map/ppermute | solution.py:347
  113.9 1.0 add_convert_fusion.2
  114.9 1.2 collective-permute-start.37
  116.1 1.0 add_convert_fusion.1
  117.1 1.1 collective-permute-start.39
  118.2 1.0 add_convert_fusion
  119.2 1.4 %collective-permute-start.41 = (bf16[4,160,128]{2,1,0:T(8,128)(2,1)S(1)}, bf16[4,160,128]{2,1,0:T(8,128)(2,1)S(1)}, u32[]{:S(2)}, u32[]{:S(2)}) collective-permute-start(bf16[4,160,128]{2,1,0:T(8,128)(2,1)S(1)} %add_convert_fusion), channel_id=1, source_target_pairs={{0,6},{2,4},{4,2},{6,0},{8,14},{10,12},{12,10},{14,8},{16,22},{18,... | collective-permute-start | bytes 491528 | tf_op jit(solution)/shard_map/ppermute | solution.py:347
  120.6 2.9 %place.1 = bf16[1024,8,128]{2,1,0:T(8,128)(2,1)} custom-call(s32[2]{0:T(128)S(1)} %copy-done.5, s32[16,128]{1,0:T(8,128)S(1)} %copy-done.6, bf16[4,28,8,128]{3,2,1,0:T(8,128)(2,1)S(1)} %copy-done.2, bf16[4,28,8,128]{3,2,1,0:T(8,128)(2,1)S(1)} %collective-permute-done.12.refs_1_, bf16[4,28,8,128]{3,2,1,0:T(8,128)(2,1)S(1)} %collective-permute-done.13.refs_2_, ...), custom_call_target="tpu_custom_call" | custom-call | bytes 1024 | tf_op jit(solution)/shard_map/place/pallas_call | solution.py:324
  123.6 3.1 %collective-permute-done.39 = bf16[4,160,128]{2,1,0:T(8,128)(2,1)S(1)} collective-permute-done((bf16[4,160,128]{2,1,0:T(8,128)(2,1)S(1)}, bf16[4,160,128]{2,1,0:T(8,128)(2,1)S(1)}, u32[]{:S(2)}, u32[]{:S(2)}) %collective-permute-start.39) | collective-permute-done | bytes 163872 | tf_op jit(solution)/shard_map/ppermute | solution.py:347
  126.7 1.1 fusion.5
  127.8 3.9 %collective-permute-start.42 = (bf16[160,128]{1,0:T(8,128)(2,1)S(1)}, bf16[160,128]{1,0:T(8,128)(2,1)S(1)}, u32[]{:S(2)}, u32[]{:S(2)}) collective-permute-start(bf16[160,128]{1,0:T(8,128)(2,1)S(1)} %get-tuple-element.121), channel_id=1, source_target_pairs={{0,8},{2,10},{4,12},{6,14},{8,0},{10,2},{12,4},{14,6},{16,24},{18,... | collective-permute-start | bytes 122888 | tf_op jit(solution)/shard_map/ppermute | solution.py:347
  131.6 2.2 %collective-permute-start.44 = (bf16[160,128]{1,0:T(8,128)(2,1)S(1)}, bf16[160,128]{1,0:T(8,128)(2,1)S(1)}, u32[]{:S(2)}, u32[]{:S(2)}) collective-permute-start(bf16[160,128]{1,0:T(8,128)(2,1)S(1)} %get-tuple-element.122), channel_id=1, source_target_pairs={{0,24},{2,26},{4,28},{6,30},{8,16},{10,18},{12,20},{14,22},{16,8},... | collective-permute-start | bytes 122888 | tf_op jit(solution)/shard_map/ppermute | solution.py:347
  133.9 3.6 %collective-permute-done.44 = bf16[160,128]{1,0:T(8,128)(2,1)S(1)} collective-permute-done((bf16[160,128]{1,0:T(8,128)(2,1)S(1)}, bf16[160,128]{1,0:T(8,128)(2,1)S(1)}, u32[]{:S(2)}, u32[]{:S(2)}) %collective-permute-start.44) | collective-permute-done | bytes 40992 | tf_op jit(solution)/shard_map/ppermute | solution.py:347
  137.4 1.3 collective-permute-done.43
  138.9 1.2 collective-permute-done.45
  (122 shorter events, 17.2 us)
Async XLA Ops:
  0.6 52.4 %copy-start = (bf16[2048,320]{0,1:T(8,128)(2,1)S(1)}, bf16[2048,320]{0,1:T(8,128)(2,1)}, u32[]{:S(2)}) copy-start(bf16[2048,320]{0,1:T(8,128)(2,1)} %param.21) | copy-start | bytes 3932164
  1.5 15.1 %collective-permute-start.2 = (s32[1,128]{1,0:T(1,128)S(1)}, s32[1,128]{1,0:T(1,128)S(1)}, u32[]{:S(2)}, u32[]{:S(2)}) collective-permute-start(s32[1,128]{1,0:T(1,128)S(1)} %bitcast.81), channel_id=1, source_target_pairs={{0,24},{2,26},{4,28},{6,30},{8,16},{10,18},{12,20},{14,22},{16,8},... | collective-permute-start | bytes 1544 | tf_op jit(solution)/shard_map/ppermute | solution.py:347
  6.5 10.0 %collective-permute-start.1 = (s32[1,128]{1,0:T(1,128)S(1)}, s32[1,128]{1,0:T(1,128)S(1)}, u32[]{:S(2)}, u32[]{:S(2)}) collective-permute-start(s32[1,128]{1,0:T(1,128)S(1)} %bitcast.82), channel_id=1, source_target_pairs={{0,16},{2,18},{4,20},{6,22},{8,24},{10,26},{12,28},{14,30},{16,0},... | collective-permute-start | bytes 1544 | tf_op jit(solution)/shard_map/ppermute | solution.py:347
  6.5 10.1 %collective-permute-start = (s32[1,128]{1,0:T(1,128)S(1)}, s32[1,128]{1,0:T(1,128)S(1)}, u32[]{:S(2)}, u32[]{:S(2)}) collective-permute-start(s32[1,128]{1,0:T(1,128)S(1)} %bitcast.83), channel_id=1, source_target_pairs={{0,8},{2,10},{4,12},{6,14},{8,0},{10,2},{12,4},{14,6},{16,24},{18,... | collective-permute-start | bytes 1544 | tf_op jit(solution)/shard_map/ppermute | solution.py:347
  16.6 7.6 %collective-permute-start.8 = (bf16[17,16,128]{2,1,0:T(8,128)(2,1)}, bf16[17,16,128]{2,1,0:T(8,128)(2,1)S(1)}, u32[]{:S(2)}, u32[]{:S(2)}) collective-permute-start(bf16[17,16,128]{2,1,0:T(8,128)(2,1)} %get-tuple-element.64), channel_id=1, source_target_pairs={{0,24},{2,26},{4,28},{6,30},{8,16},{10,18},{12,20},{14,22},{16,8},... | collective-permute-start | bytes 208904 | tf_op jit(solution)/shard_map/ppermute | solution.py:347
  20.4 5.5 %collective-permute-start.7 = (bf16[17,16,128]{2,1,0:T(8,128)(2,1)}, bf16[17,16,128]{2,1,0:T(8,128)(2,1)S(1)}, u32[]{:S(2)}, u32[]{:S(2)}) collective-permute-start(bf16[17,16,128]{2,1,0:T(8,128)(2,1)} %get-tuple-element.64), channel_id=1, source_target_pairs={{0,16},{2,18},{4,20},{6,22},{8,24},{10,26},{12,28},{14,30},{16,0},... | collective-permute-start | bytes 208904 | tf_op jit(solution)/shard_map/ppermute | solution.py:347
  20.4 5.8 %collective-permute-start.6 = (bf16[17,16,128]{2,1,0:T(8,128)(2,1)}, bf16[17,16,128]{2,1,0:T(8,128)(2,1)S(1)}, u32[]{:S(2)}, u32[]{:S(2)}) collective-permute-start(bf16[17,16,128]{2,1,0:T(8,128)(2,1)} %get-tuple-element.64), channel_id=1, source_target_pairs={{0,8},{2,10},{4,12},{6,14},{8,0},{10,2},{12,4},{14,6},{16,24},{18,... | collective-permute-start | bytes 208904 | tf_op jit(solution)/shard_map/ppermute | solution.py:347
  21.1 6.0 %collective-permute-start.5 = (s32[4,1,128]{2,1,0:T(1,128)S(1)}, s32[4,1,128]{2,1,0:T(1,128)S(1)}, u32[]{:S(2)}, u32[]{:S(2)}) collective-permute-start(s32[4,1,128]{2,1,0:T(1,128)S(1)} %pad_add_fusion.refs_0_), channel_id=1, source_target_pairs={{0,6},{2,4},{4,2},{6,0},{8,14},{10,12},{12,10},{14,8},{16,22},{18,... | collective-permute-start | bytes 6152 | tf_op jit(solution)/shard_map/ppermute | solution.py:347
  23.7 3.6 %collective-permute-start.4 = (s32[4,1,128]{2,1,0:T(1,128)S(1)}, s32[4,1,128]{2,1,0:T(1,128)S(1)}, u32[]{:S(2)}, u32[]{:S(2)}) collective-permute-start(s32[4,1,128]{2,1,0:T(1,128)S(1)} %pad_add_fusion.refs_0_), channel_id=1, source_target_pairs={{0,4},{2,6},{4,0},{6,2},{8,12},{10,14},{12,8},{14,10},{16,20},{18,... | collective-permute-start | bytes 6152 | tf_op jit(solution)/shard_map/ppermute | solution.py:347
  24.2 3.6 %collective-permute-start.3 = (s32[4,1,128]{2,1,0:T(1,128)S(1)}, s32[4,1,128]{2,1,0:T(1,128)S(1)}, u32[]{:S(2)}, u32[]{:S(2)}) collective-permute-start(s32[4,1,128]{2,1,0:T(1,128)S(1)} %pad_add_fusion.refs_0_), channel_id=1, source_target_pairs={{0,2},{2,0},{4,6},{6,4},{8,10},{10,8},{12,14},{14,12},{16,18},{18,... | collective-permute-start | bytes 6152 | tf_op jit(solution)/shard_map/ppermute | solution.py:347
  27.8 14.6 %collective-permute-start.17 = (bf16[4,17,16,128]{3,2,1,0:T(8,128)(2,1)S(1)}, bf16[4,17,16,128]{3,2,1,0:T(8,128)(2,1)S(1)}, u32[]{:S(2)}, u32[]{:S(2)}) collective-permute-start(bf16[4,17,16,128]{3,2,1,0:T(8,128)(2,1)S(1)} %pad_maximum_fusion.refs_0_), channel_id=1, source_target_pairs={{0,6},{2,4},{4,2},{6,0},{8,14},{10,12},{12,10},{14,8},{16,22},{18,... | collective-permute-start | bytes 835592 | tf_op jit(solution)/shard_map/ppermute | solution.py:347
  29.7 13.1 %collective-permute-start.16 = (bf16[4,17,16,128]{3,2,1,0:T(8,128)(2,1)S(1)}, bf16[4,17,16,128]{3,2,1,0:T(8,128)(2,1)S(1)}, u32[]{:S(2)}, u32[]{:S(2)}) collective-permute-start(bf16[4,17,16,128]{3,2,1,0:T(8,128)(2,1)S(1)} %pad_maximum_fusion.refs_0_), channel_id=1, source_target_pairs={{0,4},{2,6},{4,0},{6,2},{8,12},{10,14},{12,8},{14,10},{16,20},{18,... | collective-permute-start | bytes 835592 | tf_op jit(solution)/shard_map/ppermute | solution.py:347
  30.2 12.6 %collective-permute-start.15 = (bf16[4,17,16,128]{3,2,1,0:T(8,128)(2,1)S(1)}, bf16[4,17,16,128]{3,2,1,0:T(8,128)(2,1)S(1)}, u32[]{:S(2)}, u32[]{:S(2)}) collective-permute-start(bf16[4,17,16,128]{3,2,1,0:T(8,128)(2,1)S(1)} %pad_maximum_fusion.refs_0_), channel_id=1, source_target_pairs={{0,2},{2,0},{4,6},{6,4},{8,10},{10,8},{12,14},{14,12},{16,18},{18,... | collective-permute-start | bytes 835592 | tf_op jit(solution)/shard_map/ppermute | solution.py:347
  37.4 11.1 %collective-permute-start.9 = (bf16[4,28,8,128]{3,2,1,0:T(8,128)(2,1)}, bf16[4,28,8,128]{3,2,1,0:T(8,128)(2,1)S(1)}, u32[]{:S(2)}, u32[]{:S(2)}) collective-permute-start(bf16[4,28,8,128]{3,2,1,0:T(8,128)(2,1)} %bitcast.93), channel_id=1, source_target_pairs={{0,8},{2,10},{4,12},{6,14},{8,0},{10,2},{12,4},{14,6},{16,24},{18,... | collective-permute-start | bytes 688136 | tf_op jit(solution)/shard_map/ppermute | solution.py:347
  38.7 18.0 %collective-permute-start.10 = (bf16[4,28,8,128]{3,2,1,0:T(8,128)(2,1)}, bf16[4,28,8,128]{3,2,1,0:T(8,128)(2,1)S(1)}, u32[]{:S(2)}, u32[]{:S(2)}) collective-permute-start(bf16[4,28,8,128]{3,2,1,0:T(8,128)(2,1)} %bitcast.92), channel_id=1, source_target_pairs={{0,16},{2,18},{4,20},{6,22},{8,24},{10,26},{12,28},{14,30},{16,0},... | collective-permute-start | bytes 688136 | tf_op jit(solution)/shard_map/ppermute | solution.py:347
  42.4 14.3 %collective-permute-start.11 = (bf16[4,28,8,128]{3,2,1,0:T(8,128)(2,1)}, bf16[4,28,8,128]{3,2,1,0:T(8,128)(2,1)S(1)}, u32[]{:S(2)}, u32[]{:S(2)}) collective-permute-start(bf16[4,28,8,128]{3,2,1,0:T(8,128)(2,1)} %bitcast.91), channel_id=1, source_target_pairs={{0,24},{2,26},{4,28},{6,30},{8,16},{10,18},{12,20},{14,22},{16,8},... | collective-permute-start | bytes 688136 | tf_op jit(solution)/shard_map/ppermute | solution.py:347
  42.7 28.9 %collective-permute-start.18 = (bf16[4,36,8,128]{3,2,1,0:T(8,128)(2,1)}, bf16[4,36,8,128]{3,2,1,0:T(8,128)(2,1)S(1)}, u32[]{:S(2)}, u32[]{:S(2)}) collective-permute-start(bf16[4,36,8,128]{3,2,1,0:T(8,128)(2,1)} %bitcast.90), channel_id=1, source_target_pairs={{0,2},{2,0},{4,6},{6,4},{8,10},{10,8},{12,14},{14,12},{16,18},{18,... | collective-permute-start | bytes 884744 | tf_op jit(solution)/shard_map/ppermute | solution.py:347
  43.7 28.0 %collective-permute-start.19 = (bf16[4,36,8,128]{3,2,1,0:T(8,128)(2,1)}, bf16[4,36,8,128]{3,2,1,0:T(8,128)(2,1)S(1)}, u32[]{:S(2)}, u32[]{:S(2)}) collective-permute-start(bf16[4,36,8,128]{3,2,1,0:T(8,128)(2,1)} %bitcast.89), channel_id=1, source_target_pairs={{0,4},{2,6},{4,0},{6,2},{8,12},{10,14},{12,8},{14,10},{16,20},{18,... | collective-permute-start | bytes 884744 | tf_op jit(solution)/shard_map/ppermute | solution.py:347
  48.5 23.2 %collective-permute-start.20 = (bf16[4,36,8,128]{3,2,1,0:T(8,128)(2,1)}, bf16[4,36,8,128]{3,2,1,0:T(8,128)(2,1)S(1)}, u32[]{:S(2)}, u32[]{:S(2)}) collective-permute-start(bf16[4,36,8,128]{3,2,1,0:T(8,128)(2,1)} %bitcast.88), channel_id=1, source_target_pairs={{0,6},{2,4},{4,2},{6,0},{8,14},{10,12},{12,10},{14,8},{16,22},{18,... | collective-permute-start | bytes 884744 | tf_op jit(solution)/shard_map/ppermute | solution.py:347
  56.7 1.3 collective-permute-start.24
  60.3 6.3 %collective-permute-start.27 = (bf16[176,128]{1,0:T(8,128)(2,1)}, bf16[176,128]{1,0:T(8,128)(2,1)S(1)}, u32[]{:S(2)}, u32[]{:S(2)}) collective-permute-start(bf16[176,128]{1,0:T(8,128)(2,1)} %get-tuple-element.100), channel_id=1, source_target_pairs={{0,24},{2,26},{4,28},{6,30},{8,16},{10,18},{12,20},{14,22},{16,8},... | collective-permute-start | bytes 135176 | tf_op jit(solution)/shard_map/ppermute | solution.py:347
  62.3 6.4 %collective-permute-start.26 = (bf16[176,128]{1,0:T(8,128)(2,1)}, bf16[176,128]{1,0:T(8,128)(2,1)S(1)}, u32[]{:S(2)}, u32[]{:S(2)}) collective-permute-start(bf16[176,128]{1,0:T(8,128)(2,1)} %get-tuple-element.100), channel_id=1, source_target_pairs={{0,16},{2,18},{4,20},{6,22},{8,24},{10,26},{12,28},{14,30},{16,0},... | collective-permute-start | bytes 135176 | tf_op jit(solution)/shard_map/ppermute | solution.py:347
  66.6 4.3 %collective-permute-start.25 = (bf16[176,128]{1,0:T(8,128)(2,1)}, bf16[176,128]{1,0:T(8,128)(2,1)S(1)}, u32[]{:S(2)}, u32[]{:S(2)}) collective-permute-start(bf16[176,128]{1,0:T(8,128)(2,1)} %get-tuple-element.100), channel_id=1, source_target_pairs={{0,8},{2,10},{4,12},{6,14},{8,0},{10,2},{12,4},{14,6},{16,24},{18,... | collective-permute-start | bytes 135176 | tf_op jit(solution)/shard_map/ppermute | solution.py:347
  74.9 63.9 %copy-start.21 = (f32[160,128]{1,0:T(8,128)S(1)}, f32[160,128]{1,0:T(8,128)}, u32[]{:S(2)}) copy-start(f32[160,128]{1,0:T(8,128)} %get-tuple-element.99) | copy-start | bytes 245764
  74.9 8.5 %collective-permute-start.30 = (bf16[4,176,128]{2,1,0:T(8,128)(2,1)S(1)}, bf16[4,176,128]{2,1,0:T(8,128)(2,1)S(1)}, u32[]{:S(2)}, u32[]{:S(2)}) collective-permute-start(bf16[4,176,128]{2,1,0:T(8,128)(2,1)S(1)} %pad_maximum_fusion.1.refs_0_), channel_id=1, source_target_pairs={{0,6},{2,4},{4,2},{6,0},{8,14},{10,12},{12,10},{14,8},{16,22},{18,... | collective-permute-start | bytes 540680 | tf_op jit(solution)/shard_map/ppermute | solution.py:347
  76.2 7.6 %collective-permute-start.29 = (bf16[4,176,128]{2,1,0:T(8,128)(2,1)S(1)}, bf16[4,176,128]{2,1,0:T(8,128)(2,1)S(1)}, u32[]{:S(2)}, u32[]{:S(2)}) collective-permute-start(bf16[4,176,128]{2,1,0:T(8,128)(2,1)S(1)} %pad_maximum_fusion.1.refs_0_), channel_id=1, source_target_pairs={{0,4},{2,6},{4,0},{6,2},{8,12},{10,14},{12,8},{14,10},{16,20},{18,... | collective-permute-start | bytes 540680 | tf_op jit(solution)/shard_map/ppermute | solution.py:347
  77.1 8.6 %collective-permute-start.28 = (bf16[4,176,128]{2,1,0:T(8,128)(2,1)S(1)}, bf16[4,176,128]{2,1,0:T(8,128)(2,1)S(1)}, u32[]{:S(2)}, u32[]{:S(2)}) collective-permute-start(bf16[4,176,128]{2,1,0:T(8,128)(2,1)S(1)} %pad_maximum_fusion.1.refs_0_), channel_id=1, source_target_pairs={{0,2},{2,0},{4,6},{6,4},{8,10},{10,8},{12,14},{14,12},{16,18},{18,... | collective-permute-start | bytes 540680 | tf_op jit(solution)/shard_map/ppermute | solution.py:347
  78.5 9.6 %collective-permute-start.12 = (bf16[4,28,8,128]{3,2,1,0:T(8,128)(2,1)}, bf16[4,28,8,128]{3,2,1,0:T(8,128)(2,1)S(1)}, u32[]{:S(2)}, u32[]{:S(2)}) collective-permute-start(bf16[4,28,8,128]{3,2,1,0:T(8,128)(2,1)} %get-tuple-element.76), channel_id=1, source_target_pairs={{0,2},{2,0},{4,6},{6,4},{8,10},{10,8},{12,14},{14,12},{16,18},{18,... | collective-permute-start | bytes 688136 | tf_op jit(solution)/shard_map/ppermute | solution.py:347
  79.1 9.5 %collective-permute-start.31 = (bf16[4,176,128]{2,1,0:T(8,128)(2,1)S(1)}, bf16[4,176,128]{2,1,0:T(8,128)(2,1)S(1)}, u32[]{:S(2)}, u32[]{:S(2)}) collective-permute-start(bf16[4,176,128]{2,1,0:T(8,128)(2,1)S(1)} %pad_maximum_fusion.1.refs_0_), channel_id=1, source_target_pairs={{0,1},{1,0},{2,3},{3,2},{4,5},{5,4},{6,7},{7,6},{8,9},{9,8},{10,11... | collective-permute-start | bytes 540680 | tf_op jit(solution)/shard_map/ppermute | solution.py:347
  83.4 7.5 %collective-permute-start.34 = (bf16[4,176,128]{2,1,0:T(8,128)(2,1)S(1)}, bf16[4,176,128]{2,1,0:T(8,128)(2,1)S(1)}, u32[]{:S(2)}, u32[]{:S(2)}) collective-permute-start(bf16[4,176,128]{2,1,0:T(8,128)(2,1)S(1)} %collective-permute-done.30.refs_3_), channel_id=1, source_target_pairs={{0,1},{1,0},{2,3},{3,2},{4,5},{5,4},{6,7},{7,6},{8,9},{9,8},{10,11... | collective-permute-start | bytes 540680 | tf_op jit(solution)/shard_map/ppermute | solution.py:347
  83.9 8.6 %collective-permute-start.33 = (bf16[4,176,128]{2,1,0:T(8,128)(2,1)S(1)}, bf16[4,176,128]{2,1,0:T(8,128)(2,1)S(1)}, u32[]{:S(2)}, u32[]{:S(2)}) collective-permute-start(bf16[4,176,128]{2,1,0:T(8,128)(2,1)S(1)} %collective-permute-done.29.refs_2_), channel_id=1, source_target_pairs={{0,1},{1,0},{2,3},{3,2},{4,5},{5,4},{6,7},{7,6},{8,9},{9,8},{10,11... | collective-permute-start | bytes 540680 | tf_op jit(solution)/shard_map/ppermute | solution.py:347
  85.6 8.1 %collective-permute-start.32 = (bf16[4,176,128]{2,1,0:T(8,128)(2,1)S(1)}, bf16[4,176,128]{2,1,0:T(8,128)(2,1)S(1)}, u32[]{:S(2)}, u32[]{:S(2)}) collective-permute-start(bf16[4,176,128]{2,1,0:T(8,128)(2,1)S(1)} %collective-permute-done.28.refs_1_), channel_id=1, source_target_pairs={{0,1},{1,0},{2,3},{3,2},{4,5},{5,4},{6,7},{7,6},{8,9},{9,8},{10,11... | collective-permute-start | bytes 540680 | tf_op jit(solution)/shard_map/ppermute | solution.py:347
  88.1 22.3 %collective-permute-start.21 = (bf16[4,36,8,128]{3,2,1,0:T(8,128)(2,1)}, bf16[4,36,8,128]{3,2,1,0:T(8,128)(2,1)S(1)}, u32[]{:S(2)}, u32[]{:S(2)}) collective-permute-start(bf16[4,36,8,128]{3,2,1,0:T(8,128)(2,1)} %get-tuple-element.88), channel_id=1, source_target_pairs={{0,8},{2,10},{4,12},{6,14},{8,0},{10,2},{12,4},{14,6},{16,24},{18,... | collective-permute-start | bytes 884744 | tf_op jit(solution)/shard_map/ppermute | solution.py:347
  88.6 23.6 %collective-permute-start.22 = (bf16[4,36,8,128]{3,2,1,0:T(8,128)(2,1)}, bf16[4,36,8,128]{3,2,1,0:T(8,128)(2,1)S(1)}, u32[]{:S(2)}, u32[]{:S(2)}) collective-permute-start(bf16[4,36,8,128]{3,2,1,0:T(8,128)(2,1)} %get-tuple-element.89), channel_id=1, source_target_pairs={{0,16},{2,18},{4,20},{6,22},{8,24},{10,26},{12,28},{14,30},{16,0},... | collective-permute-start | bytes 884744 | tf_op jit(solution)/shard_map/ppermute | solution.py:347
  90.9 21.4 %collective-permute-start.23 = (bf16[4,36,8,128]{3,2,1,0:T(8,128)(2,1)}, bf16[4,36,8,128]{3,2,1,0:T(8,128)(2,1)S(1)}, u32[]{:S(2)}, u32[]{:S(2)}) collective-permute-start(bf16[4,36,8,128]{3,2,1,0:T(8,128)(2,1)} %get-tuple-element.90), channel_id=1, source_target_pairs={{0,24},{2,26},{4,28},{6,30},{8,16},{10,18},{12,20},{14,22},{16,8},... | collective-permute-start | bytes 884744 | tf_op jit(solution)/shard_map/ppermute | solution.py:347
  92.5 17.9 %collective-permute-start.13 = (bf16[4,28,8,128]{3,2,1,0:T(8,128)(2,1)}, bf16[4,28,8,128]{3,2,1,0:T(8,128)(2,1)S(1)}, u32[]{:S(2)}, u32[]{:S(2)}) collective-permute-start(bf16[4,28,8,128]{3,2,1,0:T(8,128)(2,1)} %get-tuple-element.77), channel_id=1, source_target_pairs={{0,4},{2,6},{4,0},{6,2},{8,12},{10,14},{12,8},{14,10},{16,20},{18,... | collective-permute-start | bytes 688136 | tf_op jit(solution)/shard_map/ppermute | solution.py:347
  93.8 16.6 %collective-permute-start.14 = (bf16[4,28,8,128]{3,2,1,0:T(8,128)(2,1)}, bf16[4,28,8,128]{3,2,1,0:T(8,128)(2,1)S(1)}, u32[]{:S(2)}, u32[]{:S(2)}) collective-permute-start(bf16[4,28,8,128]{3,2,1,0:T(8,128)(2,1)} %get-tuple-element.78), channel_id=1, source_target_pairs={{0,6},{2,4},{4,2},{6,0},{8,14},{10,12},{12,10},{14,8},{16,22},{18,... | collective-permute-start | bytes 688136 | tf_op jit(solution)/shard_map/ppermute | solution.py:347
  112.3 1.6 %collective-permute-start.36 = (bf16[4,160,128]{2,1,0:T(8,128)(2,1)}, bf16[4,160,128]{2,1,0:T(8,128)(2,1)S(1)}, u32[]{:S(2)}, u32[]{:S(2)}) collective-permute-start(bf16[4,160,128]{2,1,0:T(8,128)(2,1)} %get-tuple-element.113), channel_id=1, source_target_pairs={{0,1},{1,0},{2,3},{3,2},{4,5},{5,4},{6,7},{7,6},{8,9},{9,8},{10,11... | collective-permute-start | bytes 491528 | tf_op jit(solution)/shard_map/ppermute | solution.py:347
  112.3 11.3 %collective-permute-start.35 = (bf16[4,160,128]{2,1,0:T(8,128)(2,1)}, bf16[4,160,128]{2,1,0:T(8,128)(2,1)S(1)}, u32[]{:S(2)}, u32[]{:S(2)}) collective-permute-start(bf16[4,160,128]{2,1,0:T(8,128)(2,1)} %get-tuple-element.111), channel_id=1, source_target_pairs={{0,1},{1,0},{2,3},{3,2},{4,5},{5,4},{6,7},{7,6},{8,9},{9,8},{10,11... | collective-permute-start | bytes 491528 | tf_op jit(solution)/shard_map/ppermute | solution.py:347
  112.8 3.3 %collective-permute-start.38 = (bf16[4,160,128]{2,1,0:T(8,128)(2,1)}, bf16[4,160,128]{2,1,0:T(8,128)(2,1)S(1)}, u32[]{:S(2)}, u32[]{:S(2)}) collective-permute-start(bf16[4,160,128]{2,1,0:T(8,128)(2,1)} %get-tuple-element.115), channel_id=1, source_target_pairs={{0,1},{1,0},{2,3},{3,2},{4,5},{5,4},{6,7},{7,6},{8,9},{9,8},{10,11... | collective-permute-start | bytes 491528 | tf_op jit(solution)/shard_map/ppermute | solution.py:347
  112.8 5.4 %collective-permute-start.40 = (bf16[4,160,128]{2,1,0:T(8,128)(2,1)}, bf16[4,160,128]{2,1,0:T(8,128)(2,1)S(1)}, u32[]{:S(2)}, u32[]{:S(2)}) collective-permute-start(bf16[4,160,128]{2,1,0:T(8,128)(2,1)} %get-tuple-element.117), channel_id=1, source_target_pairs={{0,1},{1,0},{2,3},{3,2},{4,5},{5,4},{6,7},{7,6},{8,9},{9,8},{10,11... | collective-permute-start | bytes 491528 | tf_op jit(solution)/shard_map/ppermute | solution.py:347
  114.9 8.7 %collective-permute-start.37 = (bf16[4,160,128]{2,1,0:T(8,128)(2,1)S(1)}, bf16[4,160,128]{2,1,0:T(8,128)(2,1)S(1)}, u32[]{:S(2)}, u32[]{:S(2)}) collective-permute-start(bf16[4,160,128]{2,1,0:T(8,128)(2,1)S(1)} %add_convert_fusion.2), channel_id=1, source_target_pairs={{0,2},{2,0},{4,6},{6,4},{8,10},{10,8},{12,14},{14,12},{16,18},{18,... | collective-permute-start | bytes 491528 | tf_op jit(solution)/shard_map/ppermute | solution.py:347
  117.1 9.5 %collective-permute-start.39 = (bf16[4,160,128]{2,1,0:T(8,128)(2,1)S(1)}, bf16[4,160,128]{2,1,0:T(8,128)(2,1)S(1)}, u32[]{:S(2)}, u32[]{:S(2)}) collective-permute-start(bf16[4,160,128]{2,1,0:T(8,128)(2,1)S(1)} %add_convert_fusion.1), channel_id=1, source_target_pairs={{0,4},{2,6},{4,0},{6,2},{8,12},{10,14},{12,8},{14,10},{16,20},{18,... | collective-permute-start | bytes 491528 | tf_op jit(solution)/shard_map/ppermute | solution.py:347
  119.2 7.4 %collective-permute-start.41 = (bf16[4,160,128]{2,1,0:T(8,128)(2,1)S(1)}, bf16[4,160,128]{2,1,0:T(8,128)(2,1)S(1)}, u32[]{:S(2)}, u32[]{:S(2)}) collective-permute-start(bf16[4,160,128]{2,1,0:T(8,128)(2,1)S(1)} %add_convert_fusion), channel_id=1, source_target_pairs={{0,6},{2,4},{4,2},{6,0},{8,14},{10,12},{12,10},{14,8},{16,22},{18,... | collective-permute-start | bytes 491528 | tf_op jit(solution)/shard_map/ppermute | solution.py:347
  127.8 6.1 %collective-permute-start.42 = (bf16[160,128]{1,0:T(8,128)(2,1)S(1)}, bf16[160,128]{1,0:T(8,128)(2,1)S(1)}, u32[]{:S(2)}, u32[]{:S(2)}) collective-permute-start(bf16[160,128]{1,0:T(8,128)(2,1)S(1)} %get-tuple-element.121), channel_id=1, source_target_pairs={{0,8},{2,10},{4,12},{6,14},{8,0},{10,2},{12,4},{14,6},{16,24},{18,... | collective-permute-start | bytes 122888 | tf_op jit(solution)/shard_map/ppermute | solution.py:347
  131.6 5.8 %collective-permute-start.44 = (bf16[160,128]{1,0:T(8,128)(2,1)S(1)}, bf16[160,128]{1,0:T(8,128)(2,1)S(1)}, u32[]{:S(2)}, u32[]{:S(2)}) collective-permute-start(bf16[160,128]{1,0:T(8,128)(2,1)S(1)} %get-tuple-element.122), channel_id=1, source_target_pairs={{0,24},{2,26},{4,28},{6,30},{8,16},{10,18},{12,20},{14,22},{16,8},... | collective-permute-start | bytes 122888 | tf_op jit(solution)/shard_map/ppermute | solution.py:347
  133.9 4.9 %collective-permute-start.43 = (bf16[160,128]{1,0:T(8,128)(2,1)S(1)}, bf16[160,128]{1,0:T(8,128)(2,1)S(1)}, u32[]{:S(2)}, u32[]{:S(2)}) collective-permute-start(bf16[160,128]{1,0:T(8,128)(2,1)S(1)} %get-tuple-element.123), channel_id=1, source_target_pairs={{0,16},{2,18},{4,20},{6,22},{8,24},{10,26},{12,28},{14,30},{16,0},... | collective-permute-start | bytes 122888 | tf_op jit(solution)/shard_map/ppermute | solution.py:347
  138.8 1.3 collective-permute-start.45
  (25 other events, 323.4 us)

commit v4 on v3

--- a/solution.py
+++ b/solution.py
@@ -267,7 +267,7 @@
             pltpu.SemaphoreType.DMA((n, m)),
             pltpu.SemaphoreType.DMA((m,)),
         ],
-        compiler_params=params(60),
+        compiler_params=params(6),
         cost_estimate=SMALL,
         name="regroup",
     )(*values)
@@ -365,17 +365,20 @@
     return own ^ ((position % n) * len(inner)) ^ (position // n)
 
 
-def project_kernel(size, halves, place_ref, ends_ref, starts_ref, w_ref, *refs):
+def project_kernel(size, halves, place_ref, req_ref, w_ref, *refs):
     parts = refs[:len(strides(size)[1])]
     outs, (att, full) = refs[len(parts):-2], refs[-2:]
     heads = parts[0].shape[1] - 1
     nb = parts[0].shape[2]
     blocks = size * nb
-    requests = ends_ref.shape[1]
+    requests = req_ref.shape[1]
     own, half = place_ref[0], place_ref[1]
     at = lax.broadcasted_iota(jnp.int32, (blocks, requests), 0)
     ids = relative(size, own, at // nb) * nb + at % nb
-    member = (ids >= starts_ref[...]) & (ids < ends_ref[...])
+    lengths = jnp.broadcast_to(req_ref[...].astype(F32), (16, requests)).astype(BF)
+    upto = (lax.broadcasted_iota(jnp.int32, (requests, requests), 0) <= lax.broadcasted_iota(jnp.int32, (requests, requests), 1))
+    ends = jnp.dot(lengths, upto.astype(F32).astype(BF), preferred_element_type=F32)[:1].astype(jnp.int32)
+    member = (ids >= ends - req_ref[...]) & (ids < ends)
     packed = jnp.concatenate([part[:, heads].reshape(-1, LANE) for part in parts], axis=0).astype(F32)
     lse = packed + pltpu.roll(packed, LANE - 32, 1) + pltpu.roll(packed, LANE - 64, 1)
     for g in range(heads):
@@ -395,31 +398,34 @@
         outs[0][...] = full[...]
 
 
-def project(size, halves, where, ends, starts, w_out_t, parts):
+def project(size, halves, where, req_row, w_out_t, parts):
     width, depth = w_out_t.shape
-    requests = ends.shape[1]
+    requests = req_row.shape[1]
     outs = tuple(jax.ShapeDtypeStruct((width // halves, requests), F32) for _ in range(halves))
     return pl.pallas_call(
         functools.partial(project_kernel, size, halves),
         out_shape=outs,
-        in_specs=[SMEM] + [VMEM] * (3 + len(parts)),
+        in_specs=[SMEM] + [VMEM] * (2 + len(parts)),
         out_specs=tuple(VMEM for _ in outs),
         scratch_shapes=[pltpu.VMEM((depth, requests), BF), pltpu.VMEM((width, requests), F32)],
-        compiler_params=params(24),
+        compiler_params=params(12),
         cost_estimate=SMALL,
         name="project",
-    )(where, ends, starts, w_out_t, *parts)
+    )(where, req_row, w_out_t, *parts)
 
 
 def stream_kernel(halves, place_ref, res_ref, gain_ref, *refs):
-    terms, (hidden_ref, msg_ref) = refs[:-2], refs[-2:]
+    terms, (hidden_ref, msg_ref, gain) = refs[:-3], refs[-3:]
     n = hidden_ref.shape[0]
     first = pl.multiple_of(place_ref[1] * n, 16) if halves == 2 else 0
     hidden = res_ref[pl.ds(first, n), :].astype(F32)
     for term in terms:
         hidden = hidden + term[...]
     hidden_ref[...] = hidden
-    msg_ref[:n, :] = (hidden * gain_ref[pl.ds(first, n), :]).astype(BF)
+    width = gain_ref.shape[1]
+    row = jnp.concatenate([gain_ref[...], jnp.zeros((1, -width % LANE), F32)], axis=1)
+    gain[...] = jnp.transpose(jnp.broadcast_to(row, (hidden.shape[1], row.shape[1])))
+    msg_ref[:n, :] = (hidden * gain[pl.ds(first, n), :]).astype(BF)
     squares = jnp.sum(hidden * hidden, axis=0, keepdims=True)
     row = lax.broadcasted_iota(jnp.int32, (STAT, hidden.shape[1]), 0)
     stat = jnp.zeros((STAT, hidden.shape[1]), F32)
@@ -428,45 +434,29 @@
     msg_ref[n:, :] = stat.astype(BF)
 
 
-def stream(halves, where, residual_t, gain_wide, terms):
+def stream(halves, where, residual_t, gain, terms):
     n, requests = terms[0].shape
     return pl.pallas_call(
         functools.partial(stream_kernel, halves),
         out_shape=(jax.ShapeDtypeStruct((n, requests), F32), jax.ShapeDtypeStruct((n + STAT, requests), BF)),
         in_specs=[SMEM] + [VMEM] * (2 + len(terms)),
         out_specs=(VMEM, VMEM),
+        scratch_shapes=[pltpu.VMEM((-(-gain.shape[1] // LANE) * LANE, requests), F32)],
+        compiler_params=params(6),
         cost_estimate=SMALL,
         name="stream",
-    )(where, residual_t, gain_wide, *terms)
-
-
-def swiglu_kernel(size, halves, chunk, place_ref, gate_any, up_any, down_any, *refs):
+    )(where, residual_t, gain, *terms)
+
+
+def gate_up_kernel(size, halves, chunk, place_ref, gate, up, *refs):
     n_in = len(strides(size)[1])
     msgs = [refs[h * n_in:(h + 1) * n_in] for h in range(halves)]
-    outs = [refs[(halves + h) * n_in:(halves + h + 1) * n_in] for h in range(halves)]
-    gate, up, down, x, xt, acc_g, acc_u, h_scr, full, sem = refs[2 * halves * n_in:]
+    h_ref, x, xt, acc_g, acc_u = refs[halves * n_in:]
     width, units = gate.shape
     requests = x.shape[1]
-    pieces = width // chunk
     n_outer = len(strides(size)[0])
     own, half = place_ref[0], place_ref[1]
     n = msgs[0][0].shape[1] - STAT
-
-    def copies(i):
-        at = pl.ds(i * chunk if isinstance(i, int) else pl.multiple_of(i * chunk, chunk), chunk)
-        return (pltpu.make_async_copy(gate_any.at[at], gate.at[at], sem.at[0, i]),
-                pltpu.make_async_copy(up_any.at[at], up.at[at], sem.at[1, i]))
-
-    def down_copy(i):
-        at = pl.ds(i * chunk if isinstance(i, int) else pl.multiple_of(i * chunk, chunk), chunk)
-        return pltpu.make_async_copy(down_any.at[:, at], down.at[:, at], sem.at[2, i])
-
-    for i in range(pieces):
-        for c in copies(i):
-            c.start()
-    for i in range(pieces):
-        down_copy(i).start()
-
     squares = jnp.zeros((1, requests), F32)
     for h in range(halves):
         side = half if h == 0 else 1 - half
@@ -485,24 +475,30 @@
     acc_u[...] = jnp.zeros_like(acc_u)
 
     def lap(i, carry):
-        for c in copies(i):
-            c.wait()
         at = pl.ds(pl.multiple_of(i * chunk, chunk), chunk)
         acc_g[...] += jnp.dot(xt[:, at], gate[at, :], preferred_element_type=F32)
         acc_u[...] += jnp.dot(xt[:, at], up[at, :], preferred_element_type=F32)
         return carry
 
-    lax.fori_loop(0, pieces, lap, 0)
+    lax.fori_loop(0, width // chunk, lap, 0)
     g = acc_g[...] * column
-    h_scr[...] = (g / (1.0 + jnp.exp(-g)) * (acc_u[...] * column)).astype(BF)
+    h_ref[...] = (g / (1.0 + jnp.exp(-g)) * (acc_u[...] * column)).astype(BF)
+
+
+def down_kernel(size, halves, chunk, place_ref, h_ref, down, *refs):
+    n_in = len(strides(size)[1])
+    outs, full = [refs[h * n_in:(h + 1) * n_in] for h in range(halves)], refs[-1]
+    width = down.shape[1]
+    n_outer = len(strides(size)[0])
+    own, half = place_ref[0], place_ref[1]
+    n = outs[0][0].shape[1]
 
     def lap_down(i, carry):
-        down_copy(i).wait()
         at = pl.ds(pl.multiple_of(i * chunk, chunk), chunk)
-        full[at, :] = jnp.transpose(jnp.dot(h_scr[...], down[:, at], preferred_element_type=F32))
+        full[at, :] = jnp.transpose(jnp.dot(h_ref[...], down[:, at], preferred_element_type=F32))
         return carry
 
-    lax.fori_loop(0, pieces, lap_down, 0)
+    lax.fori_loop(0, width // chunk, lap_down, 0)
     for h in range(halves):
         side = half if h == 0 else 1 - half
         for k in range(n_in):
@@ -518,30 +514,34 @@
     requests = messages[0].shape[-1]
     n = messages[0].shape[1] - STAT
     chunk = 512
+    hidden = pl.pallas_call(
+        functools.partial(gate_up_kernel, size, halves, chunk),
+        out_shape=jax.ShapeDtypeStruct((requests, units), BF),
+        in_specs=[SMEM] + [VMEM] * (2 + len(messages)),
+        out_specs=VMEM,
+        scratch_shapes=[
+            pltpu.VMEM((width, requests), BF),
+            pltpu.VMEM((requests, width), BF),
+            pltpu.VMEM((requests, units), F32),
+            pltpu.VMEM((requests, units), F32),
+        ],
+        compiler_params=params(29),
+        cost_estimate=SMALL,
+        name="gate_up",
+    )(where, w_gate, w_up, *messages)
     outs = tuple(
         jax.ShapeDtypeStruct((len(outer), n, requests), F32 if h == 0 else BF) for h in range(halves) for _ in inner
     )
     return pl.pallas_call(
-        functools.partial(swiglu_kernel, size, halves, chunk),
+        functools.partial(down_kernel, size, halves, chunk),
         out_shape=outs,
-        in_specs=[SMEM, ANY, ANY, ANY] + [VMEM] * len(messages),
+        in_specs=[SMEM] + [VMEM] * 2,
         out_specs=tuple(VMEM for _ in outs),
-        scratch_shapes=[
-            pltpu.VMEM((width, units), BF),
-            pltpu.VMEM((width, units), BF),
-            pltpu.VMEM((units, width), BF),
-            pltpu.VMEM((width, requests), BF),
-            pltpu.VMEM((requests, width), BF),
-            pltpu.VMEM((requests, units), F32),
-            pltpu.VMEM((requests, units), F32),
-            pltpu.VMEM((requests, units), BF),
-            pltpu.VMEM((width, requests), F32),
-            pltpu.SemaphoreType.DMA((3, width // chunk)),
-        ],
-        compiler_params=params(56),
+        scratch_shapes=[pltpu.VMEM((width, requests), F32)],
+        compiler_params=params(20),
         cost_estimate=SMALL,
-        name="swiglu",
-    )(where, w_gate, w_up, w_down, *messages)
+        name="down",
+    )(where, hidden, w_down)
 
 
 def shards(
@@ -584,7 +584,6 @@
     partial, summaries, rank = attend(
         where, req_blocks, tenant_sizes, drop_table, by_row, keep, level, queries, kvl
     )
-    gain_wide = jnp.broadcast_to(norm_gain[:, None], (norm_gain.shape[0], requests))
     near_parts = after(gather_near(after(partial, near_counts), size), counts)
     parts = gather_far(near_parts, size)
 
@@ -603,16 +602,12 @@
     packed = place(size, where, early_in, late_in, totals)
     packed = packed.reshape(slots, 2, kvl, LANE).transpose(0, 2, 1, 3).reshape(1, slots, kvl, 2 * LANE)
 
-    request_ids = jnp.arange(requests, dtype=jnp.int32)
-    ends = jnp.sum(jnp.where(request_ids[None, :] <= request_ids[:, None], req_blocks[None, :], 0), axis=1)
-    starts = ends - req_blocks
-
-    terms = project(size, halves, where, ends.reshape(1, -1), starts.reshape(1, -1), w_out.T, after(parts, gain_wide))
+    terms = project(size, halves, where, req_blocks.reshape(1, -1), w_out.T, parts)
     if halves == 2:
         terms = (terms[0], swap(terms[1], "mp", 2, 1))
     else:
         terms = (lax.psum(terms[0], "mp"),)
-    hidden, message = stream(halves, where, residual.T, gain_wide, after(terms, first_a))
+    hidden, message = stream(halves, where, residual.T, norm_gain.reshape(1, -1), after(terms, first_a))
 
     near_message = after(gather_near(message, size), second_a, second_b)
     messages = gather_far(near_message, size)

time: 141 us -> 136 us (0.965)
  local copies, waits for them, and re-layouts: 4.41 us -> 11.2 us
  other arithmetic: 9.45 us -> 3.23 us
  Pallas kernels: 41.2 us -> 36.2 us
  waiting for transfers between devices: 33.2 us -> 30.4 us
  starting transfers between devices: 51.4 us -> 53.7 us
    unnamed x54 -> x32, local copies, waits for them, and re-layouts: 2.93 us -> 11.1 us
    pallas_call x1 -> x2, Pallas kernels: 15.1 us -> 10.9 us  [the longest x1 6.04 us: swiglu(): pl.pallas_call(functools.partial(gate_up_kernel, size, halves, chunk), ou...]
    convert_element_type x3, other arithmetic: 3.05 us -> 0.11 us  [shards(): (mine + swap(theirs, 'mp', 2, 1).astype(F32)).astype(BF)]
    ppermute x46, waiting for transfers between devices: 33.2 us -> 30.4 us  [swap(): return lax.ppermute(value, axis, [(i, i ^ distance) for i in range(size)])]
    ppermute x46, starting transfers between devices: 51.4 us -> 53.7 us  [swap(): return lax.ppermute(value, axis, [(i, i ^ distance) for i in range(size)])]
    broadcast_in_dim x1 -> x0, local copies, waits for them, and re-layouts: 1.47 us -> none  [shards(): jnp.broadcast_to(norm_gain[:, None], (norm_gain.shape[0], requests))]
  transfers between devices with their start and end apart: 46 -> 46, of which waited for: 18 -> 18; matrix products, arithmetic and copies ran while one was open for 6% -> 1% of each run, Pallas kernels for 28% -> 25%
where the time goes in v4:
time: 136 us
  starting transfers between devices  53.7 us (39%)
  Pallas kernels  36.2 us (27%)
  waiting for transfers between devices  30.4 us (22%)
  local copies, waits for them, and re-layouts  11.2 us (8%)
  other arithmetic  3.23 us (2%)
    ppermute x46, starting transfers between devices, swap(): return lax.ppermute(value, axis, [(i, i ^ distance) for i in range(size)])  53.7 us
    ppermute x46, waiting for transfers between devices, swap(): return lax.ppermute(value, axis, [(i, i ^ distance) for i in range(size)])  30.4 us
    unnamed x32, local copies, waits for them, and re-layouts  11.1 us
    pallas_call x1, Pallas kernels, attend(): pl.pallas_call(functools.partial(attend_kernel, kvl), out_shape=(jax.Shap...  8.71 us
    pallas_call x1, Pallas kernels, compact(): pl.pallas_call(functools.partial(compact_kernel, size, early, late), out_...  6.12 us
    pallas_call x1, Pallas kernels, swiglu(): pl.pallas_call(functools.partial(gate_up_kernel, size, halves, chunk), ou...  6.04 us
    pallas_call x1, Pallas kernels, swiglu(): pl.pallas_call(functools.partial(down_kernel, size, halves, chunk), out_s...  4.9 us
    pallas_call x2, Pallas kernels, regroup(): pl.pallas_call(functools.partial(regroup_kernel, n), out_shape=(jax.Shape...  4.56 us
  transfers between devices with their start and end apart: 46, of which 18 were waited for; matrix products, arithmetic and copies ran while one was open for 1% of the time, Pallas kernels for 25%

profile of v4, /device:TPU:0, one launch (start us, length us, event | category | flops | bytes accessed | tf_op | source)
XLA Modules:
  0.0 135.8 jit_solution(8238823167651891808)
XLA Ops:
  1.5 5.0 %collective-permute-start.2 = (s32[1,128]{1,0:T(1,128)S(1)}, s32[1,128]{1,0:T(1,128)S(1)}, u32[]{:S(2)}, u32[]{:S(2)}) collective-permute-start(s32[1,128]{1,0:T(1,128)S(1)} %bitcast.79), channel_id=1, source_target_pairs={{0,24},{2,26},{4,28},{6,30},{8,16},{10,18},{12,20},{14,22},{16,8},... | collective-permute-start | bytes 1544 | tf_op jit(solution)/shard_map/ppermute | solution.py:347
  7.7 8.7 %attend.1 = (bf16[17,16,128]{2,1,0:T(8,128)(2,1)}, bf16[16,4,256]{2,1,0:T(4,128)(2,1)}, s32[16,128]{1,0:T(8,128)}) custom-call(s32[2]{0:T(128)} %pad_add_fusion.1.place_ref, s32[128]{0:T(128)} %req_ref.1, s32[4]{0:T(128)} %ten_ref.1, f32[4,16]{1,0:T(4,128)} %table.1, bf16[16384,128]{1,0:T(8,128)(2,1)} %bitcast.67, s32[16,128]{1,0:T(8,128)} %bitcast.77, ...), custom_call_target="tpu_custom_call" | custom-call | flops 335544320 | bytes 5242880 | tf_op jit(solution)/shard_map/attend/pallas_call | solution.py:143
  16.5 3.8 %collective-permute-start.8 = (bf16[17,16,128]{2,1,0:T(8,128)(2,1)}, bf16[17,16,128]{2,1,0:T(8,128)(2,1)S(1)}, u32[]{:S(2)}, u32[]{:S(2)}) collective-permute-start(bf16[17,16,128]{2,1,0:T(8,128)(2,1)} %get-tuple-element.60), channel_id=1, source_target_pairs={{0,24},{2,26},{4,28},{6,30},{8,16},{10,18},{12,20},{14,22},{16,8},... | collective-permute-start | bytes 208904 | tf_op jit(solution)/shard_map/ppermute | solution.py:347
  21.0 2.6 %collective-permute-start.5 = (s32[4,1,128]{2,1,0:T(1,128)S(1)}, s32[4,1,128]{2,1,0:T(1,128)S(1)}, u32[]{:S(2)}, u32[]{:S(2)}) collective-permute-start(s32[4,1,128]{2,1,0:T(1,128)S(1)} %pad_add_fusion.refs_0_), channel_id=1, source_target_pairs={{0,6},{2,4},{4,2},{6,0},{8,14},{10,12},{12,10},{14,8},{16,22},{18,... | collective-permute-start | bytes 6152 | tf_op jit(solution)/shard_map/ppermute | solution.py:347
  24.7 1.0 collective-permute-done.7
  26.1 0.9 pad_maximum_fusion.refs_0_
  27.7 1.9 %collective-permute-start.17 = (bf16[4,17,16,128]{3,2,1,0:T(8,128)(2,1)S(1)}, bf16[4,17,16,128]{3,2,1,0:T(8,128)(2,1)S(1)}, u32[]{:S(2)}, u32[]{:S(2)}) collective-permute-start(bf16[4,17,16,128]{3,2,1,0:T(8,128)(2,1)S(1)} %pad_maximum_fusion.refs_0_), channel_id=1, source_target_pairs={{0,6},{2,4},{4,2},{6,0},{8,14},{10,12},{12,10},{14,8},{16,22},{18,... | collective-permute-start | bytes 835592 | tf_op jit(solution)/shard_map/ppermute | solution.py:347
  30.1 1.0 collective-permute-start.15
  31.2 6.1 %compact.1 = (bf16[112,8,128]{2,1,0:T(8,128)(2,1)}, bf16[112,8,128]{2,1,0:T(8,128)(2,1)}, bf16[112,8,128]{2,1,0:T(8,128)(2,1)}, bf16[112,8,128]{2,1,0:T(8,128)(2...) custom-call(s32[2]{0:T(128)} %pad_add_fusion.1.place_ref, ...), custom_call_target="tpu_custom_call" | custom-call | bytes 1024 | tf_op jit(solution)/shard_map/compact/pallas_call | solution.py:220
  37.3 1.3 collective-permute-start.9
  38.6 2.9 %collective-permute-start.10 = (bf16[4,28,8,128]{3,2,1,0:T(8,128)(2,1)}, bf16[4,28,8,128]{3,2,1,0:T(8,128)(2,1)S(1)}, u32[]{:S(2)}, u32[]{:S(2)}) collective-permute-start(bf16[4,28,8,128]{3,2,1,0:T(8,128)(2,1)} %bitcast.90), channel_id=1, source_target_pairs={{0,16},{2,18},{4,20},{6,22},{8,24},{10,26},{12,28},{14,30},{16,0},... | collective-permute-start | bytes 688136 | tf_op jit(solution)/shard_map/ppermute | solution.py:347
  41.8 1.1 collective-permute-start.18
  42.9 1.4 %collective-permute-start.19 = (bf16[4,36,8,128]{3,2,1,0:T(8,128)(2,1)}, bf16[4,36,8,128]{3,2,1,0:T(8,128)(2,1)S(1)}, u32[]{:S(2)}, u32[]{:S(2)}) collective-permute-start(bf16[4,36,8,128]{3,2,1,0:T(8,128)(2,1)} %bitcast.87), channel_id=1, source_target_pairs={{0,4},{2,6},{4,0},{6,2},{8,12},{10,14},{12,8},{14,10},{16,20},{18,... | collective-permute-start | bytes 884744 | tf_op jit(solution)/shard_map/ppermute | solution.py:347
  44.3 4.1 %collective-permute-done.9.refs_1_ = bf16[4,28,8,128]{3,2,1,0:T(8,128)(2,1)S(1)} collective-permute-done((bf16[4,28,8,128]{3,2,1,0:T(8,128)(2,1)}, bf16[4,28,8,128]{3,2,1,0:T(8,128)(2,1)S(1)}, u32[]{:S(2)}, u32[]{:S(2)}) %collective-permute-start.9) | collective-permute-done | bytes 229408 | tf_op jit(solution)/shard_map/ppermute | solution.py:347
  48.4 2.5 %collective-permute-start.20 = (bf16[4,36,8,128]{3,2,1,0:T(8,128)(2,1)}, bf16[4,36,8,128]{3,2,1,0:T(8,128)(2,1)S(1)}, u32[]{:S(2)}, u32[]{:S(2)}) collective-permute-start(bf16[4,36,8,128]{3,2,1,0:T(8,128)(2,1)} %bitcast.86), channel_id=1, source_target_pairs={{0,6},{2,4},{4,2},{6,0},{8,14},{10,12},{12,10},{14,8},{16,22},{18,... | collective-permute-start | bytes 884744 | tf_op jit(solution)/shard_map/ppermute | solution.py:347
  52.1 2.3 %project.1 = (f32[160,128]{1,0:T(8,128)S(1)}, f32[160,128]{1,0:T(8,128)S(1)}) custom-call(s32[2]{0:T(128)S(1)} %copy-done.7, s32[1,128]{1,0:T(1,128)S(1)} %bitcast.66, bf16[320,2048]{1,0:T(8,128)(2,1)S(1)} %bitcast.61, bf16[4,17,16,128]{3,2,1,0:T(8,128)(2,1)S(1)} %pad_maximum_fusion.refs_0_, bf16[4,17,16,128]{3,2,1,0:T(8,128)(2,1)S(1)} %collective-permute-done.15.refs_1_, ...), custom_call_target="tpu_custom_call" | custom-call | bytes 1024 | tf_op jit(solution)/shard_map/project/pallas_call | solution.py:405
  54.4 1.2 collective-permute-done.10.refs_2_
  55.6 1.3 collective-permute-done.24.refs_1_
  57.5 2.2 %collective-permute-start.27 = (bf16[176,128]{1,0:T(8,128)(2,1)S(1)}, bf16[176,128]{1,0:T(8,128)(2,1)S(1)}, u32[]{:S(2)}, u32[]{:S(2)}) collective-permute-start(bf16[176,128]{1,0:T(8,128)(2,1)S(1)} %get-tuple-element.92), channel_id=1, source_target_pairs={{0,24},{2,26},{4,28},{6,30},{8,16},{10,18},{12,20},{14,22},{16,8},... | collective-permute-start | bytes 135176 | tf_op jit(solution)/shard_map/ppermute | solution.py:347
  59.7 1.3 collective-permute-start.26
  61.0 2.7 %collective-permute-done.27 = bf16[176,128]{1,0:T(8,128)(2,1)S(1)} collective-permute-done((bf16[176,128]{1,0:T(8,128)(2,1)S(1)}, bf16[176,128]{1,0:T(8,128)(2,1)S(1)}, u32[]{:S(2)}, u32[]{:S(2)}) %collective-permute-start.27) | collective-permute-done | bytes 45088 | tf_op jit(solution)/shard_map/ppermute | solution.py:347
  63.7 1.4 %collective-permute-start.25 = (bf16[176,128]{1,0:T(8,128)(2,1)S(1)}, bf16[176,128]{1,0:T(8,128)(2,1)S(1)}, u32[]{:S(2)}, u32[]{:S(2)}) collective-permute-start(bf16[176,128]{1,0:T(8,128)(2,1)S(1)} %get-tuple-element.92), channel_id=1, source_target_pairs={{0,8},{2,10},{4,12},{6,14},{8,0},{10,2},{12,4},{14,6},{16,24},{18,... | collective-permute-start | bytes 135176 | tf_op jit(solution)/shard_map/ppermute | solution.py:347
  65.1 0.9 copy-done.5
  66.0 2.6 %regroup.2 = (bf16[4,28,8,128]{3,2,1,0:T(8,128)(2,1)S(1)}, bf16[4,28,8,128]{3,2,1,0:T(8,128)(2,1)S(1)}, bf16[4,28,8,128]{3,2,1,0:T(8,128)(2,1)}, bf16[4,28,8,128]{3,2,1,0:T(8,128)(2,1)S(1)}) custom-call(bf16[4,28,8,128]{3,2,1,0:T(8,128)(2,1)S(1)} %bitcast.63, bf16[4,28,8,128]{3,2,1,0:T(8,128)(2,1)S(1)} %collective-permute-done.9.refs_1_, ...), custom_call_target="tpu_custom_call" | custom-call | bytes 1024 | tf_op jit(solution)/shard_map/regroup/pallas_call | solution.py:260
  68.7 1.0 copy-done.4
  69.7 1.9 %regroup.3 = (bf16[4,36,8,128]{3,2,1,0:T(8,128)(2,1)S(1)}, bf16[4,36,8,128]{3,2,1,0:T(8,128)(2,1)S(1)}, bf16[4,36,8,128]{3,2,1,0:T(8,128)(2,1)S(1)}, bf16[4,36,8,128]{3,2,1,0:T(8,128)(2,1)S(1)}) custom-call(bf16[4,36,8,128]{3,2,1,0:T(8,128)(2,1)S(1)} %bitcast.62, bf16[4,36,8,128]{3,2,1,0:T(8,128)(2,1)S(1)} %collective-permute-done.18.refs_1_, ...), custom_call_target="tpu_custom_call" | custom-call | bytes 1024 | tf_op jit(solution)/shard_map/regroup/pallas_call | solution.py:260
  71.6 2.1 %collective-permute-start.30 = (bf16[4,176,128]{2,1,0:T(8,128)(2,1)S(1)}, bf16[4,176,128]{2,1,0:T(8,128)(2,1)S(1)}, u32[]{:S(2)}, u32[]{:S(2)}) collective-permute-start(bf16[4,176,128]{2,1,0:T(8,128)(2,1)S(1)} %pad_maximum_fusion.1.refs_0_), channel_id=1, source_target_pairs={{0,6},{2,4},{4,2},{6,0},{8,14},{10,12},{12,10},{14,8},{16,22},{18,... | collective-permute-start | bytes 540680 | tf_op jit(solution)/shard_map/ppermute | solution.py:347
  75.2 1.2 collective-permute-start.12
  76.4 3.7 %collective-permute-done.30.refs_3_ = bf16[4,176,128]{2,1,0:T(8,128)(2,1)S(1)} collective-permute-done((bf16[4,176,128]{2,1,0:T(8,128)(2,1)S(1)}, bf16[4,176,128]{2,1,0:T(8,128)(2,1)S(1)}, u32[]{:S(2)}, u32[]{:S(2)}) %collective-permute-start.30) | collective-permute-done | bytes 180256 | tf_op jit(solution)/shard_map/ppermute | solution.py:347
  80.6 2.2 %collective-permute-done.28.refs_1_ = bf16[4,176,128]{2,1,0:T(8,128)(2,1)S(1)} collective-permute-done((bf16[4,176,128]{2,1,0:T(8,128)(2,1)S(1)}, bf16[4,176,128]{2,1,0:T(8,128)(2,1)S(1)}, u32[]{:S(2)}, u32[]{:S(2)}) %collective-permute-start.28) | collective-permute-done | bytes 180256 | tf_op jit(solution)/shard_map/ppermute | solution.py:347
  82.8 2.5 %collective-permute-done.12.refs_1_ = bf16[4,28,8,128]{3,2,1,0:T(8,128)(2,1)S(1)} collective-permute-done((bf16[4,28,8,128]{3,2,1,0:T(8,128)(2,1)S(1)}, bf16[4,28,8,128]{3,2,1,0:T(8,128)(2,1)S(1)}, u32[]{:S(2)}, u32[]{:S(2)}) %collective-permute-start.12) | collective-permute-done | bytes 229408 | tf_op jit(solution)/shard_map/ppermute | solution.py:347
  85.3 1.7 %collective-permute-start.21 = (bf16[4,36,8,128]{3,2,1,0:T(8,128)(2,1)S(1)}, bf16[4,36,8,128]{3,2,1,0:T(8,128)(2,1)S(1)}, u32[]{:S(2)}, u32[]{:S(2)}) collective-permute-start(bf16[4,36,8,128]{3,2,1,0:T(8,128)(2,1)S(1)} %get-tuple-element.84), channel_id=1, source_target_pairs={{0,8},{2,10},{4,12},{6,14},{8,0},{10,2},{12,4},{14,6},{16,24},{18,... | collective-permute-start | bytes 884744 | tf_op jit(solution)/shard_map/ppermute | solution.py:347
  87.0 1.0 collective-permute-start.22
  88.0 1.7 %collective-permute-start.23 = (bf16[4,36,8,128]{3,2,1,0:T(8,128)(2,1)S(1)}, bf16[4,36,8,128]{3,2,1,0:T(8,128)(2,1)S(1)}, u32[]{:S(2)}, u32[]{:S(2)}) collective-permute-start(bf16[4,36,8,128]{3,2,1,0:T(8,128)(2,1)S(1)} %get-tuple-element.86), channel_id=1, source_target_pairs={{0,24},{2,26},{4,28},{6,30},{8,16},{10,18},{12,20},{14,22},{16,8},... | collective-permute-start | bytes 884744 | tf_op jit(solution)/shard_map/ppermute | solution.py:347
  90.3 2.0 %collective-permute-start.14 = (bf16[4,28,8,128]{3,2,1,0:T(8,128)(2,1)S(1)}, bf16[4,28,8,128]{3,2,1,0:T(8,128)(2,1)S(1)}, u32[]{:S(2)}, u32[]{:S(2)}) collective-permute-start(bf16[4,28,8,128]{3,2,1,0:T(8,128)(2,1)S(1)} %get-tuple-element.74), channel_id=1, source_target_pairs={{0,6},{2,4},{4,2},{6,0},{8,14},{10,12},{12,10},{14,8},{16,22},{18,... | collective-permute-start | bytes 688136 | tf_op jit(solution)/shard_map/ppermute | solution.py:347
  92.3 4.0 %copy-done = bf16[5120,1024]{1,0:T(8,128)(2,1)S(1)} copy-done((bf16[5120,1024]{1,0:T(8,128)(2,1)S(1)}, bf16[5120,1024]{1,0:T(8,128)(2,1)}, u32[]{:S(2)}) %copy-start) | copy-done | bytes 10485784
  96.3 4.0 %copy-done.1 = bf16[5120,1024]{1,0:T(8,128)(2,1)S(1)} copy-done((bf16[5120,1024]{1,0:T(8,128)(2,1)S(1)}, bf16[5120,1024]{1,0:T(8,128)(2,1)}, u32[]{:S(2)}) %copy-start.1) | copy-done | bytes 10485784
  100.2 6.0 %gate_up.1.h_ref = bf16[128,1024]{1,0:T(8,128)(2,1)S(1)} custom-call(s32[2]{0:T(128)S(1)} %copy-done.8, bf16[5120,1024]{1,0:T(8,128)(2,1)S(1)} %copy-done, bf16[5120,1024]{1,0:T(8,128)(2,1)S(1)} %copy-done.1, bf16[4,176,128]{2,1,0:T(8,128)(2,1)S(1)} %pad_maximum_fusion.1.refs_0_, bf16[4,176,128]{2,1,0:T(8,128)(2,1)S(1)} %collective-permute-done.28.refs_1_, ...), custom_call_target="tpu_custom_call" | custom-call | bytes 1024 | tf_op jit(solution)/shard_map/gate_up/pallas_call | solution.py:517
  106.3 4.9 %down.2 = (f32[4,160,128]{2,1,0:T(8,128)S(1)}, f32[4,160,128]{2,1,0:T(8,128)S(1)}, f32[4,160,128]{2,1,0:T(8,128)S(1)}, f32[4,160,128]{2,1,0:T(8,128)S(1)}, bf16[...) custom-call(s32[2]{0:T(128)S(1)} %copy-done.8, ...), custom_call_target="tpu_custom_call" | custom-call | bytes 1024 | tf_op jit(solution)/shard_map/down/pallas_call | solution.py:535
  112.8 1.0 collective-permute-start.37
  114.5 2.0 %collective-permute-start.41 = (bf16[4,160,128]{2,1,0:T(8,128)(2,1)S(1)}, bf16[4,160,128]{2,1,0:T(8,128)(2,1)S(1)}, u32[]{:S(2)}, u32[]{:S(2)}) collective-permute-start(bf16[4,160,128]{2,1,0:T(8,128)(2,1)S(1)} %add_convert_fusion), channel_id=1, source_target_pairs={{0,6},{2,4},{4,2},{6,0},{8,14},{10,12},{12,10},{14,8},{16,22},{18,... | collective-permute-start | bytes 491528 | tf_op jit(solution)/shard_map/ppermute | solution.py:347
  116.5 2.9 %place.1 = bf16[1024,8,128]{2,1,0:T(8,128)(2,1)} custom-call(s32[2]{0:T(128)S(1)} %copy-done.8, s32[16,128]{1,0:T(8,128)S(1)} %copy-done.9, bf16[4,28,8,128]{3,2,1,0:T(8,128)(2,1)S(1)} %get-tuple-element.71.refs_0_, bf16[4,28,8,128]{3,2,1,0:T(8,128)(2,1)S(1)} %collective-permute-done.12.refs_1_, bf16[4,28,8,128]{3,2,1,0:T(8,128)(2,1)S(1)} %collective-permute-done.13.refs_2_, ...), custom_call_target="tpu_custom_call" | custom-call | bytes 1024 | tf_op jit(solution)/shard_map/place/pallas_call | solution.py:324
  119.9 3.5 %collective-permute-done.39 = bf16[4,160,128]{2,1,0:T(8,128)(2,1)S(1)} collective-permute-done((bf16[4,160,128]{2,1,0:T(8,128)(2,1)S(1)}, bf16[4,160,128]{2,1,0:T(8,128)(2,1)S(1)}, u32[]{:S(2)}, u32[]{:S(2)}) %collective-permute-start.39) | collective-permute-done | bytes 163872 | tf_op jit(solution)/shard_map/ppermute | solution.py:347
  123.4 3.1 %collective-permute-start.42 = (bf16[160,128]{1,0:T(8,128)(2,1)S(1)}, bf16[160,128]{1,0:T(8,128)(2,1)S(1)}, u32[]{:S(2)}, u32[]{:S(2)}) collective-permute-start(bf16[160,128]{1,0:T(8,128)(2,1)S(1)} %get-tuple-element.113), channel_id=1, source_target_pairs={{0,8},{2,10},{4,12},{6,14},{8,0},{10,2},{12,4},{14,6},{16,24},{18,... | collective-permute-start | bytes 122888 | tf_op jit(solution)/shard_map/ppermute | solution.py:347
  126.6 2.3 %collective-permute-start.44 = (bf16[160,128]{1,0:T(8,128)(2,1)S(1)}, bf16[160,128]{1,0:T(8,128)(2,1)S(1)}, u32[]{:S(2)}, u32[]{:S(2)}) collective-permute-start(bf16[160,128]{1,0:T(8,128)(2,1)S(1)} %get-tuple-element.114), channel_id=1, source_target_pairs={{0,24},{2,26},{4,28},{6,30},{8,16},{10,18},{12,20},{14,22},{16,8},... | collective-permute-start | bytes 122888 | tf_op jit(solution)/shard_map/ppermute | solution.py:347
  128.9 3.5 %collective-permute-done.44 = bf16[160,128]{1,0:T(8,128)(2,1)S(1)} collective-permute-done((bf16[160,128]{1,0:T(8,128)(2,1)S(1)}, bf16[160,128]{1,0:T(8,128)(2,1)S(1)}, u32[]{:S(2)}, u32[]{:S(2)}) %collective-permute-start.44) | collective-permute-done | bytes 40992 | tf_op jit(solution)/shard_map/ppermute | solution.py:347
  132.4 1.4 %collective-permute-done.43 = bf16[160,128]{1,0:T(8,128)(2,1)S(1)} collective-permute-done((bf16[160,128]{1,0:T(8,128)(2,1)S(1)}, bf16[160,128]{1,0:T(8,128)(2,1)S(1)}, u32[]{:S(2)}, u32[]{:S(2)}) %collective-permute-start.43) | collective-permute-done | bytes 40992 | tf_op jit(solution)/shard_map/ppermute | solution.py:347
  133.9 1.2 collective-permute-done.45
  (99 shorter events, 13.7 us)
Async XLA Ops:
  0.7 56.2 %copy-start.6 = (bf16[128,320]{0,1:T(8,128)(2,1)S(1)}, bf16[128,320]{0,1:T(8,128)(2,1)}, u32[]{:S(2)}) copy-start(bf16[128,320]{0,1:T(8,128)(2,1)} %param.20) | copy-start | bytes 245764
  1.5 15.0 %collective-permute-start.2 = (s32[1,128]{1,0:T(1,128)S(1)}, s32[1,128]{1,0:T(1,128)S(1)}, u32[]{:S(2)}, u32[]{:S(2)}) collective-permute-start(s32[1,128]{1,0:T(1,128)S(1)} %bitcast.79), channel_id=1, source_target_pairs={{0,24},{2,26},{4,28},{6,30},{8,16},{10,18},{12,20},{14,22},{16,8},... | collective-permute-start | bytes 1544 | tf_op jit(solution)/shard_map/ppermute | solution.py:347
  6.5 9.9 %collective-permute-start.1 = (s32[1,128]{1,0:T(1,128)S(1)}, s32[1,128]{1,0:T(1,128)S(1)}, u32[]{:S(2)}, u32[]{:S(2)}) collective-permute-start(s32[1,128]{1,0:T(1,128)S(1)} %bitcast.80), channel_id=1, source_target_pairs={{0,16},{2,18},{4,20},{6,22},{8,24},{10,26},{12,28},{14,30},{16,0},... | collective-permute-start | bytes 1544 | tf_op jit(solution)/shard_map/ppermute | solution.py:347
  6.5 9.9 %collective-permute-start = (s32[1,128]{1,0:T(1,128)S(1)}, s32[1,128]{1,0:T(1,128)S(1)}, u32[]{:S(2)}, u32[]{:S(2)}) collective-permute-start(s32[1,128]{1,0:T(1,128)S(1)} %bitcast.81), channel_id=1, source_target_pairs={{0,8},{2,10},{4,12},{6,14},{8,0},{10,2},{12,4},{14,6},{16,24},{18,... | collective-permute-start | bytes 1544 | tf_op jit(solution)/shard_map/ppermute | solution.py:347
  7.7 84.5 %copy-start.8 = (s32[2]{0:T(128)S(1)}, s32[2]{0:T(128)}, u32[]{:S(2)}) copy-start(s32[2]{0:T(128)} %pad_add_fusion.1.place_ref) | copy-start | bytes 28
  16.5 7.6 %collective-permute-start.8 = (bf16[17,16,128]{2,1,0:T(8,128)(2,1)}, bf16[17,16,128]{2,1,0:T(8,128)(2,1)S(1)}, u32[]{:S(2)}, u32[]{:S(2)}) collective-permute-start(bf16[17,16,128]{2,1,0:T(8,128)(2,1)} %get-tuple-element.60), channel_id=1, source_target_pairs={{0,24},{2,26},{4,28},{6,30},{8,16},{10,18},{12,20},{14,22},{16,8},... | collective-permute-start | bytes 208904 | tf_op jit(solution)/shard_map/ppermute | solution.py:347
  20.3 5.5 %collective-permute-start.7 = (bf16[17,16,128]{2,1,0:T(8,128)(2,1)}, bf16[17,16,128]{2,1,0:T(8,128)(2,1)S(1)}, u32[]{:S(2)}, u32[]{:S(2)}) collective-permute-start(bf16[17,16,128]{2,1,0:T(8,128)(2,1)} %get-tuple-element.60), channel_id=1, source_target_pairs={{0,16},{2,18},{4,20},{6,22},{8,24},{10,26},{12,28},{14,30},{16,0},... | collective-permute-start | bytes 208904 | tf_op jit(solution)/shard_map/ppermute | solution.py:347
  20.3 5.8 %collective-permute-start.6 = (bf16[17,16,128]{2,1,0:T(8,128)(2,1)}, bf16[17,16,128]{2,1,0:T(8,128)(2,1)S(1)}, u32[]{:S(2)}, u32[]{:S(2)}) collective-permute-start(bf16[17,16,128]{2,1,0:T(8,128)(2,1)} %get-tuple-element.60), channel_id=1, source_target_pairs={{0,8},{2,10},{4,12},{6,14},{8,0},{10,2},{12,4},{14,6},{16,24},{18,... | collective-permute-start | bytes 208904 | tf_op jit(solution)/shard_map/ppermute | solution.py:347
  21.0 6.0 %collective-permute-start.5 = (s32[4,1,128]{2,1,0:T(1,128)S(1)}, s32[4,1,128]{2,1,0:T(1,128)S(1)}, u32[]{:S(2)}, u32[]{:S(2)}) collective-permute-start(s32[4,1,128]{2,1,0:T(1,128)S(1)} %pad_add_fusion.refs_0_), channel_id=1, source_target_pairs={{0,6},{2,4},{4,2},{6,0},{8,14},{10,12},{12,10},{14,8},{16,22},{18,... | collective-permute-start | bytes 6152 | tf_op jit(solution)/shard_map/ppermute | solution.py:347
  23.5 3.6 %collective-permute-start.4 = (s32[4,1,128]{2,1,0:T(1,128)S(1)}, s32[4,1,128]{2,1,0:T(1,128)S(1)}, u32[]{:S(2)}, u32[]{:S(2)}) collective-permute-start(s32[4,1,128]{2,1,0:T(1,128)S(1)} %pad_add_fusion.refs_0_), channel_id=1, source_target_pairs={{0,4},{2,6},{4,0},{6,2},{8,12},{10,14},{12,8},{14,10},{16,20},{18,... | collective-permute-start | bytes 6152 | tf_op jit(solution)/shard_map/ppermute | solution.py:347
  24.1 3.6 %collective-permute-start.3 = (s32[4,1,128]{2,1,0:T(1,128)S(1)}, s32[4,1,128]{2,1,0:T(1,128)S(1)}, u32[]{:S(2)}, u32[]{:S(2)}) collective-permute-start(s32[4,1,128]{2,1,0:T(1,128)S(1)} %pad_add_fusion.refs_0_), channel_id=1, source_target_pairs={{0,2},{2,0},{4,6},{6,4},{8,10},{10,8},{12,14},{14,12},{16,18},{18,... | collective-permute-start | bytes 6152 | tf_op jit(solution)/shard_map/ppermute | solution.py:347
  27.7 13.9 %collective-permute-start.17 = (bf16[4,17,16,128]{3,2,1,0:T(8,128)(2,1)S(1)}, bf16[4,17,16,128]{3,2,1,0:T(8,128)(2,1)S(1)}, u32[]{:S(2)}, u32[]{:S(2)}) collective-permute-start(bf16[4,17,16,128]{3,2,1,0:T(8,128)(2,1)S(1)} %pad_maximum_fusion.refs_0_), channel_id=1, source_target_pairs={{0,6},{2,4},{4,2},{6,0},{8,14},{10,12},{12,10},{14,8},{16,22},{18,... | collective-permute-start | bytes 835592 | tf_op jit(solution)/shard_map/ppermute | solution.py:347
  29.6 12.2 %collective-permute-start.16 = (bf16[4,17,16,128]{3,2,1,0:T(8,128)(2,1)S(1)}, bf16[4,17,16,128]{3,2,1,0:T(8,128)(2,1)S(1)}, u32[]{:S(2)}, u32[]{:S(2)}) collective-permute-start(bf16[4,17,16,128]{3,2,1,0:T(8,128)(2,1)S(1)} %pad_maximum_fusion.refs_0_), channel_id=1, source_target_pairs={{0,4},{2,6},{4,0},{6,2},{8,12},{10,14},{12,8},{14,10},{16,20},{18,... | collective-permute-start | bytes 835592 | tf_op jit(solution)/shard_map/ppermute | solution.py:347
  30.1 11.6 %collective-permute-start.15 = (bf16[4,17,16,128]{3,2,1,0:T(8,128)(2,1)S(1)}, bf16[4,17,16,128]{3,2,1,0:T(8,128)(2,1)S(1)}, u32[]{:S(2)}, u32[]{:S(2)}) collective-permute-start(bf16[4,17,16,128]{3,2,1,0:T(8,128)(2,1)S(1)} %pad_maximum_fusion.refs_0_), channel_id=1, source_target_pairs={{0,2},{2,0},{4,6},{6,4},{8,10},{10,8},{12,14},{14,12},{16,18},{18,... | collective-permute-start | bytes 835592 | tf_op jit(solution)/shard_map/ppermute | solution.py:347
  37.3 11.1 %collective-permute-start.9 = (bf16[4,28,8,128]{3,2,1,0:T(8,128)(2,1)}, bf16[4,28,8,128]{3,2,1,0:T(8,128)(2,1)S(1)}, u32[]{:S(2)}, u32[]{:S(2)}) collective-permute-start(bf16[4,28,8,128]{3,2,1,0:T(8,128)(2,1)} %bitcast.91), channel_id=1, source_target_pairs={{0,8},{2,10},{4,12},{6,14},{8,0},{10,2},{12,4},{14,6},{16,24},{18,... | collective-permute-start | bytes 688136 | tf_op jit(solution)/shard_map/ppermute | solution.py:347
  38.6 16.9 %collective-permute-start.10 = (bf16[4,28,8,128]{3,2,1,0:T(8,128)(2,1)}, bf16[4,28,8,128]{3,2,1,0:T(8,128)(2,1)S(1)}, u32[]{:S(2)}, u32[]{:S(2)}) collective-permute-start(bf16[4,28,8,128]{3,2,1,0:T(8,128)(2,1)} %bitcast.90), channel_id=1, source_target_pairs={{0,16},{2,18},{4,20},{6,22},{8,24},{10,26},{12,28},{14,30},{16,0},... | collective-permute-start | bytes 688136 | tf_op jit(solution)/shard_map/ppermute | solution.py:347
  41.5 14.0 %collective-permute-start.11 = (bf16[4,28,8,128]{3,2,1,0:T(8,128)(2,1)}, bf16[4,28,8,128]{3,2,1,0:T(8,128)(2,1)S(1)}, u32[]{:S(2)}, u32[]{:S(2)}) collective-permute-start(bf16[4,28,8,128]{3,2,1,0:T(8,128)(2,1)} %bitcast.89), channel_id=1, source_target_pairs={{0,24},{2,26},{4,28},{6,30},{8,16},{10,18},{12,20},{14,22},{16,8},... | collective-permute-start | bytes 688136 | tf_op jit(solution)/shard_map/ppermute | solution.py:347
  41.8 26.9 %collective-permute-start.18 = (bf16[4,36,8,128]{3,2,1,0:T(8,128)(2,1)}, bf16[4,36,8,128]{3,2,1,0:T(8,128)(2,1)S(1)}, u32[]{:S(2)}, u32[]{:S(2)}) collective-permute-start(bf16[4,36,8,128]{3,2,1,0:T(8,128)(2,1)} %bitcast.88), channel_id=1, source_target_pairs={{0,2},{2,0},{4,6},{6,4},{8,10},{10,8},{12,14},{14,12},{16,18},{18,... | collective-permute-start | bytes 884744 | tf_op jit(solution)/shard_map/ppermute | solution.py:347
  42.9 25.8 %collective-permute-start.19 = (bf16[4,36,8,128]{3,2,1,0:T(8,128)(2,1)}, bf16[4,36,8,128]{3,2,1,0:T(8,128)(2,1)S(1)}, u32[]{:S(2)}, u32[]{:S(2)}) collective-permute-start(bf16[4,36,8,128]{3,2,1,0:T(8,128)(2,1)} %bitcast.87), channel_id=1, source_target_pairs={{0,4},{2,6},{4,0},{6,2},{8,12},{10,14},{12,8},{14,10},{16,20},{18,... | collective-permute-start | bytes 884744 | tf_op jit(solution)/shard_map/ppermute | solution.py:347
  48.4 20.3 %collective-permute-start.20 = (bf16[4,36,8,128]{3,2,1,0:T(8,128)(2,1)}, bf16[4,36,8,128]{3,2,1,0:T(8,128)(2,1)S(1)}, u32[]{:S(2)}, u32[]{:S(2)}) collective-permute-start(bf16[4,36,8,128]{3,2,1,0:T(8,128)(2,1)} %bitcast.86), channel_id=1, source_target_pairs={{0,6},{2,4},{4,2},{6,0},{8,14},{10,12},{12,10},{14,8},{16,22},{18,... | collective-permute-start | bytes 884744 | tf_op jit(solution)/shard_map/ppermute | solution.py:347
  55.5 1.3 collective-permute-start.24
  57.5 6.2 %collective-permute-start.27 = (bf16[176,128]{1,0:T(8,128)(2,1)S(1)}, bf16[176,128]{1,0:T(8,128)(2,1)S(1)}, u32[]{:S(2)}, u32[]{:S(2)}) collective-permute-start(bf16[176,128]{1,0:T(8,128)(2,1)S(1)} %get-tuple-element.92), channel_id=1, source_target_pairs={{0,24},{2,26},{4,28},{6,30},{8,16},{10,18},{12,20},{14,22},{16,8},... | collective-permute-start | bytes 135176 | tf_op jit(solution)/shard_map/ppermute | solution.py:347
  59.7 8.9 %collective-permute-start.26 = (bf16[176,128]{1,0:T(8,128)(2,1)S(1)}, bf16[176,128]{1,0:T(8,128)(2,1)S(1)}, u32[]{:S(2)}, u32[]{:S(2)}) collective-permute-start(bf16[176,128]{1,0:T(8,128)(2,1)S(1)} %get-tuple-element.92), channel_id=1, source_target_pairs={{0,16},{2,18},{4,20},{6,22},{8,24},{10,26},{12,28},{14,30},{16,0},... | collective-permute-start | bytes 135176 | tf_op jit(solution)/shard_map/ppermute | solution.py:347
  63.7 5.0 %collective-permute-start.25 = (bf16[176,128]{1,0:T(8,128)(2,1)S(1)}, bf16[176,128]{1,0:T(8,128)(2,1)S(1)}, u32[]{:S(2)}, u32[]{:S(2)}) collective-permute-start(bf16[176,128]{1,0:T(8,128)(2,1)S(1)} %get-tuple-element.92), channel_id=1, source_target_pairs={{0,8},{2,10},{4,12},{6,14},{8,0},{10,2},{12,4},{14,6},{16,24},{18,... | collective-permute-start | bytes 135176 | tf_op jit(solution)/shard_map/ppermute | solution.py:347
  71.6 8.5 %collective-permute-start.30 = (bf16[4,176,128]{2,1,0:T(8,128)(2,1)S(1)}, bf16[4,176,128]{2,1,0:T(8,128)(2,1)S(1)}, u32[]{:S(2)}, u32[]{:S(2)}) collective-permute-start(bf16[4,176,128]{2,1,0:T(8,128)(2,1)S(1)} %pad_maximum_fusion.1.refs_0_), channel_id=1, source_target_pairs={{0,6},{2,4},{4,2},{6,0},{8,14},{10,12},{12,10},{14,8},{16,22},{18,... | collective-permute-start | bytes 540680 | tf_op jit(solution)/shard_map/ppermute | solution.py:347
  73.8 6.9 %collective-permute-start.29 = (bf16[4,176,128]{2,1,0:T(8,128)(2,1)S(1)}, bf16[4,176,128]{2,1,0:T(8,128)(2,1)S(1)}, u32[]{:S(2)}, u32[]{:S(2)}) collective-permute-start(bf16[4,176,128]{2,1,0:T(8,128)(2,1)S(1)} %pad_maximum_fusion.1.refs_0_), channel_id=1, source_target_pairs={{0,4},{2,6},{4,0},{6,2},{8,12},{10,14},{12,8},{14,10},{16,20},{18,... | collective-permute-start | bytes 540680 | tf_op jit(solution)/shard_map/ppermute | solution.py:347
  74.4 8.4 %collective-permute-start.28 = (bf16[4,176,128]{2,1,0:T(8,128)(2,1)S(1)}, bf16[4,176,128]{2,1,0:T(8,128)(2,1)S(1)}, u32[]{:S(2)}, u32[]{:S(2)}) collective-permute-start(bf16[4,176,128]{2,1,0:T(8,128)(2,1)S(1)} %pad_maximum_fusion.1.refs_0_), channel_id=1, source_target_pairs={{0,2},{2,0},{4,6},{6,4},{8,10},{10,8},{12,14},{14,12},{16,18},{18,... | collective-permute-start | bytes 540680 | tf_op jit(solution)/shard_map/ppermute | solution.py:347
  75.2 10.1 %collective-permute-start.12 = (bf16[4,28,8,128]{3,2,1,0:T(8,128)(2,1)S(1)}, bf16[4,28,8,128]{3,2,1,0:T(8,128)(2,1)S(1)}, u32[]{:S(2)}, u32[]{:S(2)}) collective-permute-start(bf16[4,28,8,128]{3,2,1,0:T(8,128)(2,1)S(1)} %get-tuple-element.72), channel_id=1, source_target_pairs={{0,2},{2,0},{4,6},{6,4},{8,10},{10,8},{12,14},{14,12},{16,18},{18,... | collective-permute-start | bytes 688136 | tf_op jit(solution)/shard_map/ppermute | solution.py:347
  76.4 10.6 %collective-permute-start.31 = (bf16[4,176,128]{2,1,0:T(8,128)(2,1)S(1)}, bf16[4,176,128]{2,1,0:T(8,128)(2,1)S(1)}, u32[]{:S(2)}, u32[]{:S(2)}) collective-permute-start(bf16[4,176,128]{2,1,0:T(8,128)(2,1)S(1)} %pad_maximum_fusion.1.refs_0_), channel_id=1, source_target_pairs={{0,1},{1,0},{2,3},{3,2},{4,5},{5,4},{6,7},{7,6},{8,9},{9,8},{10,11... | collective-permute-start | bytes 540680 | tf_op jit(solution)/shard_map/ppermute | solution.py:347
  80.1 7.9 %collective-permute-start.34 = (bf16[4,176,128]{2,1,0:T(8,128)(2,1)S(1)}, bf16[4,176,128]{2,1,0:T(8,128)(2,1)S(1)}, u32[]{:S(2)}, u32[]{:S(2)}) collective-permute-start(bf16[4,176,128]{2,1,0:T(8,128)(2,1)S(1)} %collective-permute-done.30.refs_3_), channel_id=1, source_target_pairs={{0,1},{1,0},{2,3},{3,2},{4,5},{5,4},{6,7},{7,6},{8,9},{9,8},{10,11... | collective-permute-start | bytes 540680 | tf_op jit(solution)/shard_map/ppermute | solution.py:347
  80.6 9.0 %collective-permute-start.33 = (bf16[4,176,128]{2,1,0:T(8,128)(2,1)S(1)}, bf16[4,176,128]{2,1,0:T(8,128)(2,1)S(1)}, u32[]{:S(2)}, u32[]{:S(2)}) collective-permute-start(bf16[4,176,128]{2,1,0:T(8,128)(2,1)S(1)} %collective-permute-done.29.refs_2_), channel_id=1, source_target_pairs={{0,1},{1,0},{2,3},{3,2},{4,5},{5,4},{6,7},{7,6},{8,9},{9,8},{10,11... | collective-permute-start | bytes 540680 | tf_op jit(solution)/shard_map/ppermute | solution.py:347
  82.8 7.5 %collective-permute-start.32 = (bf16[4,176,128]{2,1,0:T(8,128)(2,1)S(1)}, bf16[4,176,128]{2,1,0:T(8,128)(2,1)S(1)}, u32[]{:S(2)}, u32[]{:S(2)}) collective-permute-start(bf16[4,176,128]{2,1,0:T(8,128)(2,1)S(1)} %collective-permute-done.28.refs_1_), channel_id=1, source_target_pairs={{0,1},{1,0},{2,3},{3,2},{4,5},{5,4},{6,7},{7,6},{8,9},{9,8},{10,11... | collective-permute-start | bytes 540680 | tf_op jit(solution)/shard_map/ppermute | solution.py:347
  85.3 26.0 %collective-permute-start.21 = (bf16[4,36,8,128]{3,2,1,0:T(8,128)(2,1)S(1)}, bf16[4,36,8,128]{3,2,1,0:T(8,128)(2,1)S(1)}, u32[]{:S(2)}, u32[]{:S(2)}) collective-permute-start(bf16[4,36,8,128]{3,2,1,0:T(8,128)(2,1)S(1)} %get-tuple-element.84), channel_id=1, source_target_pairs={{0,8},{2,10},{4,12},{6,14},{8,0},{10,2},{12,4},{14,6},{16,24},{18,... | collective-permute-start | bytes 884744 | tf_op jit(solution)/shard_map/ppermute | solution.py:347
  87.0 24.2 %collective-permute-start.22 = (bf16[4,36,8,128]{3,2,1,0:T(8,128)(2,1)S(1)}, bf16[4,36,8,128]{3,2,1,0:T(8,128)(2,1)S(1)}, u32[]{:S(2)}, u32[]{:S(2)}) collective-permute-start(bf16[4,36,8,128]{3,2,1,0:T(8,128)(2,1)S(1)} %get-tuple-element.85), channel_id=1, source_target_pairs={{0,16},{2,18},{4,20},{6,22},{8,24},{10,26},{12,28},{14,30},{16,0},... | collective-permute-start | bytes 884744 | tf_op jit(solution)/shard_map/ppermute | solution.py:347
  88.0 23.2 %collective-permute-start.23 = (bf16[4,36,8,128]{3,2,1,0:T(8,128)(2,1)S(1)}, bf16[4,36,8,128]{3,2,1,0:T(8,128)(2,1)S(1)}, u32[]{:S(2)}, u32[]{:S(2)}) collective-permute-start(bf16[4,36,8,128]{3,2,1,0:T(8,128)(2,1)S(1)} %get-tuple-element.86), channel_id=1, source_target_pairs={{0,24},{2,26},{4,28},{6,30},{8,16},{10,18},{12,20},{14,22},{16,8},... | collective-permute-start | bytes 884744 | tf_op jit(solution)/shard_map/ppermute | solution.py:347
  89.7 21.5 %collective-permute-start.13 = (bf16[4,28,8,128]{3,2,1,0:T(8,128)(2,1)}, bf16[4,28,8,128]{3,2,1,0:T(8,128)(2,1)S(1)}, u32[]{:S(2)}, u32[]{:S(2)}) collective-permute-start(bf16[4,28,8,128]{3,2,1,0:T(8,128)(2,1)} %get-tuple-element.73), channel_id=1, source_target_pairs={{0,4},{2,6},{4,0},{6,2},{8,12},{10,14},{12,8},{14,10},{16,20},{18,... | collective-permute-start | bytes 688136 | tf_op jit(solution)/shard_map/ppermute | solution.py:347
  90.3 20.9 %collective-permute-start.14 = (bf16[4,28,8,128]{3,2,1,0:T(8,128)(2,1)S(1)}, bf16[4,28,8,128]{3,2,1,0:T(8,128)(2,1)S(1)}, u32[]{:S(2)}, u32[]{:S(2)}) collective-permute-start(bf16[4,28,8,128]{3,2,1,0:T(8,128)(2,1)S(1)} %get-tuple-element.74), channel_id=1, source_target_pairs={{0,6},{2,4},{4,2},{6,0},{8,14},{10,12},{12,10},{14,8},{16,22},{18,... | collective-permute-start | bytes 688136 | tf_op jit(solution)/shard_map/ppermute | solution.py:347
  111.3 1.5 %collective-permute-start.36 = (bf16[4,160,128]{2,1,0:T(8,128)(2,1)S(1)}, bf16[4,160,128]{2,1,0:T(8,128)(2,1)S(1)}, u32[]{:S(2)}, u32[]{:S(2)}) collective-permute-start(bf16[4,160,128]{2,1,0:T(8,128)(2,1)S(1)} %get-tuple-element.105), channel_id=1, source_target_pairs={{0,1},{1,0},{2,3},{3,2},{4,5},{5,4},{6,7},{7,6},{8,9},{9,8},{10,11... | collective-permute-start | bytes 491528 | tf_op jit(solution)/shard_map/ppermute | solution.py:347
  111.3 8.1 %collective-permute-start.35 = (bf16[4,160,128]{2,1,0:T(8,128)(2,1)S(1)}, bf16[4,160,128]{2,1,0:T(8,128)(2,1)S(1)}, u32[]{:S(2)}, u32[]{:S(2)}) collective-permute-start(bf16[4,160,128]{2,1,0:T(8,128)(2,1)S(1)} %get-tuple-element.103), channel_id=1, source_target_pairs={{0,1},{1,0},{2,3},{3,2},{4,5},{5,4},{6,7},{7,6},{8,9},{9,8},{10,11... | collective-permute-start | bytes 491528 | tf_op jit(solution)/shard_map/ppermute | solution.py:347
  111.8 1.9 %collective-permute-start.38 = (bf16[4,160,128]{2,1,0:T(8,128)(2,1)S(1)}, bf16[4,160,128]{2,1,0:T(8,128)(2,1)S(1)}, u32[]{:S(2)}, u32[]{:S(2)}) collective-permute-start(bf16[4,160,128]{2,1,0:T(8,128)(2,1)S(1)} %get-tuple-element.107), channel_id=1, source_target_pairs={{0,1},{1,0},{2,3},{3,2},{4,5},{5,4},{6,7},{7,6},{8,9},{9,8},{10,11... | collective-permute-start | bytes 491528 | tf_op jit(solution)/shard_map/ppermute | solution.py:347
  111.9 2.5 %collective-permute-start.40 = (bf16[4,160,128]{2,1,0:T(8,128)(2,1)S(1)}, bf16[4,160,128]{2,1,0:T(8,128)(2,1)S(1)}, u32[]{:S(2)}, u32[]{:S(2)}) collective-permute-start(bf16[4,160,128]{2,1,0:T(8,128)(2,1)S(1)} %get-tuple-element.109), channel_id=1, source_target_pairs={{0,1},{1,0},{2,3},{3,2},{4,5},{5,4},{6,7},{7,6},{8,9},{9,8},{10,11... | collective-permute-start | bytes 491528 | tf_op jit(solution)/shard_map/ppermute | solution.py:347
  112.8 7.1 %collective-permute-start.37 = (bf16[4,160,128]{2,1,0:T(8,128)(2,1)S(1)}, bf16[4,160,128]{2,1,0:T(8,128)(2,1)S(1)}, u32[]{:S(2)}, u32[]{:S(2)}) collective-permute-start(bf16[4,160,128]{2,1,0:T(8,128)(2,1)S(1)} %add_convert_fusion.2), channel_id=1, source_target_pairs={{0,2},{2,0},{4,6},{6,4},{8,10},{10,8},{12,14},{14,12},{16,18},{18,... | collective-permute-start | bytes 491528 | tf_op jit(solution)/shard_map/ppermute | solution.py:347
  113.8 9.5 %collective-permute-start.39 = (bf16[4,160,128]{2,1,0:T(8,128)(2,1)S(1)}, bf16[4,160,128]{2,1,0:T(8,128)(2,1)S(1)}, u32[]{:S(2)}, u32[]{:S(2)}) collective-permute-start(bf16[4,160,128]{2,1,0:T(8,128)(2,1)S(1)} %add_convert_fusion.1), channel_id=1, source_target_pairs={{0,4},{2,6},{4,0},{6,2},{8,12},{10,14},{12,8},{14,10},{16,20},{18,... | collective-permute-start | bytes 491528 | tf_op jit(solution)/shard_map/ppermute | solution.py:347
  114.5 8.8 %collective-permute-start.41 = (bf16[4,160,128]{2,1,0:T(8,128)(2,1)S(1)}, bf16[4,160,128]{2,1,0:T(8,128)(2,1)S(1)}, u32[]{:S(2)}, u32[]{:S(2)}) collective-permute-start(bf16[4,160,128]{2,1,0:T(8,128)(2,1)S(1)} %add_convert_fusion), channel_id=1, source_target_pairs={{0,6},{2,4},{4,2},{6,0},{8,14},{10,12},{12,10},{14,8},{16,22},{18,... | collective-permute-start | bytes 491528 | tf_op jit(solution)/shard_map/ppermute | solution.py:347
  123.4 5.5 %collective-permute-start.42 = (bf16[160,128]{1,0:T(8,128)(2,1)S(1)}, bf16[160,128]{1,0:T(8,128)(2,1)S(1)}, u32[]{:S(2)}, u32[]{:S(2)}) collective-permute-start(bf16[160,128]{1,0:T(8,128)(2,1)S(1)} %get-tuple-element.113), channel_id=1, source_target_pairs={{0,8},{2,10},{4,12},{6,14},{8,0},{10,2},{12,4},{14,6},{16,24},{18,... | collective-permute-start | bytes 122888 | tf_op jit(solution)/shard_map/ppermute | solution.py:347
  126.6 5.8 %collective-permute-start.44 = (bf16[160,128]{1,0:T(8,128)(2,1)S(1)}, bf16[160,128]{1,0:T(8,128)(2,1)S(1)}, u32[]{:S(2)}, u32[]{:S(2)}) collective-permute-start(bf16[160,128]{1,0:T(8,128)(2,1)S(1)} %get-tuple-element.114), channel_id=1, source_target_pairs={{0,24},{2,26},{4,28},{6,30},{8,16},{10,18},{12,20},{14,22},{16,8},... | collective-permute-start | bytes 122888 | tf_op jit(solution)/shard_map/ppermute | solution.py:347
  128.9 4.9 %collective-permute-start.43 = (bf16[160,128]{1,0:T(8,128)(2,1)S(1)}, bf16[160,128]{1,0:T(8,128)(2,1)S(1)}, u32[]{:S(2)}, u32[]{:S(2)}) collective-permute-start(bf16[160,128]{1,0:T(8,128)(2,1)S(1)} %get-tuple-element.115), channel_id=1, source_target_pairs={{0,16},{2,18},{4,20},{6,22},{8,24},{10,26},{12,28},{14,30},{16,0},... | collective-permute-start | bytes 122888 | tf_op jit(solution)/shard_map/ppermute | solution.py:347
  133.8 1.3 collective-permute-start.45
  (14 other events, 158.8 us)
